TPU v7x, 128 devices: a whole 4x4x4 slice. The times are simulated.
128 devices in a mesh: gx: 4 (over y), gy: 4 (over z_lo, core), gz: 8 (over z_hi, x).
Axes of the slice: x: 4, y: 4, z: 4 (z_hi: 2, z_lo: 2; z = z_hi * 2 + z_lo), core: 2. Of those that a mesh axis runs over, the one named last changes fastest.
Arguments:
- density: bfloat16 [256, 512, 512], P('gz', 'gx', 'gy'), as said below
Outputs:
- potential: float32 [256, 512, 512], P('gz', 'gx', 'gy')
- acceleration: bfloat16 [3, 256, 512, 512], P(None, 'gz', 'gx', 'gy')
Inputs may be any that keep to these rules, and one draw needn't show every extreme that they name: `density`: every cell's mass is positive.
All inputs are finite; a program needn't handle non-finite values.
Results may differ from a plain program's by a relative error of at most 0.0025.
Values sent between devices are 32-bit elements; how exact they have to be, the bound alone decides.
No kernel may reach another device: no remote copies, remote signals or barrier semaphores. Data moves between devices by JAX's collectives and lax.ppermute only.
A program may use at most 192 MiB of HBM per device.

v0:
```python
import math

import jax
import jax.numpy as jnp
from jax import lax
from jax.sharding import PartitionSpec as P

HOCK = 72
RATIO = 4
PATCH = 32
CQ = 8


highest = lax.Precision.HIGHEST
full_turn = 2.0 * math.pi


def padded(block, sides, width):
    for axis, dim in sides:
        count = lax.axis_size(axis)
        forward = [(i, i + 1) for i in range(count - 1)]
        forward.append((count - 1, 0))
        backward = [(target, source) for source, target in forward]
        low = lax.ppermute(
            lax.slice_in_dim(block, block.shape[dim] - width, None, axis=dim), axis, forward
        )
        high = lax.ppermute(lax.slice_in_dim(block, 0, width, axis=dim), axis, backward)
        block = jnp.concatenate([low, block, high], axis=dim)
    return block


def green_cube(length):
    index = jnp.arange(length, dtype=jnp.int32)
    offset = jnp.minimum(index, length - index).astype(jnp.float32)
    square = offset[:, None, None] ** 2 + offset[None, :, None] ** 2 + offset[None, None, :] ** 2
    radius = jnp.sqrt(jnp.maximum(square, 1.0))
    return jnp.where(square > 0.0, 1.0 / (4.0 * math.pi * radius), 0.25)


def coarse_table(cells, ratio):
    source = jnp.arange(cells, dtype=jnp.int32) + 2
    target = jnp.arange(cells + 4, dtype=jnp.int32)
    apart = (target[None, :] - source[:, None]).astype(jnp.float32)
    sq_apart = apart**2
    square = (
        sq_apart[:, None, None, :, None, None]
        + sq_apart[None, :, None, None, :, None]
        + sq_apart[None, None, :, None, None, :]
    )
    radius = jnp.sqrt(jnp.maximum(square, 1.0))
    table = jnp.where(square > 0.0, 1.0 / (4.0 * math.pi * ratio * radius), 0.25 / ratio)
    return table.reshape(cells**3, (cells + 4) ** 3)


def refine(coarse_ext, axis, ratio):
    inner = coarse_ext.shape[axis] - 2
    shifted = [
        lax.slice_in_dim(coarse_ext, offset, offset + inner, axis=axis) for offset in range(3)
    ]
    layers = []
    for within in range(ratio):
        place = (within + 0.5) / ratio + 0.5
        weights = [max(0.0, 1.0 - abs(place - offset)) for offset in range(3)]
        layers.append(weights[0] * shifted[0] + weights[1] * shifted[1] + weights[2] * shifted[2])
    stacked = jnp.stack(layers, axis=axis + 1)
    new_shape = list(coarse_ext.shape)
    new_shape[axis] = inner * ratio
    return stacked.reshape(new_shape)


def pad_along(values, axis, low, high):
    widths = [(0, 0)] * values.ndim
    widths[axis] = (low, high)
    return jnp.pad(values, widths)


def intersection_add(values, axis, span):
    count = values.shape[axis]
    width = values.shape[axis + 1]
    extra = width - span
    shape = list(values.shape)
    main = lax.slice_in_dim(values, 0, span, axis=axis + 1)
    main = main.reshape(shape[:axis] + [count * span] + shape[axis + 2 :])
    main = pad_along(main, axis, 0, extra)
    tail = lax.slice_in_dim(values, span, width, axis=axis + 1)
    tail = pad_along(pad_along(tail, axis + 1, 0, span - extra), axis, 1, 0)
    tail = tail.reshape(shape[:axis] + [(count + 1) * span] + shape[axis + 2 :])
    tail = lax.slice_in_dim(tail, 0, count * span + extra, axis=axis)
    return main + tail


def fold_margin(values, axis, margin, length):
    middle = lax.slice_in_dim(values, 2 * margin, 2 * margin + length, axis=axis)
    before = lax.slice_in_dim(values, 0, margin, axis=axis)
    beyond = lax.slice_in_dim(values, length + 3 * margin, length + 4 * margin, axis=axis)
    return (
        middle
        + pad_along(before, axis, 0, length - margin)
        + pad_along(beyond, axis, length - margin, 0)
    )


def even_table(length, slot_index, cell_index):
    half_len = length // 2
    is_cosine = slot_index <= half_len
    freq = jnp.where(is_cosine, slot_index, slot_index - half_len)
    weight = jnp.where((freq == 0) | (freq == half_len), 1.0, 2.0)
    phase = freq[:, None] * (cell_index[None, :] % length) % length
    angle = phase.astype(jnp.float32) * (full_turn / length)
    basis = jnp.where(is_cosine[:, None], jnp.cos(angle), jnp.sin(angle))
    return basis * jnp.sqrt(weight / length)[:, None]


def wave_tables(length, row_index, col_index, sign, scale):
    phase = row_index[:, None] % length * (col_index[None, :] % length) % length
    angle = phase.astype(jnp.float32) * (full_turn / length)
    return (jnp.cos(angle) * scale, jnp.sin(angle) * (sign * scale))


def forward_tables(length, cell_index):
    slots = jnp.arange(length, dtype=jnp.int32)
    return wave_tables(length, slots, cell_index, -1.0, 1.0)


def inverse_tables(length, slot_index):
    cells = jnp.arange(length, dtype=jnp.int32)
    return wave_tables(length, cells, slot_index, 1.0, 1.0 / length)


def apply_dim(values, tables, form, real_out):
    with_cosine = jnp.einsum(form, tables[0], values, precision=highest)
    with_sine = jnp.einsum(form, tables[1], values, precision=highest)
    if values.shape[0] == 1:
        return jnp.concatenate([with_cosine, with_sine], axis=0)
    real_part = with_cosine[0:1] - with_sine[1:2]
    if real_out:
        return real_part
    return jnp.concatenate([real_part, with_cosine[1:2] + with_sine[0:1]], axis=0)


def lattice_eigen(freq, length):
    return 2.0 - 2.0 * jnp.cos((freq % length).astype(jnp.float32) * (full_turn / length))


def body(density):
    size_gx = lax.axis_size("gx")
    size_gy = lax.axis_size("gy")
    size_gz = lax.axis_size("gz")
    fine_z, fine_x, fine_y = density.shape
    coarse_z, coarse_x, coarse_y = (fine_z // RATIO, fine_x // RATIO, fine_y // RATIO)
    total_z = coarse_z * size_gz
    total_x = coarse_x * size_gx
    total_y = coarse_y * size_gy
    y_part = total_y // (size_gx * size_gz)
    z_part = total_z // size_gy
    margin = RATIO
    region = PATCH + 2 * margin
    masses = (
        density.astype(jnp.float32)
        .reshape(coarse_z, RATIO, coarse_x, RATIO, coarse_y, RATIO)
        .sum(axis=(1, 3, 5))
    )
    spectra = lax.all_to_all(masses[None], "gz", split_axis=2, concat_axis=1, tiled=True)
    z_cells = jnp.arange(total_z, dtype=jnp.int32)
    spectra = apply_dim(spectra, forward_tables(total_z, z_cells), "ab,cbxy->caxy", False)
    spectra = lax.all_to_all(spectra, "gy", split_axis=1, concat_axis=3, tiled=True)
    y_cells = jnp.arange(total_y, dtype=jnp.int32)
    spectra = apply_dim(spectra, forward_tables(total_y, y_cells), "ab,czxb->czxa", False)
    position = jnp.arange(total_x, dtype=jnp.int32)
    y_position = jnp.arange(total_y, dtype=jnp.int32)
    spectra = lax.all_to_all(spectra, ("gx", "gz"), split_axis=3, concat_axis=2, tiled=True)
    spectra = apply_dim(spectra, forward_tables(total_x, position), "ab,czby->czay", False)
    z_slots = lax.axis_index("gy") * z_part + jnp.arange(z_part, dtype=jnp.int32)
    x_slots = jnp.arange(total_x, dtype=jnp.int32)
    y_slots = (lax.axis_index("gx") * size_gz + lax.axis_index("gz")) * y_part + jnp.arange(
        y_part, dtype=jnp.int32
    )
    eigen = (
        lattice_eigen(z_slots, total_z)[:, None, None]
        + lattice_eigen(x_slots, total_x)[None, :, None]
        + lattice_eigen(y_slots, total_y)[None, None, :]
    )
    zero_mode = (
        (z_slots == 0)[:, None, None]
        & (x_slots == 0)[None, :, None]
        & (y_slots == 0)[None, None, :]
    )
    factor = jnp.where(zero_mode, 0.0, 1.0 / (RATIO * jnp.where(zero_mode, 1.0, eigen)))
    spectra = spectra * factor[None]
    spectra = apply_dim(spectra, inverse_tables(total_x, x_slots), "ab,czby->czay", False)
    spectra = lax.all_to_all(spectra, ("gx", "gz"), split_axis=2, concat_axis=3, tiled=True)
    spectra = apply_dim(spectra, inverse_tables(total_y, y_position), "ab,czxb->czxa", False)
    spectra = lax.all_to_all(spectra, "gy", split_axis=3, concat_axis=1, tiled=True)
    spectra = apply_dim(spectra, inverse_tables(total_z, z_cells), "ab,cbxy->caxy", True)
    far = lax.all_to_all(spectra[0], "gz", split_axis=0, concat_axis=1, tiled=True)
    far_ext = padded(far, (("gx", 1), ("gy", 2), ("gz", 0)), 1)
    count_z, count_x, count_y = (fine_z // PATCH, fine_x // PATCH, fine_y // PATCH)
    blocks = masses.reshape(count_z, CQ, count_x, CQ, count_y, CQ).transpose(0, 2, 4, 1, 3, 5)
    local_coarse = jnp.dot(
        blocks.reshape(-1, CQ**3),
        coarse_table(CQ, RATIO),
        precision=highest,
        preferred_element_type=jnp.float32,
    )
    local_coarse = local_coarse.reshape(count_z, count_x, count_y, CQ + 4, CQ + 4, CQ + 4)
    slot_index = jnp.arange(HOCK, dtype=jnp.int32)
    forward = even_table(HOCK, slot_index, jnp.arange(PATCH, dtype=jnp.int32) + margin)
    backward = even_table(HOCK, slot_index, jnp.arange(region, dtype=jnp.int32))
    slot_freq = jnp.where(slot_index <= HOCK // 2, slot_index, slot_index - HOCK // 2)
    cosine = jnp.cos(
        (slot_freq[:, None] * slot_index[None, :] % HOCK).astype(jnp.float32) * (full_turn / HOCK)
    )
    green_hat = jnp.einsum("an,nxy->axy", cosine, green_cube(HOCK), precision=highest)
    green_hat = jnp.einsum("bx,axy->aby", cosine, green_hat, precision=highest)
    green_hat = jnp.einsum("cy,aby->abc", cosine, green_hat, precision=highest)

    def patch_row(row_x, summed):
        slab = lax.dynamic_slice_in_dim(density, row_x * PATCH, PATCH, 1).astype(jnp.float32)
        values = slab.reshape(fine_z, PATCH, count_y, PATCH)
        values = jnp.einsum("sm,zxbm->zxbs", forward, values, precision=highest)
        values = jnp.einsum("tx,zxbs->ztbs", forward, values, precision=highest)
        values = values.reshape(count_z, PATCH, HOCK, count_y, HOCK)
        values = jnp.einsum("uz,aztbs->autbs", forward, values, precision=highest)
        values = values * green_hat[None, :, :, None, :]
        values = jnp.einsum("uz,autbs->aztbs", backward, values, precision=highest)
        values = jnp.einsum("tx,aztbs->azxbs", backward, values, precision=highest)
        values = jnp.einsum("sm,azxbs->azxbm", backward, values, precision=highest)
        windows = lax.dynamic_index_in_dim(local_coarse, row_x, 1, keepdims=False)
        windows = windows.transpose(0, 2, 3, 1, 4)
        smooth = refine(refine(refine(windows, 1, RATIO), 2, RATIO), 4, RATIO)
        part = intersection_add(values - smooth, 0, PATCH)
        part = intersection_add(part, 2, PATCH)
        old = lax.dynamic_slice_in_dim(summed, row_x * PATCH, region, 1)
        return lax.dynamic_update_slice_in_dim(summed, old + part, row_x * PATCH, 1)

    summed = jnp.zeros((fine_z + 2 * margin, fine_x + 2 * margin, fine_y + 2 * margin), jnp.float32)
    summed = lax.fori_loop(0, count_x, patch_row, summed)
    summed = padded(summed, (("gx", 1), ("gy", 2), ("gz", 0)), margin)
    near_field = fold_margin(summed, 0, margin, fine_z)
    near_field = fold_margin(near_field, 1, margin, fine_x)
    near_field = fold_margin(near_field, 2, margin, fine_y)
    far_fine = refine(refine(refine(far_ext, 0, RATIO), 1, RATIO), 2, RATIO)
    potential = near_field + far_fine
    field_ext = padded(potential, (("gx", 1), ("gy", 2), ("gz", 0)), 2)
    extents = (fine_z, fine_x, fine_y)

    def shifted(axis, offset):
        index = [slice(2, 2 + extents[0]), slice(2, 2 + extents[1]), slice(2, 2 + extents[2])]
        index[axis] = slice(2 + offset, 2 + offset + extents[axis])
        return field_ext[tuple(index)]

    def gradient(axis):
        value = -(
            2.0 / 3.0 * (shifted(axis, 1) - shifted(axis, -1))
            - 1.0 / 12.0 * (shifted(axis, 2) - shifted(axis, -2))
        )
        return value.astype(jnp.bfloat16)

    acceleration = jnp.stack([gradient(0), gradient(1), gradient(2)])
    return (potential, acceleration)


def solution(mesh):
    placed = (P("gz", "gx", "gy"),)
    return jax.shard_map(
        body,
        mesh=mesh,
        in_specs=placed,
        out_specs=(P("gz", "gx", "gy"), P(None, "gz", "gx", "gy")),
        check_vma=False,
    )
```

profile of v0, /device:TPU:39, one launch (start us, length us, event | category | flops | bytes accessed | tf_op | source)
XLA Modules:
  0.0 917.4 jit_solution(461943475722066602)
XLA Ops:
  0.6 70.2 %reshape.575 = f32[8,4,32,4,32,4]{5,4,3,2,1,0:T(8,128)} reshape(bf16[32,128,128]{2,1,0:T(8,128)(2,1)} %param.3) | data formatting | bytes 3145728 | tf_op jit(solution)/shard_map/reshape | solution.py:160
  70.8 20.8 %reduce_sum.9 = f32[8,32,32]{2,1,0:T(8,128)S(1)} reduce(f32[8,4,32,4,32,4]{5,4,3,2,1,0:T(8,128)} %reshape.575, f32[]{:T(128)} %constant.351.clone.1), dimensions={1,3,5}, to_apply=%region_0.0 | reduce | flops 516096 | bytes 2129924 | tf_op jit(solution)/shard_map/reduce_sum | solution.py:161
  92.4 6.6 all-to-all-start
  114.4 10.5 %fusion.138 = f32[72,72,72]{0,2,1:T(8,128)} fusion(f32[72,72,72]{2,0,1:T(8,128)} %copy.344, s32[72]{0:T(128)S(1)} %add_select_fusion.5), kind=kOutput, calls=%fused_computation.269 | convolution fusion | flops 322532928 | bytes 2986272 | tf_op jit(solution)/shard_map/cy,aby->abc/dot_general | solution.py:215
  125.1 24.2 %fusion.58 = f32[8,8,8,12,12,12]{5,4,3,2,1,0:T(8,128)} fusion(f32[8,12]{1,0:T(8,128)S(1)} %convert_multiply_fusion, f32[8,8,12,12]{3,2,1,0:T(8,128)S(1)} %broadcast_add_fusion), kind=kLoop, calls=%fused_computation.88 | loop fusion | flops 5308416 | bytes 3576192 | tf_op jit(solution)/shard_map/jit(_where)/select_n | solution.py:51
  149.3 29.4 %reshape.579 = f32[512,1728]{1,0:T(8,128)} reshape(f32[8,8,8,12,12,12]{5,4,3,2,1,0:T(8,128)} %fusion.58) | data formatting | bytes 7077888 | tf_op jit(solution)/shard_map/jit(_where)/select_n | solution.py:51
  187.8 19.6 %convolution_bitcast_fusion.1 = f32[1,4,4,12,12,12]{5,2,4,3,1,0:T(4,128)S(1)} fusion(f32[12,12,12,512,1]{3,2,1,0,4:T(8,128)} %reshape.606, f32[4,4,512,1,1]{2,1,0,3,4:T(4,128)S(1)} %reshape.605), kind=kOutput, calls=%fused_computation.157 | convolution fusion | flops 169869312 | bytes 3682304 | tf_op jit(solution)/shard_map/dot_general | solution.py:199
  222.7 8.8 all-to-all-start.2
  231.5 7.1 all-to-all-done.2
  245.1 6.0 all-to-all-start.3
  254.0 514.4 %while.18 = (s32[]{:T(128)}, f32[40,136,136]{1,2,0:T(8,128)}, bf16[32,128,128]{2,1,0:T(8,128)(2,1)}, f32[72,72,72]{0,2,1:T(8,128)}, f32[1,4,4,12,12,12]{5,2,4,3,...) while((s32[]{:T(128)}, f32[40,136,136]{1,2,0:T(8,128)}, ...), condition=%wide.region_2.3_spmd.clone.clone.clone, body=%wide.region_1.2_spmd.clone.clone.clone.sunk | while | flops 2282412800 | bytes 70401000 | solution.py:237
  257.0 9.3 %convolution_bitcast_fusion.11 = f32[32,72,4,72]{1,3,2,0:T(8,128)} fusion(f32[32,32,4,72]{3,1,2,0:T(8,128)S(1)} %fusion.332, f32[72]{0:T(128)S(1)} %get-tuple-element.540, s32[32]{0:T(128)S(1)} %get-tuple-element.537, s32[72]{0:T(128)S(1)} %get-tuple-element.538, pred[72]{0:T(512)(128)(4,1)S(1)} %get-tuple-element.539), kind=kOutput, calls=%fused_computation.18.clone.1 | convolution fusion | flops 254829312 | bytes 3834632 | tf_op jit(solution)/shard_map/while/body/eval_jaxpr/tx,zxbs->ztbs/dot_general | solution.py:221
  266.3 6.7 copy.398
  273.1 19.6 %fusion.333 = f32[72,4,72,72]{3,2,1,0:T(8,128)S(1)} fusion(f32[32,72,4,72]{3,0,2,1:T(8,128)} %copy.398, f32[72]{0:T(128)S(1)} %get-tuple-element.540, s32[32]{0:T(128)S(1)} %get-tuple-element.537, s32[72]{0:T(128)S(1)} %get-tuple-element.538, pred[72]{0:T(512)(128)(4,1)S(1)} %get-tuple-element.539), kind=kOutput, calls=%fused_computation.55.clone.1 | convolution fusion | flops 573334272 | bytes 8626952 | tf_op jit(solution)/shard_map/while/body/eval_jaxpr/uz,aztbs->autbs/dot_general | solution.py:223
  292.7 27.4 %fusion.334 = f32[40,72,4,72]{3,0,2,1:T(8,128)S(1)} fusion(f32[72,4,72,72]{3,2,1,0:T(8,128)S(1)} %fusion.333, f32[72,72,72]{0,2,1:T(8,128)S(1)} %copy-done, f32[72]{0:T(128)S(1)} %get-tuple-element.540, s32[72]{0:T(128)S(1)} %get-tuple-element.538, pred[72]{0:T(512)(128)(4,1)S(1)} %get-tuple-element.539), kind=kOutput, calls=%fused_computation.17.clone.1 | convolution fusion | flops 718160832 | bytes 10783368 | tf_op jit(solution)/shard_map/while/body/eval_jaxpr/uz,autbs->aztbs/dot_general | solution.py:225
  320.1 8.7 fusion.335
  338.9 15.4 %subtract_bitcast_fusion.2 = f32[1,40,40,4,40]{2,4,3,1,0:T(8,128)S(1)} fusion(f32[40,40,4,40]{1,3,2,0:T(8,128)} %bitcast.312, f32[40,4,72,40]{2,3,1,0:T(8,128)} %fusion.335, f32[72]{0:T(128)S(1)} %get-tuple-element.540, s32[72]{0:T(128)S(1)} %get-tuple-element.538, pred[72]{0:T(512)(128)(4,1)S(1)} %get-tuple-element.539), kind=kOutput, calls=%fused_computation.13.clone.1 | convolution fusion | flops 221471680 | bytes 3891848 | tf_op jit(solution)/shard_map/while/body/eval_jaxpr/sm,azxbs->azxbm/dot_general | solution.py:227
  357.9 5.7 fusion.336
  363.7 13.9 %dynamic_update_slice.14 = f32[40,136,136]{1,2,0:T(8,128)} dynamic-update-slice(f32[40,136,136]{1,2,0:T(8,128)} %get-tuple-element.518, f32[40,40,136]{1,2,0:T(8,128)} %fusion.336, s32[]{:T(128)} %constant.350.clone.1..sunk, s32[]{:T(128)S(6)} %select_n.562, s32[]{:T(128)} %constant.350.clone.1..sunk) | dynamic-update-slice | bytes 1740804 | tf_op jit(solution)/shard_map/while/body/eval_jaxpr/dynamic_update_slice | solution.py:234
  380.5 9.3 %convolution_bitcast_fusion.11 = f32[32,72,4,72]{1,3,2,0:T(8,128)} fusion(f32[32,32,4,72]{3,1,2,0:T(8,128)S(1)} %fusion.332, f32[72]{0:T(128)S(1)} %get-tuple-element.540, s32[32]{0:T(128)S(1)} %get-tuple-element.537, s32[72]{0:T(128)S(1)} %get-tuple-element.538, pred[72]{0:T(512)(128)(4,1)S(1)} %get-tuple-element.539), kind=kOutput, calls=%fused_computation.18.clone.1 | convolution fusion | flops 254829312 | bytes 3834632 | tf_op jit(solution)/shard_map/while/body/eval_jaxpr/tx,zxbs->ztbs/dot_general | solution.py:221
  389.8 6.7 copy.398
  396.6 19.5 %fusion.333 = f32[72,4,72,72]{3,2,1,0:T(8,128)S(1)} fusion(f32[32,72,4,72]{3,0,2,1:T(8,128)} %copy.398, f32[72]{0:T(128)S(1)} %get-tuple-element.540, s32[32]{0:T(128)S(1)} %get-tuple-element.537, s32[72]{0:T(128)S(1)} %get-tuple-element.538, pred[72]{0:T(512)(128)(4,1)S(1)} %get-tuple-element.539), kind=kOutput, calls=%fused_computation.55.clone.1 | convolution fusion | flops 573334272 | bytes 8626952 | tf_op jit(solution)/shard_map/while/body/eval_jaxpr/uz,aztbs->autbs/dot_general | solution.py:223
  416.1 27.3 %fusion.334 = f32[40,72,4,72]{3,0,2,1:T(8,128)S(1)} fusion(f32[72,4,72,72]{3,2,1,0:T(8,128)S(1)} %fusion.333, f32[72,72,72]{0,2,1:T(8,128)S(1)} %copy-done, f32[72]{0:T(128)S(1)} %get-tuple-element.540, s32[72]{0:T(128)S(1)} %get-tuple-element.538, pred[72]{0:T(512)(128)(4,1)S(1)} %get-tuple-element.539), kind=kOutput, calls=%fused_computation.17.clone.1 | convolution fusion | flops 718160832 | bytes 10783368 | tf_op jit(solution)/shard_map/while/body/eval_jaxpr/uz,autbs->aztbs/dot_general | solution.py:225
  443.5 8.7 fusion.335
  462.0 15.4 %subtract_bitcast_fusion.2 = f32[1,40,40,4,40]{2,4,3,1,0:T(8,128)S(1)} fusion(f32[40,40,4,40]{1,3,2,0:T(8,128)} %bitcast.312, f32[40,4,72,40]{2,3,1,0:T(8,128)} %fusion.335, f32[72]{0:T(128)S(1)} %get-tuple-element.540, s32[72]{0:T(128)S(1)} %get-tuple-element.538, pred[72]{0:T(512)(128)(4,1)S(1)} %get-tuple-element.539), kind=kOutput, calls=%fused_computation.13.clone.1 | convolution fusion | flops 221471680 | bytes 3891848 | tf_op jit(solution)/shard_map/while/body/eval_jaxpr/sm,azxbs->azxbm/dot_general | solution.py:227
  481.1 5.7 fusion.336
  486.8 18.0 %dynamic_update_slice.14 = f32[40,136,136]{1,2,0:T(8,128)} dynamic-update-slice(f32[40,136,136]{1,2,0:T(8,128)} %get-tuple-element.518, f32[40,40,136]{1,2,0:T(8,128)} %fusion.336, s32[]{:T(128)} %constant.350.clone.1..sunk, s32[]{:T(128)S(6)} %select_n.562, s32[]{:T(128)} %constant.350.clone.1..sunk) | dynamic-update-slice | bytes 1740804 | tf_op jit(solution)/shard_map/while/body/eval_jaxpr/dynamic_update_slice | solution.py:234
  507.9 9.3 %convolution_bitcast_fusion.11 = f32[32,72,4,72]{1,3,2,0:T(8,128)} fusion(f32[32,32,4,72]{3,1,2,0:T(8,128)S(1)} %fusion.332, f32[72]{0:T(128)S(1)} %get-tuple-element.540, s32[32]{0:T(128)S(1)} %get-tuple-element.537, s32[72]{0:T(128)S(1)} %get-tuple-element.538, pred[72]{0:T(512)(128)(4,1)S(1)} %get-tuple-element.539), kind=kOutput, calls=%fused_computation.18.clone.1 | convolution fusion | flops 254829312 | bytes 3834632 | tf_op jit(solution)/shard_map/while/body/eval_jaxpr/tx,zxbs->ztbs/dot_general | solution.py:221
  517.3 6.7 copy.398
  524.0 19.3 %fusion.333 = f32[72,4,72,72]{3,2,1,0:T(8,128)S(1)} fusion(f32[32,72,4,72]{3,0,2,1:T(8,128)} %copy.398, f32[72]{0:T(128)S(1)} %get-tuple-element.540, s32[32]{0:T(128)S(1)} %get-tuple-element.537, s32[72]{0:T(128)S(1)} %get-tuple-element.538, pred[72]{0:T(512)(128)(4,1)S(1)} %get-tuple-element.539), kind=kOutput, calls=%fused_computation.55.clone.1 | convolution fusion | flops 573334272 | bytes 8626952 | tf_op jit(solution)/shard_map/while/body/eval_jaxpr/uz,aztbs->autbs/dot_general | solution.py:223
  543.3 27.6 %fusion.334 = f32[40,72,4,72]{3,0,2,1:T(8,128)S(1)} fusion(f32[72,4,72,72]{3,2,1,0:T(8,128)S(1)} %fusion.333, f32[72,72,72]{0,2,1:T(8,128)S(1)} %copy-done, f32[72]{0:T(128)S(1)} %get-tuple-element.540, s32[72]{0:T(128)S(1)} %get-tuple-element.538, pred[72]{0:T(512)(128)(4,1)S(1)} %get-tuple-element.539), kind=kOutput, calls=%fused_computation.17.clone.1 | convolution fusion | flops 718160832 | bytes 10783368 | tf_op jit(solution)/shard_map/while/body/eval_jaxpr/uz,autbs->aztbs/dot_general | solution.py:225
  570.9 8.7 fusion.335
  589.5 15.4 %subtract_bitcast_fusion.2 = f32[1,40,40,4,40]{2,4,3,1,0:T(8,128)S(1)} fusion(f32[40,40,4,40]{1,3,2,0:T(8,128)} %bitcast.312, f32[40,4,72,40]{2,3,1,0:T(8,128)} %fusion.335, f32[72]{0:T(128)S(1)} %get-tuple-element.540, s32[72]{0:T(128)S(1)} %get-tuple-element.538, pred[72]{0:T(512)(128)(4,1)S(1)} %get-tuple-element.539), kind=kOutput, calls=%fused_computation.13.clone.1 | convolution fusion | flops 221471680 | bytes 3891848 | tf_op jit(solution)/shard_map/while/body/eval_jaxpr/sm,azxbs->azxbm/dot_general | solution.py:227
  608.5 5.7 fusion.336
  614.2 18.0 %dynamic_update_slice.14 = f32[40,136,136]{1,2,0:T(8,128)} dynamic-update-slice(f32[40,136,136]{1,2,0:T(8,128)} %get-tuple-element.518, f32[40,40,136]{1,2,0:T(8,128)} %fusion.336, s32[]{:T(128)} %constant.350.clone.1..sunk, s32[]{:T(128)S(6)} %select_n.562, s32[]{:T(128)} %constant.350.clone.1..sunk) | dynamic-update-slice | bytes 1740804 | tf_op jit(solution)/shard_map/while/body/eval_jaxpr/dynamic_update_slice | solution.py:234
  635.2 9.3 %convolution_bitcast_fusion.11 = f32[32,72,4,72]{1,3,2,0:T(8,128)} fusion(f32[32,32,4,72]{3,1,2,0:T(8,128)S(1)} %fusion.332, f32[72]{0:T(128)S(1)} %get-tuple-element.540, s32[32]{0:T(128)S(1)} %get-tuple-element.537, s32[72]{0:T(128)S(1)} %get-tuple-element.538, pred[72]{0:T(512)(128)(4,1)S(1)} %get-tuple-element.539), kind=kOutput, calls=%fused_computation.18.clone.1 | convolution fusion | flops 254829312 | bytes 3834632 | tf_op jit(solution)/shard_map/while/body/eval_jaxpr/tx,zxbs->ztbs/dot_general | solution.py:221
  644.5 6.7 copy.398
  651.3 19.5 %fusion.333 = f32[72,4,72,72]{3,2,1,0:T(8,128)S(1)} fusion(f32[32,72,4,72]{3,0,2,1:T(8,128)} %copy.398, f32[72]{0:T(128)S(1)} %get-tuple-element.540, s32[32]{0:T(128)S(1)} %get-tuple-element.537, s32[72]{0:T(128)S(1)} %get-tuple-element.538, pred[72]{0:T(512)(128)(4,1)S(1)} %get-tuple-element.539), kind=kOutput, calls=%fused_computation.55.clone.1 | convolution fusion | flops 573334272 | bytes 8626952 | tf_op jit(solution)/shard_map/while/body/eval_jaxpr/uz,aztbs->autbs/dot_general | solution.py:223
  670.8 27.4 %fusion.334 = f32[40,72,4,72]{3,0,2,1:T(8,128)S(1)} fusion(f32[72,4,72,72]{3,2,1,0:T(8,128)S(1)} %fusion.333, f32[72,72,72]{0,2,1:T(8,128)S(1)} %copy-done, f32[72]{0:T(128)S(1)} %get-tuple-element.540, s32[72]{0:T(128)S(1)} %get-tuple-element.538, pred[72]{0:T(512)(128)(4,1)S(1)} %get-tuple-element.539), kind=kOutput, calls=%fused_computation.17.clone.1 | convolution fusion | flops 718160832 | bytes 10783368 | tf_op jit(solution)/shard_map/while/body/eval_jaxpr/uz,autbs->aztbs/dot_general | solution.py:225
  698.2 8.7 fusion.335
  717.0 15.4 %subtract_bitcast_fusion.2 = f32[1,40,40,4,40]{2,4,3,1,0:T(8,128)S(1)} fusion(f32[40,40,4,40]{1,3,2,0:T(8,128)} %bitcast.312, f32[40,4,72,40]{2,3,1,0:T(8,128)} %fusion.335, f32[72]{0:T(128)S(1)} %get-tuple-element.540, s32[72]{0:T(128)S(1)} %get-tuple-element.538, pred[72]{0:T(512)(128)(4,1)S(1)} %get-tuple-element.539), kind=kOutput, calls=%fused_computation.13.clone.1 | convolution fusion | flops 221471680 | bytes 3891848 | tf_op jit(solution)/shard_map/while/body/eval_jaxpr/sm,azxbs->azxbm/dot_general | solution.py:227
  736.0 5.7 fusion.336
  741.8 18.0 %dynamic_update_slice.14 = f32[40,136,136]{1,2,0:T(8,128)} dynamic-update-slice(f32[40,136,136]{1,2,0:T(8,128)} %get-tuple-element.518, f32[40,40,136]{1,2,0:T(8,128)} %fusion.336, s32[]{:T(128)} %constant.350.clone.1..sunk, s32[]{:T(128)S(6)} %select_n.562, s32[]{:T(128)} %constant.350.clone.1..sunk) | dynamic-update-slice | bytes 1740804 | tf_op jit(solution)/shard_map/while/body/eval_jaxpr/dynamic_update_slice | solution.py:234
  768.4 7.9 copy.295
  782.4 7.9 all-to-all-start.4
  797.8 6.1 all-to-all-start.5
  803.9 6.8 copy.298
  846.2 5.7 collective-permute-done.11
  (301 shorter events, 228.5 us)
Async XLA Ops:
  92.4 115.2 %all-to-all-start = ((f32[8,1,1024]{2,1,0:T(1,128)}), f32[8,1,1024]{2,1,0:T(1,128)}, u32[]{:S(2)}, u32[]{:S(2)}) async-start(f32[8,1,1024]{2,1,0:T(1,128)} %reshape.617), calls=%async_computation | async-start | bytes 65536 | tf_op jit(solution)/shard_map/all_to_all | solution.py:163
  99.1 111.4 %copy-start.6 = (s32[64]{0:T(128)}, s32[64]{0:T(128)S(1)}, u32[]{:S(2)}) copy-start(s32[64]{0:T(128)S(1)} %and_select_fusion.5) | copy-start | bytes 772
  99.1 144.1 %copy-start.8 = (s32[128]{0:T(128)}, s32[128]{0:T(128)S(1)}, u32[]{:S(2)}) copy-start(s32[128]{0:T(128)S(1)} %and_select_fusion.4) | copy-start | bytes 1540
  187.8 19.7 %copy-start.11 = (pred[4]{0:T(512)(128)(4,1)S(1)}, pred[4]{0:T(512)(128)(4,1)}, u32[]{:S(2)}) copy-start(pred[4]{0:T(512)(128)(4,1)} %fusion.211) | copy-start | bytes 16
  211.9 6.9 all-to-all-start.1
  222.7 16.0 %all-to-all-start.2 = ((f32[32,1,512]{2,1,0:T(1,128)}), f32[32,1,512]{2,1,0:T(1,128)S(1)}, u32[]{:S(2)}, u32[]{:S(2)}) async-start(f32[32,1,512]{2,1,0:T(1,128)} %reshape.621), calls=%async_computation.2 | async-start | bytes 131072 | tf_op jit(solution)/shard_map/all_to_all | solution.py:171
  245.1 531.2 %all-to-all-start.3 = ((f32[32,1,512]{2,1,0:T(1,128)}), f32[32,1,512]{2,1,0:T(1,128)}, u32[]{:S(2)}, u32[]{:S(2)}) async-start(f32[32,1,512]{2,1,0:T(1,128)} %reshape.623), calls=%async_computation.3 | async-start | bytes 131072 | tf_op jit(solution)/shard_map/all_to_all | solution.py:191
  254.2 74.6 %copy-start.4 = (f32[1,4,4,12,12,12]{5,2,4,3,1,0:T(4,128)}, f32[1,4,4,12,12,12]{5,2,4,3,1,0:T(4,128)S(1)}, u32[]{:S(2)}) copy-start(f32[1,4,4,12,12,12]{5,2,4,3,1,0:T(4,128)S(1)} %get-tuple-element.536) | copy-start | bytes 331780 | tf_op jit(solution)/shard_map/while
  273.1 19.6 %copy-start = (f32[72,72,72]{0,2,1:T(8,128)S(1)}, f32[72,72,72]{0,2,1:T(8,128)}, u32[]{:S(2)}) copy-start(f32[72,72,72]{0,2,1:T(8,128)} %get-tuple-element.535) | copy-start | bytes 4478980 | tf_op jit(solution)/shard_map/while
  363.7 13.9 %copy-start.5 = (f32[1,4,4,12,12,12]{5,2,4,3,1,0:T(4,128)S(1)}, f32[1,4,4,12,12,12]{5,2,4,3,1,0:T(4,128)}, u32[]{:S(2)}) copy-start(f32[1,4,4,12,12,12]{5,2,4,3,1,0:T(4,128)} %copy-done.4) | copy-start | bytes 331780 | tf_op jit(solution)/shard_map/while
  377.7 74.5 %copy-start.4 = (f32[1,4,4,12,12,12]{5,2,4,3,1,0:T(4,128)}, f32[1,4,4,12,12,12]{5,2,4,3,1,0:T(4,128)S(1)}, u32[]{:S(2)}) copy-start(f32[1,4,4,12,12,12]{5,2,4,3,1,0:T(4,128)S(1)} %get-tuple-element.536) | copy-start | bytes 331780 | tf_op jit(solution)/shard_map/while
  396.6 19.5 %copy-start = (f32[72,72,72]{0,2,1:T(8,128)S(1)}, f32[72,72,72]{0,2,1:T(8,128)}, u32[]{:S(2)}) copy-start(f32[72,72,72]{0,2,1:T(8,128)} %get-tuple-element.535) | copy-start | bytes 4478980 | tf_op jit(solution)/shard_map/while
  486.8 18.0 %copy-start.5 = (f32[1,4,4,12,12,12]{5,2,4,3,1,0:T(4,128)S(1)}, f32[1,4,4,12,12,12]{5,2,4,3,1,0:T(4,128)}, u32[]{:S(2)}) copy-start(f32[1,4,4,12,12,12]{5,2,4,3,1,0:T(4,128)} %copy-done.4) | copy-start | bytes 331780 | tf_op jit(solution)/shard_map/while
  505.2 74.5 %copy-start.4 = (f32[1,4,4,12,12,12]{5,2,4,3,1,0:T(4,128)}, f32[1,4,4,12,12,12]{5,2,4,3,1,0:T(4,128)S(1)}, u32[]{:S(2)}) copy-start(f32[1,4,4,12,12,12]{5,2,4,3,1,0:T(4,128)S(1)} %get-tuple-element.536) | copy-start | bytes 331780 | tf_op jit(solution)/shard_map/while
  524.0 19.3 %copy-start = (f32[72,72,72]{0,2,1:T(8,128)S(1)}, f32[72,72,72]{0,2,1:T(8,128)}, u32[]{:S(2)}) copy-start(f32[72,72,72]{0,2,1:T(8,128)} %get-tuple-element.535) | copy-start | bytes 4478980 | tf_op jit(solution)/shard_map/while
  614.2 18.0 %copy-start.5 = (f32[1,4,4,12,12,12]{5,2,4,3,1,0:T(4,128)S(1)}, f32[1,4,4,12,12,12]{5,2,4,3,1,0:T(4,128)}, u32[]{:S(2)}) copy-start(f32[1,4,4,12,12,12]{5,2,4,3,1,0:T(4,128)} %copy-done.4) | copy-start | bytes 331780 | tf_op jit(solution)/shard_map/while
  632.4 74.5 %copy-start.4 = (f32[1,4,4,12,12,12]{5,2,4,3,1,0:T(4,128)}, f32[1,4,4,12,12,12]{5,2,4,3,1,0:T(4,128)S(1)}, u32[]{:S(2)}) copy-start(f32[1,4,4,12,12,12]{5,2,4,3,1,0:T(4,128)S(1)} %get-tuple-element.536) | copy-start | bytes 331780 | tf_op jit(solution)/shard_map/while
  651.3 19.5 %copy-start = (f32[72,72,72]{0,2,1:T(8,128)S(1)}, f32[72,72,72]{0,2,1:T(8,128)}, u32[]{:S(2)}) copy-start(f32[72,72,72]{0,2,1:T(8,128)} %get-tuple-element.535) | copy-start | bytes 4478980 | tf_op jit(solution)/shard_map/while
  741.7 18.0 %copy-start.5 = (f32[1,4,4,12,12,12]{5,2,4,3,1,0:T(4,128)S(1)}, f32[1,4,4,12,12,12]{5,2,4,3,1,0:T(4,128)}, u32[]{:S(2)}) copy-start(f32[1,4,4,12,12,12]{5,2,4,3,1,0:T(4,128)} %copy-done.4) | copy-start | bytes 331780 | tf_op jit(solution)/shard_map/while
  776.3 2.5 copy-start.9
  778.8 16.8 %copy-start.7 = (s32[64]{0:T(128)S(1)}, s32[64]{0:T(128)}, u32[]{:S(2)}) copy-start(s32[64]{0:T(128)} %copy-done.6) | copy-start | bytes 772
  782.4 11.7 %all-to-all-start.4 = ((f32[4,1,4096]{2,1,0:T(1,128)}), f32[4,1,4096]{2,1,0:T(1,128)S(1)}, u32[]{:S(2)}, u32[]{:S(2)}) async-start(f32[4,1,4096]{2,1,0:T(1,128)} %reshape.625), calls=%async_computation.4 | async-start | bytes 131072 | tf_op jit(solution)/shard_map/all_to_all | solution.py:193
  791.4 19.3 %collective-permute-start = (f32[40,4,136]{2,0,1:T(8,128)S(1)}, f32[40,4,136]{2,0,1:T(8,128)S(1)}, u32[]{:S(2)}, u32[]{:S(2)}) collective-permute-start(f32[40,4,136]{2,0,1:T(8,128)S(1)} %get-tuple-element.391), channel_id=1, source_target_pairs={{0,32},{32,64},{64,96},{96,0},{1,33},{33,65},{65,97},{97,1},{2,34}... | collective-permute-start | bytes 261128 | tf_op jit(solution)/shard_map/ppermute | solution.py:24
  792.7 19.0 %collective-permute-start.1 = (f32[40,4,136]{2,0,1:T(8,128)S(1)}, f32[40,4,136]{2,0,1:T(8,128)S(1)}, u32[]{:S(2)}, u32[]{:S(2)}) collective-permute-start(f32[40,4,136]{2,0,1:T(8,128)S(1)} %get-tuple-element.392), channel_id=1, source_target_pairs={{32,0},{64,32},{96,64},{0,96},{33,1},{65,33},{97,65},{1,97},{34,2}... | collective-permute-start | bytes 261128 | tf_op jit(solution)/shard_map/ppermute | solution.py:27
  797.8 16.4 %all-to-all-start.5 = ((f32[8,1,1024]{2,1,0:T(1,128)}), f32[8,1,1024]{2,1,0:T(1,128)S(1)}, u32[]{:S(2)}, u32[]{:S(2)}) async-start(f32[8,1,1024]{2,1,0:T(1,128)} %reshape.627), calls=%async_computation.5 | async-start | bytes 65536 | tf_op jit(solution)/shard_map/all_to_all | solution.py:195
  815.1 6.5 collective-permute-start.6
  815.2 13.2 %slice-start = ((s8[5570560]{0:T(1024)(128)(4,1)}), s8[4194304]{0:T(1024)(128)(4,1)S(1)}, s32[]{:S(2)}) async-start(s8[5570560]{0:T(1024)(128)(4,1)} %bitcast.317), calls=%async_computation.6 | async-start | bytes 8388608
  815.2 13.2 %slice-start.1 = ((s8[5570560]{0:T(1024)(128)(4,1)}), s8[1376256]{0:T(1024)(128)(4,1)S(1)}, s32[]{:S(2)}) async-start(s8[5570560]{0:T(1024)(128)(4,1)} %bitcast.317), calls=%async_computation.7 | async-start | bytes 2752512
  815.2 6.4 collective-permute-start.7
  817.9 10.6 %copy-start.3 = (f32[40,4,136]{1,0,2:T(8,128)S(1)}, f32[40,4,136]{1,0,2:T(8,128)}, u32[]{:S(2)}) copy-start(f32[40,4,136]{1,0,2:T(8,128)} %copy.299) | copy-start | bytes 261124
  819.3 4.6 collective-permute-start.2
  821.6 6.8 collective-permute-start.3
  821.8 10.9 %collective-permute-start.8 = (f32[8,34,1]{2,0,1:T(8,128)S(1)}, f32[8,34,1]{2,0,1:T(8,128)S(1)}, u32[]{:S(2)}, u32[]{:S(2)}) collective-permute-start(f32[8,34,1]{2,0,1:T(8,128)S(1)} %get-tuple-element.411), channel_id=1, source_target_pairs={{0,8},{8,16},{16,24},{24,0},{1,9},{9,17},{17,25},{25,1},{2,10},{10... | collective-permute-start | bytes 3272 | tf_op jit(solution)/shard_map/ppermute | solution.py:24
  823.8 8.8 collective-permute-start.9
  830.5 36.5 %collective-permute-start.4 = (f32[4,144,144]{1,0,2:T(4,128)}, f32[4,144,144]{1,0,2:T(4,128)}, u32[]{:S(2)}, u32[]{:S(2)}) collective-permute-start(f32[4,144,144]{1,0,2:T(4,128)} %get-tuple-element.383), channel_id=1, source_target_pairs={{0,1},{1,2},{2,3},{3,4},{4,5},{5,6},{6,7},{7,0},{8,9},{9,10},{10,1... | collective-permute-start | bytes 995336 | tf_op jit(solution)/shard_map/ppermute | solution.py:24
  832.6 34.4 %collective-permute-start.5 = (f32[4,144,144]{1,0,2:T(4,128)}, f32[4,144,144]{1,0,2:T(4,128)}, u32[]{:S(2)}, u32[]{:S(2)}) collective-permute-start(f32[4,144,144]{1,0,2:T(4,128)} %get-tuple-element.384), channel_id=1, source_target_pairs={{1,0},{2,1},{3,2},{4,3},{5,4},{6,5},{7,6},{0,7},{9,8},{10,9},{11,1... | collective-permute-start | bytes 995336 | tf_op jit(solution)/shard_map/ppermute | solution.py:27
  832.8 13.3 %collective-permute-start.10 = (f32[1,34,34]{2,0,1:T(1,128)S(1)}, f32[1,34,34]{2,0,1:T(1,128)S(1)}, u32[]{:S(2)}, u32[]{:S(2)}) collective-permute-start(f32[1,34,34]{2,0,1:T(1,128)S(1)} %get-tuple-element.410), channel_id=1, source_target_pairs={{0,1},{1,2},{2,3},{3,4},{4,5},{5,6},{6,7},{7,0},{8,9},{9,10},{10,1... | collective-permute-start | bytes 13880 | tf_op jit(solution)/shard_map/ppermute | solution.py:24
  838.0 13.9 %collective-permute-start.11 = (f32[1,34,34]{2,0,1:T(1,128)S(1)}, f32[1,34,34]{2,0,1:T(1,128)S(1)}, u32[]{:S(2)}, u32[]{:S(2)}) collective-permute-start(f32[1,34,34]{2,0,1:T(1,128)S(1)} %get-tuple-element.409), channel_id=1, source_target_pairs={{1,0},{2,1},{3,2},{4,3},{5,4},{6,5},{7,6},{0,7},{9,8},{10,9},{11,1... | collective-permute-start | bytes 13880 | tf_op jit(solution)/shard_map/ppermute | solution.py:27
  864.0 3.0 slice-start.2
  865.6 1.7 slice-start.3
  877.4 7.3 collective-permute-start.12
  880.1 7.5 collective-permute-start.13
  890.4 2.7 copy-start.1
  890.4 2.7 copy-start.2
  891.5 5.5 collective-permute-start.14
  893.0 4.0 collective-permute-start.15
  897.9 10.2 %collective-permute-start.16 = (f32[2,132,132]{1,0,2:T(2,128)S(1)}, f32[2,132,132]{1,0,2:T(2,128)S(1)}, u32[]{:S(2)}, u32[]{:S(2)}) collective-permute-start(f32[2,132,132]{1,0,2:T(2,128)S(1)} %get-tuple-element.387), channel_id=1, source_target_pairs={{1,0},{2,1},{3,2},{4,3},{5,4},{6,5},{7,6},{0,7},{9,8},{10,9},{11,1... | collective-permute-start | bytes 418184 | tf_op jit(solution)/shard_map/ppermute | solution.py:27
  898.0 10.1 %collective-permute-start.17 = (f32[2,132,132]{1,0,2:T(2,128)S(1)}, f32[2,132,132]{1,0,2:T(2,128)S(1)}, u32[]{:S(2)}, u32[]{:S(2)}) collective-permute-start(f32[2,132,132]{1,0,2:T(2,128)S(1)} %get-tuple-element.388), channel_id=1, source_target_pairs={{0,1},{1,2},{2,3},{3,4},{4,5},{5,6},{6,7},{7,0},{8,9},{9,10},{10,1... | collective-permute-start | bytes 418184 | tf_op jit(solution)/shard_map/ppermute | solution.py:24
  (1 other events, 0.7 us)
where the time goes:
time: 936 us; the launch traced here: 917 us
  matrix products  373 us (40%)
  local copies, waits for them, and re-layouts  315 us (34%)
  other arithmetic  126 us (13%)
  starting transfers between devices  67.3 us (7%)
  waiting for transfers between devices  23.8 us (3%)
  loops' own time  10.4 us (1%)
    dot_general x4, matrix products, patch_row(): values = jnp.einsum('uz,autbs->aztbs', backward, values, precision=highest)  110 us
    dot_general x4, matrix products, patch_row(): values = jnp.einsum('uz,aztbs->autbs', forward, values, precision=highest)  77.9 us
    reshape x1, local copies, waits for them, and re-layouts, body(): masses = density.astype(jnp.float32).reshape(coarse_z, RATIO, coarse_x, R...  70.2 us
    dynamic_update_slice x4, local copies, waits for them, and re-layouts, patch_row(): return lax.dynamic_update_slice_in_dim(summed, old + part, row_x * PATCH, 1)  67.8 us
    dot_general x4, matrix products, patch_row(): values = jnp.einsum('sm,azxbs->azxbm', backward, values, precision=highest)  61.5 us
    dot_general x4, matrix products, patch_row(): values = jnp.einsum('tx,zxbs->ztbs', forward, values, precision=highest)  37.4 us
    dot_general x4, matrix products, patch_row(): values = jnp.einsum('tx,aztbs->azxbs', backward, values, precision=highest)  35 us
    select_n x1, local copies, waits for them, and re-layouts, coarse_table(): jnp.where(square > 0.0, 1.0 / (4.0 * math.pi * ratio * radius), 0.25 / ra...  29.4 us
  transfers between devices with their start and end apart: 24, of which 7 were waited for; matrix products, arithmetic and copies ran while one was open for 74% of the time, Pallas kernels for 0%

commit v1 on v0

v1 whole, which is shorter than its diff:
```python
import functools
import math

import jax
import jax.numpy as jnp
import ml_dtypes
import numpy as np
from jax import lax
from jax.experimental import pallas as pl
from jax.experimental.pallas import tpu as pltpu
from jax.sharding import PartitionSpec as P

HOCK = 72
RATIO = 4
PATCH = 32
CQ = 8
CH = HOCK // RATIO
NF = HOCK // 2 + 1
NC = CH // 2 + 1
NG = 48
PAIRS = 320

f32 = jnp.float32
b16 = jnp.bfloat16
MIB = 1 << 20


def halves(table):
    high = table.astype(ml_dtypes.bfloat16)
    low = (table - high.astype(np.float64)).astype(ml_dtypes.bfloat16)
    return high, low


def centred(length, cells, centre):
    freq = np.arange(length // 2 + 1)
    weight = np.where((freq == 0) | (freq == length // 2), 1.0, 2.0)
    angle = 2.0 * math.pi / length * freq[:, None] * (cells - centre)[None, :]
    basis = np.stack([np.cos(angle), np.sin(angle)], axis=1)
    basis *= np.sqrt(weight / length)[:, None, None]
    return np.where(np.abs(basis) < 1e-12, 0.0, basis)


def fine_basis(cells):
    return centred(HOCK, cells, (PATCH - 1) / 2)


def coarse_basis(cells):
    return centred(CH, cells, (CQ - 1) / 2)


def inverse_distance(square, ratio):
    return np.where(
        square > 0, 1.0 / (4.0 * math.pi * ratio * np.sqrt(np.maximum(square, 1))), 0.25 / ratio
    )


def line_spectra(length, reach, ratio):
    index = np.arange(length)
    wrap = np.minimum(index, length - index)
    side = np.arange(reach)
    square = side[:, None, None] ** 2 + side[None, :, None] ** 2 + wrap[None, None, :] ** 2
    kernel = inverse_distance(square, ratio)
    cosine = np.cos(2.0 * math.pi / length * np.outer(np.arange(length // 2 + 1), index))
    return np.einsum("fd,abd->fab", cosine, kernel)


def refine_table(fine, coarse):
    return np.maximum(0.0, 1.0 - np.abs((fine[:, None] + 0.5) / RATIO - 0.5 - coarse[None, :]))


def sign(odd, mirrored):
    return -1.0 if (odd and mirrored) else 1.0


def dense_table():
    spectra = line_spectra(HOCK, 36, 1)
    target = np.arange(20)[:, None] - RATIO
    source = np.arange(16)[None, :]
    near, far = np.abs(target - source), np.abs(target - (PATCH - 1 - source))
    result = np.empty((NF, 4, 2, 400, 256), ml_dtypes.bfloat16)

    def pick(first, second):
        return spectra[:, first[:, None, :, None], second[None, :, None, :]]

    terms = {(a, b): pick((near, far)[a], (near, far)[b]) for a in (0, 1) for b in (0, 1)}
    for parity in range(4):
        odd_z, odd_x = divmod(parity, 2)
        total = sum(sign(odd_z, a) * sign(odd_x, b) * terms[a, b] for a in (0, 1) for b in (0, 1))
        high, low = halves(0.25 * total.reshape(NF, 400, 256))
        result[:, parity, 0], result[:, parity, 1] = high, low
    return result


def coarse_dense_table():
    spectra = line_spectra(CH, 10, RATIO)
    window = np.arange(-2, CQ + 2)
    apart = np.abs(window[:, None] - np.arange(CQ)[None, :])
    kernel = spectra[:, apart[:, None, :, None], apart[None, :, None, :]]
    spread = refine_table(np.arange(20) - RATIO, window)
    kernel = np.einsum("za,xb,fabcd->fcdzx", spread, spread, kernel)
    result = np.empty((NC, 4, 2, 16, 400), ml_dtypes.bfloat16)
    for parity in range(4):
        odd_z, odd_x = divmod(parity, 2)
        mirrored = kernel[:, ::-1]
        total = kernel + (-1.0) ** odd_z * mirrored
        total = total + (-1.0) ** odd_x * total[:, :, ::-1]
        total = 0.25 * total[:, :4, :4].reshape(NC, 16, 400)
        result[:, parity, 0], result[:, parity, 1] = halves(total)
    return result


def forward_table():
    cells = np.arange(PATCH)
    lines = np.zeros((NG, 2, PATCH))
    lines[:NF] = fine_basis(cells)
    lines[NF : NF + NC] = coarse_basis(cells // RATIO)
    table = np.zeros((NG, 4, 2, 4, 4, 4, PATCH))
    for parity in range(4):
        odd_z, odd_x = divmod(parity, 2)
        for mirror in range(4):
            mirror_z, mirror_x = divmod(mirror, 2)
            factor = sign(odd_z, mirror_z) * sign(odd_x, mirror_x)
            for patch in range(4):
                table[:, parity, :, patch, mirror, patch] = factor * lines
    high, low = halves(table.reshape(12, 128, 512))
    return np.concatenate([high, low], axis=1)


def mirror_table():
    table = np.zeros((64, 128))
    for patch in range(4):
        for cell in range(16):
            table[patch * 16 + cell, patch * 32 + 31 - cell] = 1.0
    return table.astype(ml_dtypes.bfloat16)


def gather_table():
    table = np.zeros((16, 16, 4, 4))
    for z in range(16):
        for x in range(16):
            table[z, x, z // RATIO, x // RATIO] = 1.0
    return table.reshape(256, 16).astype(ml_dtypes.bfloat16)


def alias_weights():
    fine = np.arange(HOCK)
    spread = np.zeros((HOCK, CH))
    for shift in (-1, 0, 1):
        spread += refine_table(fine, np.arange(CH) + shift * CH)
    mapped = np.einsum("fct,tY,GcY->fcG", fine_basis(fine), spread, coarse_basis(np.arange(CH)))
    rest = np.arange(NF) % CH
    alias = np.minimum(rest, CH - rest)
    return mapped[np.arange(NF), :, alias]


BLOCK = 128
BEYOND = [128, 129, 130, 131, -4, -3, -2, -1]
UPPER = [128, 129, 130, 131, 124, 125, 126, 127]
LOWER = [0, 1, 2, 3, -4, -3, -2, -1]
PLACES = np.array(list(range(BLOCK)) + BEYOND + UPPER + LOWER)


def backward_table():
    table = np.zeros((160, 38, 2, 4))
    for patch in range(4):
        cells = PLACES - PATCH * patch
        inside = (cells >= -RATIO) & (cells < PATCH + RATIO)
        values = fine_basis(cells) * inside
        table[:152, :NF, :, patch] = values.transpose(2, 0, 1)
    return np.stack(halves(table.reshape(160, 304)))


def unfold_table():
    table = np.zeros((2, 2, 160, 2, 4, 2, 20))
    for odd in range(2):
        for patch in range(4):
            for row, place in enumerate(PLACES):
                cell = place - PATCH * patch + RATIO
                if 0 <= cell < 20:
                    column, value = cell, 1.0
                elif 20 <= cell < 40:
                    column, value = 39 - cell, sign(odd, 1)
                else:
                    continue
                for layer in range(2):
                    table[0, layer, row, odd, patch, layer, column] = value
                    table[1, layer, row, odd, patch, 1 - layer, column] = value
    return table.reshape(2, PAIRS, 320).astype(ml_dtypes.bfloat16)


def periodic_basis(length, cells):
    slots = np.arange(length)
    freq = np.where(slots <= length // 2, slots, slots - length // 2)
    weight = np.where((freq == 0) | (freq == length // 2), 1.0, 2.0)
    angle = 2.0 * math.pi / length * (freq[:, None] * cells[None, :] % length)
    basis = np.where((slots <= length // 2)[:, None], np.cos(angle), np.sin(angle))
    return basis * np.sqrt(weight / length)[:, None], freq


REACH = CQ + 2
SIDE = 34
LANES = 384


def far_tables(total_z, total_x, total_y, parts_x, parts_y):
    basis_y, freq_y = periodic_basis(total_y, np.arange(total_y))
    basis_x, freq_x = periodic_basis(total_x, np.arange(total_x))
    along_y = np.zeros((parts_y, 4, 32, 4, total_y))
    for layer in range(4):
        along_y[:, layer, :, layer, :] = basis_y.T.reshape(parts_y, 32, total_y)
    along_y = np.stack(halves(along_y.reshape(parts_y, 128, 4 * total_y)), axis=1)
    high, low = halves(basis_x.reshape(total_x, parts_x, 32).transpose(1, 0, 2))
    along_x = np.concatenate([high, high, low], axis=2)

    def eigen(freq, length):
        return 2.0 - 2.0 * np.cos(2.0 * math.pi / length * freq)

    freq_z = np.arange(total_z)
    square = (
        eigen(freq_z, total_z)[:, None, None]
        + eigen(freq_x, total_x)[None, :, None]
        + eigen(freq_y, total_y)[None, None, :]
    )
    square[0, 0, 0] = 1.0
    inverse = 1.0 / (RATIO * square)
    inverse[0, 0, 0] = 0.0
    steps = np.arange(total_z // 2 + 1)
    cosine = np.cos(2.0 * math.pi / total_z * np.outer(steps, freq_z)) / total_z
    column = np.einsum("dk,kxy->dxy", cosine, inverse).astype(np.float32)

    def windows(length, parts, basis):
        table = np.zeros((parts, 40, length))
        for part in range(parts):
            cells = (np.arange(SIDE) - 1 + part * 32) % length
            table[part, :SIDE] = basis[:, cells].T
        return table.reshape(parts * 40, length)

    square = eigen(freq_x, total_x)[:, None] + eigen(freq_y, total_y)[None, :]
    square[0, 0] = 1.0
    inverse = 1.0 / (RATIO * square)
    inverse[0, 0] = 0.0
    weight = np.outer(basis_x[:, :32].sum(axis=1), basis_y[:, :32].sum(axis=1)) * inverse
    flat = basis_x.T @ weight @ basis_y
    even = np.zeros((parts_x, parts_y, 40, LANES))
    for part in range(parts_x):
        cells_x = (np.arange(SIDE) - 1 + part * 32) % total_x
        for other in range(parts_y):
            cells_y = (np.arange(SIDE) - 1 + other * 32) % total_y
            values = flat[cells_x][:, cells_y].T
            even[part, other, :SIDE, : REACH * SIDE] = np.tile(values, (1, REACH))
    even = even.reshape(parts_x * parts_y, 40, LANES).astype(np.float32)

    back_x = np.concatenate(halves(windows(total_x, parts_x, basis_x)), axis=1)
    back_y = np.stack(halves(windows(total_y, parts_y, basis_y)))
    spread = refine_table(PLACES[:136], np.arange(SIDE) - 1)
    spread_x = np.zeros((REACH, 136, LANES))
    for layer in range(REACH):
        spread_x[layer, :, layer * SIDE : layer * SIDE + SIDE] = spread
    spread_y = np.zeros((40, 256))
    spread_y[:SIDE, :136] = spread.T
    spread_x = spread_x.reshape(REACH * 136, LANES).astype(ml_dtypes.bfloat16)
    spread_y = spread_y.astype(ml_dtypes.bfloat16)
    return along_y, along_x, column, back_x, back_y, even, spread_x, spread_y


def parts_of(values):
    high = values.astype(b16)
    return high, (values - high.astype(f32)).astype(b16)


def mul(left, right):
    return jnp.dot(left, right, preferred_element_type=f32)


def mul_nt(left, right):
    return lax.dot_general(left, right, (((1,), (1,)), ((), ())), preferred_element_type=f32)


def masses_kernel(rho_ref, sum_x_ref, sum_y_ref, out_ref):
    for half in range(2):
        total = jnp.zeros((32, 128), f32)
        for layer in range(4):
            z = (half * 4 + layer) * RATIO
            slab = rho_ref[pl.ds(z, RATIO)].reshape(RATIO * 128, 128)
            rows = mul(sum_x_ref[...], slab)
            high, rest = parts_of(rows)
            mid, low = parts_of(rows - high.astype(f32))
            weights = sum_y_ref[layer]
            total += mul(high, weights) + (mul(mid, weights) + mul(low, weights))
        for copy in range(out_ref.shape[0]):
            out_ref[copy, half * 32 : half * 32 + 32, :] = total


def near_kernel(
    weights_ref,
    rho_ref,
    forward_ref,
    mirror_ref,
    gather_ref,
    coarse_ref,
    backward_ref,
    dense_ref,
    wide_ref,
    upper_ref,
    lower_ref,
    lines,
    smooth,
    spectra,
    turned,
):
    step = pl.program_id(0)

    @pl.when(step == 0)
    def _():
        for z in range(PATCH):
            turned[z] = mul(mirror_ref[...], rho_ref[z]).astype(b16)
        for patch in range(4):
            def rows(mirror_z, mirror_x):
                tiles = []
                for z in range(16):
                    layer = PATCH - 1 - z if mirror_z else z
                    if mirror_x:
                        tiles.append(turned[layer, patch * 16 : patch * 16 + 16, :])
                    else:
                        tiles.append(rho_ref[layer, patch * 32 : patch * 32 + 16, :])
                return jnp.concatenate(tiles, axis=0)

            right = jnp.concatenate([rows(0, 0), rows(0, 1), rows(1, 0), rows(1, 1)], axis=1)

            def chunk(index, carry):
                both = mul_nt(forward_ref[index], right)
                both = both[:128] + both[128:]
                lines[pl.ds(index * 4, 4), :, patch] = both.reshape(4, 4, 8, 256)
                return carry

            lax.fori_loop(0, 12, chunk, 0)
        for parity in range(4):
            values = lines[NF : NF + NC, parity].reshape(NC * 32, 256)
            high, low = parts_of(values)
            sums = mul(high, gather_ref[...]) + mul(low, gather_ref[...])
            high, low = parts_of(sums)
            for freq in range(NC):
                first = high[freq * 32 : freq * 32 + 32]
                second = low[freq * 32 : freq * 32 + 32]
                smooth[freq, parity] = mul(first, coarse_ref[freq, parity, 0]) + (
                    mul(second, coarse_ref[freq, parity, 0])
                    + mul(first, coarse_ref[freq, parity, 1])
                )
        spectra[:, :, 8 * NF :, :] = jnp.zeros((4, 4, 8, 400), f32)

    rest = lax.rem(step, CH)
    alias = jnp.minimum(rest, CH - rest)
    row = lax.broadcasted_iota(jnp.int32, (32, 1), 0)
    weight = jnp.where(row % 8 < 4, weights_ref[step, 0], weights_ref[step, 1])
    for parity in range(4):
        high, low = parts_of(lines[step, parity].reshape(32, 256))
        both = mul_nt(jnp.concatenate([high, low], axis=0), dense_ref[0, parity, 0])
        value = both[:32] + (both[32:] + mul_nt(high, dense_ref[0, parity, 1]))
        value = value - weight * smooth[alias, parity]
        spectra[parity, :, pl.ds(step * 8, 8), :] = value.reshape(4, 8, 400)

    @pl.when(step == NF - 1)
    def _():
        def back(index, carry):
            parity, patch = index // 4, index % 4
            high, low = parts_of(spectra[parity, patch])
            value = mul(backward_ref[0], high) + (
                mul(backward_ref[1], high) + mul(backward_ref[0], low)
            )
            wide_ref[parity, patch] = value[:136]
            upper_ref[parity, patch] = value[136:144]
            lower_ref[parity, patch] = value[144:152]
            return carry

        lax.fori_loop(0, 16, back, 0)


def with_neighbours(values, from_lower, from_upper):
    first = lax.broadcasted_iota(jnp.int32, from_lower.shape, 0) < 4
    zero = jnp.zeros_like(from_lower)
    return jnp.concatenate(
        [
            values[0:8] + jnp.where(first, from_lower, zero),
            values[8:120],
            values[120:128] + jnp.where(first, zero, from_upper),
            values[128:136] + jnp.where(first, from_upper, from_lower),
        ],
        axis=0,
    )


def faces_kernel(wide_ref, from_lower_ref, from_upper_ref, bottom_ref, top_ref):
    even = with_neighbours(wide_ref[0, 0], from_lower_ref[0, 0], from_upper_ref[0, 0])
    odd = with_neighbours(wide_ref[1, 0], from_lower_ref[1, 0], from_upper_ref[1, 0])
    bottom_ref[0] = even + odd
    top_ref[0] = even - odd


def unfold_kernel(
    wide_ref,
    from_lower_ref,
    from_upper_ref,
    from_below_ref,
    from_above_ref,
    unfold_ref,
    near_ref,
    upper_ref,
    lower_ref,
    standing,
    given,
):
    def turn(index, carry):
        even = with_neighbours(wide_ref[0, index], from_lower_ref[0, index], from_upper_ref[0, index])
        odd = with_neighbours(wide_ref[1, index], from_lower_ref[1, index], from_upper_ref[1, index])
        for side, value in ((0, even + odd), (1, even - odd)):
            standing[side, index, :, 0:128] = value[:128].T
            standing[side, index, :, 128:136] = value[128:136].T
        for side, ref in ((0, from_below_ref), (1, from_above_ref)):
            value = ref[index]
            given[side, index, :, 0:128] = value[:128].T
            given[side, index, :, 128:136] = value[128:136].T
        return carry

    lax.fori_loop(0, 8, turn, 0)

    for pair in range(1, 10):
        for side in range(2):
            rows = jnp.concatenate(
                [standing[side, index, 40 * pair : 40 * pair + 40, :] for index in range(8)], axis=0
            )
            high, low = parts_of(rows)
            value = mul(unfold_ref[0], high) + mul(unfold_ref[0], low)
            if pair <= 3:
                other = 3 - pair
                rows = jnp.concatenate(
                    [given[side, index, 40 * other : 40 * other + 40, :] for index in range(8)],
                    axis=0,
                )
                high, low = parts_of(rows)
                value = value + (mul(unfold_ref[1], high) + mul(unfold_ref[1], low))
            for layer in range(2):
                z = 2 * pair + layer
                z = z - 2 if side == 0 else 37 - z
                near_ref[z] = value[160 * layer : 160 * layer + 136]
                upper_ref[z] = value[160 * layer + 136 : 160 * layer + 144]
                lower_ref[z] = value[160 * layer + 144 : 160 * layer + 152]


def far_kernel(
    where_ref,
    masses_ref,
    along_y_ref,
    along_x_ref,
    column_ref,
    back_x_ref,
    back_y_ref,
    even_ref,
    out_ref,
    spectra,
    lines,
    turned,
):
    blocks = masses_ref.shape[0]
    total = spectra.shape[0]
    masses = masses_ref[...].reshape(blocks * 64, 128)
    mean = jnp.sum(masses, axis=(0, 1), keepdims=True) * (1.0 / masses.size)
    high, low = parts_of(masses - mean)
    value = mul(high, along_y_ref[0, 0]) + (
        mul(low, along_y_ref[0, 0]) + mul(high, along_y_ref[0, 1])
    )
    high, low = parts_of(value)
    for half in range(2 * blocks):
        rows = slice(half * 32, half * 32 + 32)
        right = jnp.concatenate([high[rows], low[rows], high[rows]], axis=0)
        value = mul(along_x_ref[0], right)
        for layer in range(4):
            spectra[half * 4 + layer] = value[:, layer * 128 : layer * 128 + 128]

    start = where_ref[2] * CQ

    def solve(tile, carry):
        rows = pl.ds(pl.multiple_of(tile * 8, 8), 8)
        sums = [jnp.zeros((8, 128), f32) for _ in range(REACH)]
        for step in range(total):
            value = spectra[lax.rem(start + step, total), rows, :]
            for layer in range(REACH):
                apart = abs(step - (layer - 1)) % total
                sums[layer] += value * column_ref[min(apart, total - apart), rows, :]
        for layer in range(REACH):
            lines[layer, rows, :] = sums[layer]
        return carry

    lax.fori_loop(0, 16, solve, 0)

    turned[:, REACH * SIDE :, :] = jnp.zeros((4, LANES - REACH * SIDE, 128), f32)
    for layer in range(REACH):
        high, low = parts_of(lines[layer])
        value = mul(back_x_ref[:, 0:128], high) + (
            mul(back_x_ref[:, 0:128], low) + mul(back_x_ref[:, 128:256], high)
        )
        for part in range(4):
            turned[part, layer * SIDE : layer * SIDE + SIDE, :] = value[part * 40 : part * 40 + SIDE]
    for part in range(4):
        high, low = parts_of(turned[part])
        value = mul_nt(back_y_ref[0], high) + (
            mul_nt(back_y_ref[0], low) + mul_nt(back_y_ref[1], high)
        )
        for other in range(4):
            apart = lax.rem(part + 4 - where_ref[0], 4) * 4 + lax.rem(other + 4 - where_ref[1], 4)
            out_ref[part * 4 + other] = value[other * 40 : other * 40 + 40] + mean * even_ref[apart]


def final_kernel(
    near_ref,
    from_lower_ref,
    from_upper_ref,
    far_ref,
    spread_x_ref,
    spread_y_ref,
    potential_ref,
    force_ref,
    whole,
    planes,
    depth,
):
    step = pl.program_id(0)

    @pl.when(step == 0)
    def _():
        sums = far_ref[0]
        for source in range(1, far_ref.shape[0]):
            sums = sums + far_ref[source]
        high, low = parts_of(sums)
        for layer in range(REACH):
            left = spread_x_ref[layer * 136 : layer * 136 + 136, :]
            first, second = parts_of(mul_nt(left, high) + mul_nt(left, low))
            planes[layer] = mul(first, spread_y_ref[...]) + mul(second, spread_y_ref[...])
        for z in range(36):
            place = (z - 2 + 0.5) / RATIO - 0.5
            below = math.floor(place)
            upper = place - below
            value = with_neighbours(near_ref[z], from_lower_ref[z], from_upper_ref[z])
            whole[z] = value + (
                (1.0 - upper) * planes[below + 1] + upper * planes[below + 2]
            )

    row = lax.broadcasted_iota(jnp.int32, (128, 128), 0)
    lane = lax.broadcasted_iota(jnp.int32, (128, 128), 1)

    def difference(plus_one, minus_one, plus_two, minus_two):
        value = -(2.0 / 3.0 * (plus_one - minus_one) - 1.0 / 12.0 * (plus_two - minus_two))
        return value.astype(b16)

    def beyond(values, edge, mask, shift, axis):
        return pltpu.roll(jnp.where(mask, edge, values), shift, axis)

    for inner in range(depth):
        z = step * depth + inner + 2
        here = whole[z, 0:128, 0:128]
        potential_ref[inner] = here
        force_ref[0, inner] = difference(
            whole[z + 1, 0:128, 0:128],
            whole[z - 1, 0:128, 0:128],
            whole[z + 2, 0:128, 0:128],
            whole[z - 2, 0:128, 0:128],
        )
        edge = whole[z, 128:136, 0:128]
        above = jnp.concatenate([edge, here[8:]], axis=0)
        below = jnp.concatenate([here[:120], edge], axis=0)
        force_ref[1, inner] = difference(
            beyond(here, above, row < 1, 127, 0),
            beyond(here, below, row >= 127, 1, 0),
            beyond(here, above, row < 2, 126, 0),
            beyond(here, below, row >= 126, 2, 0),
        )
        above = whole[z, 0:128, 128:256]
        below = pltpu.roll(above, 120, 1)
        force_ref[2, inner] = difference(
            beyond(here, above, lane < 1, 127, 1),
            beyond(here, below, lane >= 127, 1, 1),
            beyond(here, above, lane < 2, 126, 1),
            beyond(here, below, lane >= 126, 2, 1),
        )


VMEM = pl.BlockSpec(memory_space=pltpu.VMEM)
SMEM = pl.BlockSpec(memory_space=pltpu.SMEM)


def params(size):
    return pltpu.CompilerParams(vmem_limit_bytes=size * MIB)


def cost(flops, moved):
    return pl.CostEstimate(flops=int(flops), bytes_accessed=int(moved), transcendentals=0)


def shape(*dims, dtype=f32):
    return jax.ShapeDtypeStruct(dims, dtype)


def make_tables(size_z, size_x, size_y):
    sum_x = np.zeros((32, RATIO, 128))
    for x in range(128):
        sum_x[x // RATIO, :, x] = 1.0
    sum_y = np.zeros((4, 128, 128))
    for layer in range(4):
        for y in range(128):
            sum_y[layer, y, layer * 32 + y // RATIO] = 1.0
    return dict(
        sum_x=sum_x.reshape(32, 512).astype(ml_dtypes.bfloat16),
        sum_y=sum_y.astype(ml_dtypes.bfloat16),
        weights=alias_weights().astype(np.float32),
        forward=forward_table(),
        mirror=mirror_table(),
        gather=gather_table(),
        coarse=coarse_dense_table(),
        backward=backward_table(),
        dense=dense_table(),
        unfold=unfold_table(),
        far=far_tables(size_z * CQ, size_x * 32, size_y * 32, size_x, size_y),
    )


def masses_of(density, tables, copies):
    return pl.pallas_call(
        masses_kernel,
        out_shape=shape(copies, 64, 128),
        in_specs=[VMEM] * 3,
        out_specs=VMEM,
        compiler_params=params(16),
        cost_estimate=cost(2e7, 1.2e6),
        name="masses",
    )(density, tables["sum_x"], tables["sum_y"])


def near_of(density, tables):
    return pl.pallas_call(
        near_kernel,
        grid=(NF,),
        out_shape=(shape(4, 4, 136, 400), shape(4, 4, 8, 400), shape(4, 4, 8, 400)),
        in_specs=[SMEM] + [VMEM] * 6
        + [pl.BlockSpec((1, 4, 2, 400, 256), lambda i: (i, 0, 0, 0, 0))],
        out_specs=(VMEM, VMEM, VMEM),
        scratch_shapes=[
            pltpu.VMEM((NG, 4, 4, 8, 256), f32),
            pltpu.VMEM((NC, 4, 32, 400), f32),
            pltpu.VMEM((4, 4, 304, 400), f32),
            pltpu.VMEM((PATCH, 64, 128), b16),
        ],
        compiler_params=params(56),
        cost_estimate=cost(8e9, 7e7),
        name="near",
    )(
        tables["weights"],
        density,
        tables["forward"],
        tables["mirror"],
        tables["gather"],
        tables["coarse"],
        tables["backward"],
        tables["dense"],
    )


def faces_of(wide, from_lower, from_upper):
    strip = pl.BlockSpec((2, 1, 8, 128), lambda i: (0, i, 0, 0))
    face = pl.BlockSpec((1, 136, 128), lambda i: (i, 0, 0))
    return pl.pallas_call(
        faces_kernel,
        grid=(8,),
        out_shape=(shape(8, 136, 128), shape(8, 136, 128)),
        in_specs=[pl.BlockSpec((2, 1, 136, 128), lambda i: (0, i, 0, 0)), strip, strip],
        out_specs=(face, face),
        compiler_params=params(16),
        cost_estimate=cost(1e6, 2.5e6),
        name="faces",
    )(wide, from_lower, from_upper)


def unfold_of(wide, from_lower, from_upper, from_below, from_above, tables):
    return pl.pallas_call(
        unfold_kernel,
        out_shape=(shape(36, 136, 256), shape(36, 8, 256), shape(36, 8, 256)),
        in_specs=[VMEM] * 6,
        out_specs=(VMEM, VMEM, VMEM),
        scratch_shapes=[
            pltpu.VMEM((2, 8, 400, 256), f32),
            pltpu.VMEM((2, 8, 128, 256), f32),
        ],
        compiler_params=params(56),
        cost_estimate=cost(4e9, 1.2e7),
        name="unfold",
    )(wide, from_lower, from_upper, from_below, from_above, tables["unfold"])


def far_of(where, masses, tables):
    along_y, along_x, column, back_x, back_y, even = tables["far"][:6]
    parts = along_x.shape[0] * along_y.shape[0]
    total = masses.shape[0] * CQ

    def fixed(*dims):
        return pl.BlockSpec(dims, lambda i, w: (0,) * len(dims))

    return pl.pallas_call(
        far_kernel,
        grid_spec=pltpu.PrefetchScalarGridSpec(
            num_scalar_prefetch=1,
            grid=(1,),
            in_specs=[
                fixed(*masses.shape),
                pl.BlockSpec((1, 2, 128, 512), lambda i, w: (w[1], 0, 0, 0)),
                pl.BlockSpec((1, 128, 96), lambda i, w: (w[0], 0, 0)),
                fixed(*column.shape),
                fixed(*back_x.shape),
                fixed(*back_y.shape),
                fixed(*even.shape),
            ],
            out_specs=fixed(parts, 40, LANES),
            scratch_shapes=[
                pltpu.VMEM((total, 128, 128), f32),
                pltpu.VMEM((REACH, 128, 128), f32),
                pltpu.VMEM((4, LANES, 128), f32),
            ],
        ),
        out_shape=shape(parts, 40, LANES),
        compiler_params=params(48),
        cost_estimate=cost(4e9, 9e6),
        name="far",
    )(where, masses, along_y, along_x, column, back_x, back_y, even)


def final_of(near, from_lower, from_upper, far, tables):
    depth = 4
    strip = pl.BlockSpec((36, 8, 256), lambda i: (0, 0, 0))
    return pl.pallas_call(
        functools.partial(final_kernel, depth=depth),
        grid=(PATCH // depth,),
        out_shape=(shape(PATCH, 128, 128), shape(3, PATCH, 128, 128, dtype=b16)),
        in_specs=[
            pl.BlockSpec((36, 136, 256), lambda i: (0, 0, 0)),
            strip,
            strip,
            pl.BlockSpec(far.shape, lambda i: (0, 0, 0)),
            pl.BlockSpec((REACH * 136, LANES), lambda i: (0, 0)),
            pl.BlockSpec((40, 256), lambda i: (0, 0)),
        ],
        out_specs=(
            pl.BlockSpec((depth, 128, 128), lambda i: (i, 0, 0)),
            pl.BlockSpec((3, depth, 128, 128), lambda i: (0, i, 0, 0)),
        ),
        scratch_shapes=[pltpu.VMEM((36, 136, 256), f32), pltpu.VMEM((REACH, 136, 256), f32)],
        compiler_params=params(48),
        cost_estimate=cost(2e8, 1.2e7),
        name="final",
    )(near, from_lower, from_upper, far, *tables["far"][6:])


def exchange(upper, lower, axis):
    count = lax.axis_size(axis)
    up = [(i, (i + 1) % count) for i in range(count)]
    down = [(target, source) for source, target in up]
    return lax.ppermute(upper, axis, up), lax.ppermute(lower, axis, down)


def body(tables, density):
    size_gz = lax.axis_size("gz")
    where = jnp.stack([lax.axis_index(axis) for axis in ("gx", "gy", "gz")]).astype(jnp.int32)
    masses = masses_of(density, tables, size_gz)
    masses = lax.all_to_all(masses, "gz", 0, 0, tiled=True)
    wide, upper, lower = near_of(density, tables)
    wide = wide.reshape(2, 8, 136, 400)
    from_lower, from_upper = exchange(upper, lower, "gy")
    from_lower = from_lower.reshape(2, 8, 8, 400)
    from_upper = from_upper.reshape(2, 8, 8, 400)
    far = far_of(where, masses, tables)
    far = lax.all_to_all(far, ("gx", "gy"), 0, 0, tiled=True)
    bottom, top = faces_of(wide, from_lower, from_upper)
    from_below, from_above = exchange(top, bottom, "gz")
    near, upper, lower = unfold_of(wide, from_lower, from_upper, from_below, from_above, tables)
    from_lower, from_upper = exchange(upper, lower, "gx")
    return final_of(near, from_lower, from_upper, far, tables)


def solution(mesh):
    tables = make_tables(mesh.shape["gz"], mesh.shape["gx"], mesh.shape["gy"])
    return jax.shard_map(
        functools.partial(body, tables),
        mesh=mesh,
        in_specs=(P("gz", "gx", "gy"),),
        out_specs=(P("gz", "gx", "gy"), P(None, "gz", "gx", "gy")),
        check_vma=False,
    )
```

time: 936 us -> 149 us (0.16)
  the two profiles are of different devices: /device:TPU:39 before, /device:TPU:1 now
where the time goes in v1:
time: 149 us; the launch traced here: 148 us
  Pallas kernels  101 us (68%)
  starting transfers between devices  23.2 us (16%)
  waiting for transfers between devices  14.7 us (10%)
  local copies, waits for them, and re-layouts  8.09 us (5%)
    pallas_call x1, Pallas kernels, near_of(): pl.pallas_call(near_kernel, grid=(NF,), out_shape=(shape(4, 4, 136, 400),...  65.9 us
    ppermute x6, waiting for transfers between devices, exchange(): return (lax.ppermute(upper, axis, up), lax.ppermute(lower, axis, down))  14.7 us
    pallas_call x1, Pallas kernels, unfold_of(): pl.pallas_call(unfold_kernel, out_shape=(shape(36, 136, 256), shape(36, 8...  12.7 us
    pallas_call x1, Pallas kernels, final_of(): pl.pallas_call(functools.partial(final_kernel, depth=depth), grid=(PATCH...  11.5 us
    ppermute x6, starting transfers between devices, exchange(): return (lax.ppermute(upper, axis, up), lax.ppermute(lower, axis, down))  9.62 us
    all_to_all x1, starting transfers between devices, body(): masses = lax.all_to_all(masses, 'gz', 0, 0, tiled=True)  8.16 us
    unnamed x28, local copies, waits for them, and re-layouts  8.09 us
    pallas_call x1, Pallas kernels, far_of(): pl.pallas_call(far_kernel, grid_spec=pltpu.PrefetchScalarGridSpec(num_sca...  6.87 us
  transfers between devices with their start and end apart: 8, of which 3 were waited for; matrix products, arithmetic and copies ran while one was open for 0% of the time, Pallas kernels for 60%

profile of v1, /device:TPU:1, one launch (start us, length us, event | category | flops | bytes accessed | tf_op | source)
XLA Modules:
  0.0 148.0 jit_solution(3408941514873582598)
XLA Ops:
  0.6 0.0 copy-start.1
  0.6 1.2 copy-done.1
  1.9 0.0 copy-start.5
  1.9 0.9 copy-done.5
  2.8 0.0 copy-start.6
  2.8 0.8 copy-done.6
  3.5 1.5 masses.1
  5.0 8.2 %all-to-all-start = ((f32[8,64,128]{2,1,0:T(8,128)}), f32[8,64,128]{2,1,0:T(8,128)S(1)}, u32[]{:S(2)}, u32[]{:S(2)}) async-start(f32[8,64,128]{2,1,0:T(8,128)} %masses.1), calls=%async_computation | async-start | bytes 524288 | tf_op jit(solution)/shard_map/all_to_all | solution.py:770
  13.1 0.0 copy-start.9
  13.1 0.0 copy-start.11
  13.2 0.0 copy-start.12
  13.2 0.0 copy-start.13
  13.2 65.9 %near.1 = (f32[4,4,136,400]{3,2,1,0:T(8,128)}, f32[4,4,8,400]{3,2,1,0:T(8,128)}, f32[4,4,8,400]{3,2,1,0:T(8,128)}) custom-call(f32[37,2]{1,0:T(8,128)} %constant.50.clone.weights_ref, bf16[32,128,128]{2,1,0:T(8,128)(2,1)} %rho_ref.3, bf16[12,256,512]{2,1,0:T(8,128)(2,1)} %constant.51.clone.forward_ref, bf16[64,128]{1,0:T(8,128)(2,1)} %constant.52.clone.mirror_ref, ...), custom_call_target="tpu_custom_call" | custom-call | flops 8000000000 | bytes 70000000 | tf_op jit(solution)/shard_map/near/pallas_call | solution.py:638
  79.1 1.6 %collective-permute-start = (f32[4,4,8,400]{3,2,1,0:T(8,128)}, f32[4,4,8,400]{3,2,1,0:T(8,128)S(1)}, u32[]{:S(2)}, u32[]{:S(2)}) collective-permute-start(f32[4,4,8,400]{3,2,1,0:T(8,128)} %get-tuple-element.11), channel_id=1, source_target_pairs={{0,8},{8,16},{16,24},{24,0},{1,9},{9,17},{17,25},{25,1},{2,10},{10... | collective-permute-start | bytes 614408 | tf_op jit(solution)/shard_map/ppermute | solution.py:763
  80.7 0.0 collective-permute-start.1
  80.7 0.1 pad_add_fusion.where_ref
  80.8 5.0 %collective-permute-done = f32[4,4,8,400]{3,2,1,0:T(8,128)S(1)} collective-permute-done((f32[4,4,8,400]{3,2,1,0:T(8,128)}, f32[4,4,8,400]{3,2,1,0:T(8,128)S(1)}, u32[]{:S(2)}, u32[]{:S(2)}) %collective-permute-start) | collective-permute-done | bytes 204832 | tf_op jit(solution)/shard_map/ppermute | solution.py:763
  85.8 0.0 copy-start.3
  85.8 2.4 %collective-permute-done.1 = f32[4,4,8,400]{3,2,1,0:T(8,128)S(1)} collective-permute-done((f32[4,4,8,400]{3,2,1,0:T(8,128)}, f32[4,4,8,400]{3,2,1,0:T(8,128)S(1)}, u32[]{:S(2)}, u32[]{:S(2)}) %collective-permute-start.1) | collective-permute-done | bytes 204832 | tf_op jit(solution)/shard_map/ppermute | solution.py:763
  88.2 0.0 copy-start.4
  88.2 2.4 %copy-done = f32[4,4,136,400]{3,2,1,0:T(8,128)S(1)} copy-done((f32[4,4,136,400]{3,2,1,0:T(8,128)S(1)}, f32[4,4,136,400]{3,2,1,0:T(8,128)}, u32[]{:S(2)}) %copy-start) | copy-done | bytes 3481624
  90.6 2.7 %faces.1 = (f32[8,136,128]{2,1,0:T(8,128)S(1)}, f32[8,136,128]{2,1,0:T(8,128)}) custom-call(f32[2,8,136,400]{3,2,1,0:T(8,128)S(1)} %bitcast.7, f32[2,8,8,400]{3,2,1,0:T(8,128)S(1)} %bitcast.8, f32[2,8,8,400]{3,2,1,0:T(8,128)S(1)} %bitcast.10), custom_call_target="tpu_custom_call" | custom-call | flops 1000000 | bytes 2500000 | tf_op jit(solution)/shard_map/faces/pallas_call | solution.py:669
  93.3 1.7 %collective-permute-start.2 = (f32[8,136,128]{2,1,0:T(8,128)}, f32[8,136,128]{2,1,0:T(8,128)}, u32[]{:S(2)}, u32[]{:S(2)}) collective-permute-start(f32[8,136,128]{2,1,0:T(8,128)} %get-tuple-element.13), channel_id=1, source_target_pairs={{0,1},{1,2},{2,3},{3,4},{4,5},{5,6},{6,7},{7,0},{8,9},{9,10},{10,1... | collective-permute-start | bytes 1671176 | tf_op jit(solution)/shard_map/ppermute | solution.py:763
  95.0 3.6 %collective-permute-start.3 = (f32[8,136,128]{2,1,0:T(8,128)S(1)}, f32[8,136,128]{2,1,0:T(8,128)}, u32[]{:S(2)}, u32[]{:S(2)}) collective-permute-start(f32[8,136,128]{2,1,0:T(8,128)S(1)} %get-tuple-element.14), channel_id=1, source_target_pairs={{1,0},{2,1},{3,2},{4,3},{5,4},{6,5},{7,6},{0,7},{9,8},{10,9},{11,1... | collective-permute-start | bytes 1671176 | tf_op jit(solution)/shard_map/ppermute | solution.py:763
  98.6 0.0 all-to-all-done.masses_ref
  98.6 0.0 copy-done.9
  98.6 0.0 copy-done.11
  98.6 0.0 copy-done.12
  98.7 0.0 copy-done.13
  98.7 0.0 copy-start.8
  98.7 1.6 %copy-done.8 = f32[33,128,128]{2,1,0:T(8,128)S(1)} copy-done((f32[33,128,128]{2,1,0:T(8,128)S(1)}, f32[33,128,128]{2,1,0:T(8,128)}, u32[]{:S(2)}) %copy-start.8) | copy-done | bytes 2162712
  100.3 1.2 copy-done.10
  101.5 6.9 %far.1 = f32[16,40,384]{2,1,0:T(8,128)} custom-call(s32[3]{0:T(128)S(1)} %pad_add_fusion.where_ref, f32[8,64,128]{2,1,0:T(8,128)S(1)} %all-to-all-done.masses_ref, bf16[4,2,128,512]{3,2,1,0:T(8,128)(2,1)S(1)} %copy-done.9, bf16[4,128,96]{2,1,0:T(8,128)(2,1)S(1)} %copy-done.11, f32[33,128,128]{2,1,0:T(8,128)S(1)} %copy-done.8, ...), custom_call_target="tpu_custom_call" | custom-call | flops 4000000000 | bytes 9000000 | tf_op jit(solution)/shard_map/far/pallas_call | solution.py:705
  108.4 0.0 copy-done.3
  108.4 0.0 copy-done.4
  108.4 5.4 %all-to-all-start.1 = ((f32[16,40,384]{2,1,0:T(8,128)}), f32[16,40,384]{2,1,0:T(8,128)S(1)}, u32[]{:S(2)}, u32[]{:S(2)}) async-start(f32[16,40,384]{2,1,0:T(8,128)} %far.1), calls=%async_computation.1 | async-start | bytes 1966080 | tf_op jit(solution)/shard_map/all_to_all | solution.py:777
  113.7 0.0 copy-start.7
  113.8 0.0 collective-permute-done.2.from_below_ref
  113.8 0.0 collective-permute-done.3.from_above_ref
  113.8 12.7 %unfold.1 = (f32[36,136,256]{2,1,0:T(8,128)}, f32[36,8,256]{2,1,0:T(8,128)}, f32[36,8,256]{2,1,0:T(8,128)}) custom-call(f32[2,8,136,400]{3,2,1,0:T(8,128)} %bitcast.6, f32[2,8,8,400]{3,2,1,0:T(8,128)} %bitcast.9, f32[2,8,8,400]{3,2,1,0:T(8,128)} %bitcast.11, f32[8,136,128]{2,1,0:T(8,128)} %collective-permute-done.2.from_below_ref, ...), custom_call_target="tpu_custom_call" | custom-call | flops 4000000000 | bytes 12000000 | tf_op jit(solution)/shard_map/unfold/pallas_call | solution.py:682
  126.5 1.4 collective-permute-start.4
  127.9 1.3 collective-permute-start.5
  129.2 7.3 %collective-permute-done.4.from_lower_ref = f32[36,8,256]{2,1,0:T(8,128)S(1)} collective-permute-done((f32[36,8,256]{2,1,0:T(8,128)}, f32[36,8,256]{2,1,0:T(8,128)S(1)}, u32[]{:S(2)}, u32[]{:S(2)}) %collective-permute-start.4) | collective-permute-done | bytes 294944 | tf_op jit(solution)/shard_map/ppermute | solution.py:763
  136.5 0.0 collective-permute-done.5.from_upper_ref
  136.5 0.0 all-to-all-done.1.far_ref
  136.5 0.0 copy-done.2
  136.5 0.0 copy-done.7
  136.5 11.5 %final.1 = (f32[32,128,128]{2,1,0:T(8,128)}, bf16[3,32,128,128]{3,2,1,0:T(8,128)(2,1)}) custom-call(f32[36,136,256]{2,1,0:T(8,128)} %get-tuple-element.15.near_ref, f32[36,8,256]{2,1,0:T(8,128)S(1)} %collective-permute-done.4.from_lower_ref, f32[36,8,256]{2,1,0:T(8,128)S(1)} %collective-permute-done.5.from_upper_ref, ...), custom_call_target="tpu_custom_call" | custom-call | flops 200000000 | bytes 12000000 | tf_op jit(solution)/shard_map/final/pallas_call | solution.py:736
  (3 shorter events, 0.0 us)
Async XLA Ops:
  0.6 1.2 copy-start.1
  1.9 0.9 copy-start.5
  2.8 0.8 copy-start.6
  5.0 93.7 %all-to-all-start = ((f32[8,64,128]{2,1,0:T(8,128)}), f32[8,64,128]{2,1,0:T(8,128)S(1)}, u32[]{:S(2)}, u32[]{:S(2)}) async-start(f32[8,64,128]{2,1,0:T(8,128)} %masses.1), calls=%async_computation | async-start | bytes 524288 | tf_op jit(solution)/shard_map/all_to_all | solution.py:770
  13.1 85.5 %copy-start.9 = (bf16[4,2,128,512]{3,2,1,0:T(8,128)(2,1)S(1)}, bf16[4,2,128,512]{3,2,1,0:T(8,128)(2,1)}, u32[]{:S(2)}) copy-start(bf16[4,2,128,512]{3,2,1,0:T(8,128)(2,1)} %constant.57.clone.along_y_ref) | copy-start | bytes 3145732
  13.1 85.5 %copy-start.11 = (bf16[4,128,96]{2,1,0:T(8,128)(2,1)S(1)}, bf16[4,128,96]{2,1,0:T(8,128)(2,1)}, u32[]{:S(2)}) copy-start(bf16[4,128,96]{2,1,0:T(8,128)(2,1)} %constant.58.clone.along_x_ref) | copy-start | bytes 294916
  13.2 85.5 %copy-start.12 = (bf16[160,256]{1,0:T(8,128)(2,1)S(1)}, bf16[160,256]{1,0:T(8,128)(2,1)}, u32[]{:S(2)}) copy-start(bf16[160,256]{1,0:T(8,128)(2,1)} %constant.60.clone.back_x_ref) | copy-start | bytes 245764
  13.2 85.5 %copy-start.13 = (bf16[2,160,128]{2,1,0:T(8,128)(2,1)S(1)}, bf16[2,160,128]{2,1,0:T(8,128)(2,1)}, u32[]{:S(2)}) copy-start(bf16[2,160,128]{2,1,0:T(8,128)(2,1)} %constant.61.clone.back_y_ref) | copy-start | bytes 245764
  79.1 6.7 %collective-permute-start = (f32[4,4,8,400]{3,2,1,0:T(8,128)}, f32[4,4,8,400]{3,2,1,0:T(8,128)S(1)}, u32[]{:S(2)}, u32[]{:S(2)}) collective-permute-start(f32[4,4,8,400]{3,2,1,0:T(8,128)} %get-tuple-element.11), channel_id=1, source_target_pairs={{0,8},{8,16},{16,24},{24,0},{1,9},{9,17},{17,25},{25,1},{2,10},{10... | collective-permute-start | bytes 614408 | tf_op jit(solution)/shard_map/ppermute | solution.py:763
  80.7 7.5 %collective-permute-start.1 = (f32[4,4,8,400]{3,2,1,0:T(8,128)}, f32[4,4,8,400]{3,2,1,0:T(8,128)S(1)}, u32[]{:S(2)}, u32[]{:S(2)}) collective-permute-start(f32[4,4,8,400]{3,2,1,0:T(8,128)} %get-tuple-element.12), channel_id=1, source_target_pairs={{8,0},{16,8},{24,16},{0,24},{9,1},{17,9},{25,17},{1,25},{10,2},{18... | collective-permute-start | bytes 614408 | tf_op jit(solution)/shard_map/ppermute | solution.py:763
  85.8 22.6 %copy-start.3 = (f32[4,4,8,400]{3,2,1,0:T(8,128)}, f32[4,4,8,400]{3,2,1,0:T(8,128)S(1)}, u32[]{:S(2)}) copy-start(f32[4,4,8,400]{3,2,1,0:T(8,128)S(1)} %collective-permute-done) | copy-start | bytes 614404
  88.2 20.2 %copy-start.4 = (f32[4,4,8,400]{3,2,1,0:T(8,128)}, f32[4,4,8,400]{3,2,1,0:T(8,128)S(1)}, u32[]{:S(2)}) copy-start(f32[4,4,8,400]{3,2,1,0:T(8,128)S(1)} %collective-permute-done.1) | copy-start | bytes 614404
  88.2 2.4 %copy-start = (f32[4,4,136,400]{3,2,1,0:T(8,128)S(1)}, f32[4,4,136,400]{3,2,1,0:T(8,128)}, u32[]{:S(2)}) copy-start(f32[4,4,136,400]{3,2,1,0:T(8,128)} %get-tuple-element.10) | copy-start | bytes 10444804
  93.3 20.5 %collective-permute-start.2 = (f32[8,136,128]{2,1,0:T(8,128)}, f32[8,136,128]{2,1,0:T(8,128)}, u32[]{:S(2)}, u32[]{:S(2)}) collective-permute-start(f32[8,136,128]{2,1,0:T(8,128)} %get-tuple-element.13), channel_id=1, source_target_pairs={{0,1},{1,2},{2,3},{3,4},{4,5},{5,6},{6,7},{7,0},{8,9},{9,10},{10,1... | collective-permute-start | bytes 1671176 | tf_op jit(solution)/shard_map/ppermute | solution.py:763
  95.0 18.8 %collective-permute-start.3 = (f32[8,136,128]{2,1,0:T(8,128)S(1)}, f32[8,136,128]{2,1,0:T(8,128)}, u32[]{:S(2)}, u32[]{:S(2)}) collective-permute-start(f32[8,136,128]{2,1,0:T(8,128)S(1)} %get-tuple-element.14), channel_id=1, source_target_pairs={{1,0},{2,1},{3,2},{4,3},{5,4},{6,5},{7,6},{0,7},{9,8},{10,9},{11,1... | collective-permute-start | bytes 1671176 | tf_op jit(solution)/shard_map/ppermute | solution.py:763
  98.7 1.6 %copy-start.8 = (f32[33,128,128]{2,1,0:T(8,128)S(1)}, f32[33,128,128]{2,1,0:T(8,128)}, u32[]{:S(2)}) copy-start(f32[33,128,128]{2,1,0:T(8,128)} %constant.59.clone.column_ref) | copy-start | bytes 6488068
  100.3 1.2 copy-start.10
  108.4 28.2 %all-to-all-start.1 = ((f32[16,40,384]{2,1,0:T(8,128)}), f32[16,40,384]{2,1,0:T(8,128)S(1)}, u32[]{:S(2)}, u32[]{:S(2)}) async-start(f32[16,40,384]{2,1,0:T(8,128)} %far.1), calls=%async_computation.1 | async-start | bytes 1966080 | tf_op jit(solution)/shard_map/all_to_all | solution.py:777
  113.7 22.8 %copy-start.2 = (bf16[1360,384]{1,0:T(8,128)(2,1)S(1)}, bf16[1360,384]{1,0:T(8,128)(2,1)}, u32[]{:S(2)}) copy-start(bf16[1360,384]{1,0:T(8,128)(2,1)} %constant.64.clone.spread_x_ref) | copy-start | bytes 3133444
  113.7 22.8 %copy-start.7 = (bf16[40,256]{1,0:T(8,128)(2,1)S(1)}, bf16[40,256]{1,0:T(8,128)(2,1)}, u32[]{:S(2)}) copy-start(bf16[40,256]{1,0:T(8,128)(2,1)} %constant.65.clone.spread_y_ref) | copy-start | bytes 61444
  126.5 10.0 %collective-permute-start.4 = (f32[36,8,256]{2,1,0:T(8,128)}, f32[36,8,256]{2,1,0:T(8,128)S(1)}, u32[]{:S(2)}, u32[]{:S(2)}) collective-permute-start(f32[36,8,256]{2,1,0:T(8,128)} %get-tuple-element.16), channel_id=1, source_target_pairs={{0,32},{32,64},{64,96},{96,0},{1,33},{33,65},{65,97},{97,1},{2,34}... | collective-permute-start | bytes 884744 | tf_op jit(solution)/shard_map/ppermute | solution.py:763
  127.9 8.6 %collective-permute-start.5 = (f32[36,8,256]{2,1,0:T(8,128)}, f32[36,8,256]{2,1,0:T(8,128)S(1)}, u32[]{:S(2)}, u32[]{:S(2)}) collective-permute-start(f32[36,8,256]{2,1,0:T(8,128)} %get-tuple-element.17), channel_id=1, source_target_pairs={{32,0},{64,32},{96,64},{0,96},{33,1},{65,33},{97,65},{1,97},{34,2}... | collective-permute-start | bytes 884744 | tf_op jit(solution)/shard_map/ppermute | solution.py:763

commit v2 on v1

--- a/solution.py
+++ b/solution.py
@@ -18,6 +18,9 @@
 NF = HOCK // 2 + 1
 NC = CH // 2 + 1
 NG = 48
+NR = 40
+RING = 16
+ROWS = 1056
 PAIRS = 320
 
 f32 = jnp.float32
@@ -72,23 +75,73 @@
     return -1.0 if (odd and mirrored) else 1.0
 
 
+def swap_pairs(count):
+    first, second = np.triu_indices(count)
+    above, beyond = np.triu_indices(count, 1)
+    return (first, second), (above, beyond)
+
+
 def dense_table():
     spectra = line_spectra(HOCK, 36, 1)
-    target = np.arange(20)[:, None] - RATIO
-    source = np.arange(16)[None, :]
+    target = np.arange(20)[None, :] - RATIO
+    source = np.arange(16)[:, None]
     near, far = np.abs(target - source), np.abs(target - (PATCH - 1 - source))
-    result = np.empty((NF, 4, 2, 400, 256), ml_dtypes.bfloat16)
 
     def pick(first, second):
         return spectra[:, first[:, None, :, None], second[None, :, None, :]]
 
     terms = {(a, b): pick((near, far)[a], (near, far)[b]) for a in (0, 1) for b in (0, 1)}
+    table = np.zeros((NF, ROWS, 256))
     for parity in range(4):
         odd_z, odd_x = divmod(parity, 2)
+        if parity == 2:
+            continue
         total = sum(sign(odd_z, a) * sign(odd_x, b) * terms[a, b] for a in (0, 1) for b in (0, 1))
-        high, low = halves(0.25 * total.reshape(NF, 400, 256))
-        result[:, parity, 0], result[:, parity, 1] = high, low
+        total = 0.25 * total
+        if parity == 1:
+            flat = total.reshape(NF, 256, 400)
+            table[:, 544:800] = flat[:, :, :256]
+            table[:, 800:1056, :144] = flat[:, :, 256:]
+            continue
+        base = 0 if parity == 0 else 272
+        whole_in, strict_in = swap_pairs(16)
+        whole_out, strict_out = swap_pairs(20)
+        swapped = total.transpose(0, 2, 1, 3, 4)
+        both, less = 0.5 * (total + swapped), 0.5 * (total - swapped)
+        table[:, base : base + 136, :210] = both[:, whole_in[0], whole_in[1]][
+            :, :, whole_out[0], whole_out[1]
+        ]
+        table[:, base + 144 : base + 264, :190] = less[:, strict_in[0], strict_in[1]][
+            :, :, strict_out[0], strict_out[1]
+        ]
+    result = np.empty((NF, 2, ROWS, 256), ml_dtypes.bfloat16)
+    result[:, 0], result[:, 1] = halves(table)
     return result
+
+
+def swap_tables():
+    whole, strict = swap_pairs(16)
+    inward = np.zeros((16, 16, 384))
+    spots = np.arange(136)
+    inward[whole[0], whole[1], spots] = 1.0
+    inward[whole[1], whole[0], spots] = 1.0
+    spots = 256 + np.arange(120)
+    inward[strict[0], strict[1], spots] = 1.0
+    inward[strict[1], strict[0], spots] = -1.0
+    whole, strict = swap_pairs(20)
+    outward = np.zeros((2, 512, 20, 20))
+    spots = np.arange(210)
+    outward[0, spots, whole[0], whole[1]] = 1.0
+    outward[0, spots, whole[1], whole[0]] = 1.0
+    spots = 256 + np.arange(190)
+    outward[0, spots, strict[0], strict[1]] = 1.0
+    outward[0, spots, strict[1], strict[0]] = -1.0
+    outward[1, :400] = np.eye(400).reshape(20, 20, 20, 20).transpose(1, 0, 2, 3).reshape(400, 20, 20)
+    turn = np.eye(256).reshape(16, 16, 16, 16).transpose(1, 0, 2, 3).reshape(256, 256)
+    return tuple(
+        table.astype(ml_dtypes.bfloat16)
+        for table in (inward.reshape(256, 384), turn, outward.reshape(2, 512, 400))
+    )
 
 
 def coarse_dense_table():
@@ -98,14 +151,24 @@
     kernel = spectra[:, apart[:, None, :, None], apart[None, :, None, :]]
     spread = refine_table(np.arange(20) - RATIO, window)
     kernel = np.einsum("za,xb,fabcd->fcdzx", spread, spread, kernel)
-    result = np.empty((NC, 4, 2, 16, 400), ml_dtypes.bfloat16)
+    whole, strict = swap_pairs(20)
+    result = np.empty((NC, 4, 2, 16, 512), ml_dtypes.bfloat16)
     for parity in range(4):
         odd_z, odd_x = divmod(parity, 2)
         mirrored = kernel[:, ::-1]
         total = kernel + (-1.0) ** odd_z * mirrored
         total = total + (-1.0) ** odd_x * total[:, :, ::-1]
-        total = 0.25 * total[:, :4, :4].reshape(NC, 16, 400)
-        result[:, parity, 0], result[:, parity, 1] = halves(total)
+        total = 0.25 * total[:, :4, :4].reshape(NC, 16, 20, 20)
+        swapped = total.transpose(0, 1, 3, 2)
+        table = np.zeros((NC, 16, 512))
+        if parity == 1:
+            table[:, :, :400] = total.reshape(NC, 16, 400)
+        elif parity == 2:
+            table[:, :, :400] = swapped.reshape(NC, 16, 400)
+        else:
+            table[:, :, :210] = (0.5 * (total + swapped))[:, :, whole[0], whole[1]]
+            table[:, :, 256:446] = (0.5 * (total - swapped))[:, :, strict[0], strict[1]]
+        result[:, parity, 0], result[:, parity, 1] = halves(table)
     return result
 
 
@@ -114,15 +177,10 @@
     lines = np.zeros((NG, 2, PATCH))
     lines[:NF] = fine_basis(cells)
     lines[NF : NF + NC] = coarse_basis(cells // RATIO)
-    table = np.zeros((NG, 4, 2, 4, 4, 4, PATCH))
-    for parity in range(4):
-        odd_z, odd_x = divmod(parity, 2)
-        for mirror in range(4):
-            mirror_z, mirror_x = divmod(mirror, 2)
-            factor = sign(odd_z, mirror_z) * sign(odd_x, mirror_x)
-            for patch in range(4):
-                table[:, parity, :, patch, mirror, patch] = factor * lines
-    high, low = halves(table.reshape(12, 128, 512))
+    table = np.zeros((NG, 2, 4, 4, PATCH))
+    for patch in range(4):
+        table[:, :, patch, patch] = lines
+    high, low = halves(table.reshape(4, 96, 128))
     return np.concatenate([high, low], axis=1)
 
 
@@ -276,19 +334,38 @@
     return lax.dot_general(left, right, (((1,), (1,)), ((), ())), preferred_element_type=f32)
 
 
-def masses_kernel(rho_ref, sum_x_ref, sum_y_ref, out_ref):
+def masses_kernel(rho_ref, out_ref):
+    row = lax.broadcasted_iota(jnp.int32, (32, 512), 0)
+    column = lax.broadcasted_iota(jnp.int32, (32, 512), 1)
+    sum_x = jnp.where(column % 128 // RATIO == row, 1.0, 0.0).astype(b16)
+    row = lax.broadcasted_iota(jnp.int32, (128, 128), 0)
+    column = lax.broadcasted_iota(jnp.int32, (128, 128), 1)
     for half in range(2):
         total = jnp.zeros((32, 128), f32)
         for layer in range(4):
             z = (half * 4 + layer) * RATIO
             slab = rho_ref[pl.ds(z, RATIO)].reshape(RATIO * 128, 128)
-            rows = mul(sum_x_ref[...], slab)
+            rows = mul(sum_x, slab)
             high, rest = parts_of(rows)
             mid, low = parts_of(rows - high.astype(f32))
-            weights = sum_y_ref[layer]
+            weights = jnp.where(row // RATIO + layer * 32 == column, 1.0, 0.0).astype(b16)
             total += mul(high, weights) + (mul(mid, weights) + mul(low, weights))
         for copy in range(out_ref.shape[0]):
             out_ref[copy, half * 32 : half * 32 + 32, :] = total
+
+
+def mul_pairs(values, high_table, low_table):
+    rows = values.shape[0]
+    high, low = parts_of(values)
+    both = mul(jnp.concatenate([high, low], axis=0), high_table)
+    return both[:rows] + (both[rows:] + mul(high, low_table))
+
+
+def mul_exact(values, table):
+    rows = values.shape[0]
+    high, low = parts_of(values)
+    both = mul(jnp.concatenate([high, low], axis=0), table)
+    return both[:rows] + both[rows:]
 
 
 def near_kernel(
@@ -299,80 +376,147 @@
     gather_ref,
     coarse_ref,
     backward_ref,
+    inward_ref,
+    turn_ref,
+    outward_ref,
     dense_ref,
     wide_ref,
     upper_ref,
     lower_ref,
+    bottom_ref,
+    top_ref,
     lines,
+    ready,
     smooth,
     spectra,
     turned,
+    ring,
+    arrived,
 ):
-    step = pl.program_id(0)
-
-    @pl.when(step == 0)
-    def _():
-        for z in range(PATCH):
-            turned[z] = mul(mirror_ref[...], rho_ref[z]).astype(b16)
-        for patch in range(4):
-            def rows(mirror_z, mirror_x):
-                tiles = []
-                for z in range(16):
-                    layer = PATCH - 1 - z if mirror_z else z
-                    if mirror_x:
-                        tiles.append(turned[layer, patch * 16 : patch * 16 + 16, :])
-                    else:
-                        tiles.append(rho_ref[layer, patch * 32 : patch * 32 + 16, :])
-                return jnp.concatenate(tiles, axis=0)
-
-            right = jnp.concatenate([rows(0, 0), rows(0, 1), rows(1, 0), rows(1, 1)], axis=1)
-
-            def chunk(index, carry):
-                both = mul_nt(forward_ref[index], right)
-                both = both[:128] + both[128:]
-                lines[pl.ds(index * 4, 4), :, patch] = both.reshape(4, 4, 8, 256)
-                return carry
-
-            lax.fori_loop(0, 12, chunk, 0)
-        for parity in range(4):
-            values = lines[NF : NF + NC, parity].reshape(NC * 32, 256)
-            high, low = parts_of(values)
-            sums = mul(high, gather_ref[...]) + mul(low, gather_ref[...])
-            high, low = parts_of(sums)
-            for freq in range(NC):
-                first = high[freq * 32 : freq * 32 + 32]
-                second = low[freq * 32 : freq * 32 + 32]
-                smooth[freq, parity] = mul(first, coarse_ref[freq, parity, 0]) + (
-                    mul(second, coarse_ref[freq, parity, 0])
-                    + mul(first, coarse_ref[freq, parity, 1])
+    def fetch(freq, slot):
+        return pltpu.make_async_copy(dense_ref.at[freq], ring.at[slot], arrived.at[slot])
+
+    for slot in range(RING):
+        fetch(slot, slot).start()
+
+    for z in range(PATCH):
+        turned[z] = mul(mirror_ref[...], rho_ref[z]).astype(b16)
+    for patch in range(4):
+        def rows(mirror_z, mirror_x):
+            tiles = []
+            for z in range(16):
+                layer = PATCH - 1 - z if mirror_z else z
+                if mirror_x:
+                    tiles.append(turned[layer, patch * 16 : patch * 16 + 16, :])
+                else:
+                    tiles.append(rho_ref[layer, patch * 32 : patch * 32 + 16, :])
+            return jnp.concatenate(tiles, axis=0)
+
+        right = [rows(0, 0), rows(0, 1), rows(1, 0), rows(1, 1)]
+
+        def chunk(index, carry):
+            left = forward_ref[index]
+            sums = []
+            for mirror in range(4):
+                both = mul_nt(left, right[mirror])
+                sums.append(both[:96] + both[96:])
+            even, odd = sums[0] + sums[1], sums[0] - sums[1]
+            even_far, odd_far = sums[2] + sums[3], sums[2] - sums[3]
+            freqs = pl.ds(index * 12, 12)
+            lines[freqs, 0, patch] = (even + even_far).reshape(12, 8, 256)
+            lines[freqs, 1, patch] = (odd + odd_far).reshape(12, 8, 256)
+            lines[freqs, 2, patch] = (even - even_far).reshape(12, 8, 256)
+            lines[freqs, 3, patch] = (odd - odd_far).reshape(12, 8, 256)
+            return carry
+
+        lax.fori_loop(0, 4, chunk, 0)
+
+    for parity in range(4):
+        values = lines[NF : NF + NC, parity].reshape(NC * 32, 256)
+        high, low = parts_of(mul_exact(values, gather_ref[...]))
+        for freq in range(NC):
+            both = jnp.concatenate(
+                [high[freq * 32 : freq * 32 + 32], low[freq * 32 : freq * 32 + 32]], axis=0
+            )
+            value = mul(both, coarse_ref[freq, parity, 0])
+            smooth[freq, parity] = value[:32] + (
+                value[32:] + mul(both[:32], coarse_ref[freq, parity, 1])
+            )
+
+    def prepare(index, carry):
+        freqs = pl.ds(index * 4, 4)
+        for slot, parity in ((0, 0), (1, 3)):
+            values = lines[freqs, parity].reshape(128, 256)
+            ready[freqs, slot] = mul_exact(values, inward_ref[...]).reshape(4, 32, 384)
+        values = lines[freqs, 2].reshape(128, 256)
+        ready[freqs, 2, :, 0:256] = mul_exact(values, turn_ref[...]).reshape(4, 32, 256)
+        return carry
+
+    lax.fori_loop(0, NR // 4, prepare, 0)
+    spectra[:, :, 8 * NF :, :] = jnp.zeros((4, 4, 8, 512), f32)
+    row = lax.broadcasted_iota(jnp.int32, (32, 1), 0)
+
+    def solve(freq, carry):
+        slot = lax.rem(freq, RING)
+        fetch(freq, slot).wait()
+        rest = lax.rem(freq, CH)
+        alias = jnp.minimum(rest, CH - rest)
+        weight = jnp.where(row % 8 < 4, weights_ref[freq, 0], weights_ref[freq, 1])
+        here = pl.ds(freq * 8, 8)
+
+        def keep(parity, low, high, value):
+            value = value - weight * smooth[alias, parity, :, low:high]
+            spectra[parity, :, here, low:high] = value.reshape(4, 8, 256)
+
+        for place, parity in ((0, 0), (1, 3)):
+            for base, count, lane in ((0, 144, 0), (144, 128, 256)):
+                base = base + 272 * place
+                value = mul_pairs(
+                    ready[freq, place, :, lane : lane + count],
+                    ring[slot, 0, base : base + count, :],
+                    ring[slot, 1, base : base + count, :],
                 )
-        spectra[:, :, 8 * NF :, :] = jnp.zeros((4, 4, 8, 400), f32)
-
-    rest = lax.rem(step, CH)
-    alias = jnp.minimum(rest, CH - rest)
-    row = lax.broadcasted_iota(jnp.int32, (32, 1), 0)
-    weight = jnp.where(row % 8 < 4, weights_ref[step, 0], weights_ref[step, 1])
+                keep(parity, lane, lane + 256, value)
+        values = jnp.concatenate(
+            [lines[freq, 1].reshape(32, 256), ready[freq, 2, :, 0:256]], axis=0
+        )
+        for base, lane in ((544, 0), (800, 256)):
+            value = mul_pairs(
+                values, ring[slot, 0, base : base + 256, :], ring[slot, 1, base : base + 256, :]
+            )
+            keep(1, lane, lane + 256, value[:32])
+            keep(2, lane, lane + 256, value[32:])
+
+        @pl.when(freq + RING < NF)
+        def _():
+            fetch(freq + RING, slot).start()
+
+        return carry
+
+    lax.fori_loop(0, NF, solve, 0)
+
     for parity in range(4):
-        high, low = parts_of(lines[step, parity].reshape(32, 256))
-        both = mul_nt(jnp.concatenate([high, low], axis=0), dense_ref[0, parity, 0])
-        value = both[:32] + (both[32:] + mul_nt(high, dense_ref[0, parity, 1]))
-        value = value - weight * smooth[alias, parity]
-        spectra[parity, :, pl.ds(step * 8, 8), :] = value.reshape(4, 8, 400)
-
-    @pl.when(step == NF - 1)
-    def _():
-        def back(index, carry):
-            parity, patch = index // 4, index % 4
+        def back(patch, carry):
             high, low = parts_of(spectra[parity, patch])
             value = mul(backward_ref[0], high) + (
                 mul(backward_ref[1], high) + mul(backward_ref[0], low)
             )
-            wide_ref[parity, patch] = value[:136]
-            upper_ref[parity, patch] = value[136:144]
-            lower_ref[parity, patch] = value[144:152]
+            if parity != 1:
+                value = mul_exact(value, outward_ref[1 if parity == 2 else 0])
+            wide_ref[parity, patch] = value[:136, :400]
+            upper_ref[parity, patch] = value[136:144, :400]
+            lower_ref[parity, patch] = value[144:152, :400]
             return carry
 
-        lax.fori_loop(0, 16, back, 0)
+        lax.fori_loop(0, 4, back, 0)
+
+    for odd_x in range(2):
+        for patch in range(4):
+            index = odd_x * 4 + patch
+            even = wide_ref[odd_x, patch, :, 0:128]
+            odd = wide_ref[2 + odd_x, patch, :, 0:128]
+            bottom_ref[index] = even + odd
+            top_ref[index] = even - odd
 
 
 def with_neighbours(values, from_lower, from_upper):
@@ -389,61 +533,86 @@
     )
 
 
-def faces_kernel(wide_ref, from_lower_ref, from_upper_ref, bottom_ref, top_ref):
-    even = with_neighbours(wide_ref[0, 0], from_lower_ref[0, 0], from_upper_ref[0, 0])
-    odd = with_neighbours(wide_ref[1, 0], from_lower_ref[1, 0], from_upper_ref[1, 0])
-    bottom_ref[0] = even + odd
-    top_ref[0] = even - odd
-
-
-def unfold_kernel(
+def turned_into(ref, side, index, value):
+    ref[side, index, :, 0:128] = value[:128].T
+    ref[side, index, :, 128:136] = value[128:136].T
+
+
+def rows_of(ref, side, pair):
+    rows = slice(40 * pair, 40 * pair + 40)
+    return jnp.concatenate([ref[side, index, rows, :] for index in range(8)], axis=0)
+
+
+def unfolded(table, rows):
+    high, low = parts_of(rows)
+    return mul(table, high) + mul(table, low)
+
+
+def store_layers(value, places, near_ref, upper_ref, lower_ref):
+    for layer, z in enumerate(places):
+        near_ref[z] = value[160 * layer : 160 * layer + 136]
+        upper_ref[z] = value[160 * layer + 136 : 160 * layer + 144]
+        lower_ref[z] = value[160 * layer + 144 : 160 * layer + 152]
+
+
+def inner_kernel(
     wide_ref,
     from_lower_ref,
     from_upper_ref,
-    from_below_ref,
-    from_above_ref,
     unfold_ref,
     near_ref,
     upper_ref,
     lower_ref,
+    outer_ref,
     standing,
-    given,
 ):
     def turn(index, carry):
         even = with_neighbours(wide_ref[0, index], from_lower_ref[0, index], from_upper_ref[0, index])
         odd = with_neighbours(wide_ref[1, index], from_lower_ref[1, index], from_upper_ref[1, index])
-        for side, value in ((0, even + odd), (1, even - odd)):
-            standing[side, index, :, 0:128] = value[:128].T
-            standing[side, index, :, 128:136] = value[128:136].T
+        turned_into(standing, 0, index, even + odd)
+        turned_into(standing, 1, index, even - odd)
+        return carry
+
+    lax.fori_loop(0, 8, turn, 0)
+    outer_ref[...] = standing[:, :, 40:160, :]
+    for pair in range(4, 10):
+        for side in range(2):
+            value = unfolded(unfold_ref[0], rows_of(standing, side, pair))
+            places = [2 * pair - 8, 2 * pair - 7]
+            if side == 1:
+                places = [23 - z for z in places]
+            store_layers(value, places, near_ref, upper_ref, lower_ref)
+
+
+def outer_kernel(
+    outer_ref,
+    from_below_ref,
+    from_above_ref,
+    corner_lower_ref,
+    corner_upper_ref,
+    unfold_ref,
+    near_ref,
+    upper_ref,
+    lower_ref,
+    given,
+):
+    def turn(index, carry):
         for side, ref in ((0, from_below_ref), (1, from_above_ref)):
-            value = ref[index]
-            given[side, index, :, 0:128] = value[:128].T
-            given[side, index, :, 128:136] = value[128:136].T
+            value = with_neighbours(
+                ref[index], corner_lower_ref[side, index], corner_upper_ref[side, index]
+            )
+            turned_into(given, side, index, value)
         return carry
 
     lax.fori_loop(0, 8, turn, 0)
-
-    for pair in range(1, 10):
+    for pair in range(3):
         for side in range(2):
-            rows = jnp.concatenate(
-                [standing[side, index, 40 * pair : 40 * pair + 40, :] for index in range(8)], axis=0
-            )
-            high, low = parts_of(rows)
-            value = mul(unfold_ref[0], high) + mul(unfold_ref[0], low)
-            if pair <= 3:
-                other = 3 - pair
-                rows = jnp.concatenate(
-                    [given[side, index, 40 * other : 40 * other + 40, :] for index in range(8)],
-                    axis=0,
-                )
-                high, low = parts_of(rows)
-                value = value + (mul(unfold_ref[1], high) + mul(unfold_ref[1], low))
-            for layer in range(2):
-                z = 2 * pair + layer
-                z = z - 2 if side == 0 else 37 - z
-                near_ref[z] = value[160 * layer : 160 * layer + 136]
-                upper_ref[z] = value[160 * layer + 136 : 160 * layer + 144]
-                lower_ref[z] = value[160 * layer + 144 : 160 * layer + 152]
+            value = unfolded(unfold_ref[0], rows_of(outer_ref, side, pair))
+            value = value + unfolded(unfold_ref[1], rows_of(given, side, 2 - pair))
+            places = [2 * pair, 2 * pair + 1]
+            if side == 1:
+                places = [11 - z for z in places]
+            store_layers(value, places, near_ref, upper_ref, lower_ref)
 
 
 def far_kernel(
@@ -510,38 +679,46 @@
             out_ref[part * 4 + other] = value[other * 40 : other * 40 + 40] + mean * even_ref[apart]
 
 
+def planes_kernel(far_ref, spread_x_ref, spread_y_ref, out_ref):
+    sums = far_ref[0]
+    for source in range(1, far_ref.shape[0]):
+        sums = sums + far_ref[source]
+    high, low = parts_of(sums)
+    for layer in range(REACH):
+        left = spread_x_ref[layer * 136 : layer * 136 + 136, :]
+        value = mul_nt(left, high) + mul_nt(left, low)
+        first, second = parts_of(value)
+        out_ref[layer] = mul(first, spread_y_ref[...]) + mul(second, spread_y_ref[...])
+
+
 def final_kernel(
-    near_ref,
-    from_lower_ref,
-    from_upper_ref,
-    far_ref,
-    spread_x_ref,
-    spread_y_ref,
+    inner_ref,
+    inner_lower_ref,
+    inner_upper_ref,
+    outer_ref,
+    outer_lower_ref,
+    outer_upper_ref,
+    planes_ref,
     potential_ref,
     force_ref,
     whole,
-    planes,
     depth,
 ):
     step = pl.program_id(0)
 
     @pl.when(step == 0)
     def _():
-        sums = far_ref[0]
-        for source in range(1, far_ref.shape[0]):
-            sums = sums + far_ref[source]
-        high, low = parts_of(sums)
-        for layer in range(REACH):
-            left = spread_x_ref[layer * 136 : layer * 136 + 136, :]
-            first, second = parts_of(mul_nt(left, high) + mul_nt(left, low))
-            planes[layer] = mul(first, spread_y_ref[...]) + mul(second, spread_y_ref[...])
         for z in range(36):
             place = (z - 2 + 0.5) / RATIO - 0.5
             below = math.floor(place)
-            upper = place - below
-            value = with_neighbours(near_ref[z], from_lower_ref[z], from_upper_ref[z])
+            share = place - below
+            if 6 <= z < 30:
+                refs, spot = (inner_ref, inner_lower_ref, inner_upper_ref), z - 6
+            else:
+                refs, spot = (outer_ref, outer_lower_ref, outer_upper_ref), z % 24
+            value = with_neighbours(*(ref[spot] for ref in refs))
             whole[z] = value + (
-                (1.0 - upper) * planes[below + 1] + upper * planes[below + 2]
+                (1.0 - share) * planes_ref[below + 1] + share * planes_ref[below + 2]
             )
 
     row = lax.broadcasted_iota(jnp.int32, (128, 128), 0)
@@ -600,16 +777,7 @@
 
 
 def make_tables(size_z, size_x, size_y):
-    sum_x = np.zeros((32, RATIO, 128))
-    for x in range(128):
-        sum_x[x // RATIO, :, x] = 1.0
-    sum_y = np.zeros((4, 128, 128))
-    for layer in range(4):
-        for y in range(128):
-            sum_y[layer, y, layer * 32 + y // RATIO] = 1.0
     return dict(
-        sum_x=sum_x.reshape(32, 512).astype(ml_dtypes.bfloat16),
-        sum_y=sum_y.astype(ml_dtypes.bfloat16),
         weights=alias_weights().astype(np.float32),
         forward=forward_table(),
         mirror=mirror_table(),
@@ -617,39 +785,43 @@
         coarse=coarse_dense_table(),
         backward=backward_table(),
         dense=dense_table(),
+        swap=swap_tables(),
         unfold=unfold_table(),
         far=far_tables(size_z * CQ, size_x * 32, size_y * 32, size_x, size_y),
     )
 
 
-def masses_of(density, tables, copies):
+def masses_of(density, copies):
     return pl.pallas_call(
         masses_kernel,
         out_shape=shape(copies, 64, 128),
-        in_specs=[VMEM] * 3,
+        in_specs=[VMEM],
         out_specs=VMEM,
         compiler_params=params(16),
         cost_estimate=cost(2e7, 1.2e6),
         name="masses",
-    )(density, tables["sum_x"], tables["sum_y"])
+    )(density)
 
 
 def near_of(density, tables):
+    strip = shape(4, 4, 8, 400)
+    face = shape(8, 136, 128)
     return pl.pallas_call(
         near_kernel,
-        grid=(NF,),
-        out_shape=(shape(4, 4, 136, 400), shape(4, 4, 8, 400), shape(4, 4, 8, 400)),
-        in_specs=[SMEM] + [VMEM] * 6
-        + [pl.BlockSpec((1, 4, 2, 400, 256), lambda i: (i, 0, 0, 0, 0))],
-        out_specs=(VMEM, VMEM, VMEM),
+        out_shape=(shape(4, 4, 136, 400), strip, strip, face, face),
+        in_specs=[SMEM] + [VMEM] * 9 + [pl.BlockSpec(memory_space=pl.ANY)],
+        out_specs=(VMEM,) * 5,
         scratch_shapes=[
             pltpu.VMEM((NG, 4, 4, 8, 256), f32),
-            pltpu.VMEM((NC, 4, 32, 400), f32),
-            pltpu.VMEM((4, 4, 304, 400), f32),
+            pltpu.VMEM((NR, 3, 32, 384), f32),
+            pltpu.VMEM((NC, 4, 32, 512), f32),
+            pltpu.VMEM((4, 4, 304, 512), f32),
             pltpu.VMEM((PATCH, 64, 128), b16),
+            pltpu.VMEM((RING, 2, ROWS, 256), b16),
+            pltpu.SemaphoreType.DMA((RING,)),
         ],
-        compiler_params=params(56),
-        cost_estimate=cost(8e9, 7e7),
+        compiler_params=params(54),
+        cost_estimate=cost(8e9, 5e7),
         name="near",
     )(
         tables["weights"],
@@ -659,39 +831,52 @@
         tables["gather"],
         tables["coarse"],
         tables["backward"],
+        *tables["swap"],
         tables["dense"],
     )
 
 
-def faces_of(wide, from_lower, from_upper):
-    strip = pl.BlockSpec((2, 1, 8, 128), lambda i: (0, i, 0, 0))
-    face = pl.BlockSpec((1, 136, 128), lambda i: (i, 0, 0))
+def inner_of(wide, from_lower, from_upper, tables):
     return pl.pallas_call(
-        faces_kernel,
-        grid=(8,),
-        out_shape=(shape(8, 136, 128), shape(8, 136, 128)),
-        in_specs=[pl.BlockSpec((2, 1, 136, 128), lambda i: (0, i, 0, 0)), strip, strip],
-        out_specs=(face, face),
+        inner_kernel,
+        out_shape=(
+            shape(24, 136, 256),
+            shape(24, 8, 256),
+            shape(24, 8, 256),
+            shape(2, 8, 120, 256),
+        ),
+        in_specs=[VMEM] * 4,
+        out_specs=(VMEM,) * 4,
+        scratch_shapes=[pltpu.VMEM((2, 8, 400, 256), f32)],
+        compiler_params=params(28),
+        cost_estimate=cost(5e9, 1e7),
+        name="inner",
+    )(wide, from_lower, from_upper, tables["unfold"])
+
+
+def outer_of(outer, from_below, from_above, corner_lower, corner_upper, tables):
+    return pl.pallas_call(
+        outer_kernel,
+        out_shape=(shape(12, 136, 256), shape(12, 8, 256), shape(12, 8, 256)),
+        in_specs=[VMEM] * 6,
+        out_specs=(VMEM,) * 3,
+        scratch_shapes=[pltpu.VMEM((2, 8, 128, 256), f32)],
         compiler_params=params(16),
-        cost_estimate=cost(1e6, 2.5e6),
-        name="faces",
-    )(wide, from_lower, from_upper)
-
-
-def unfold_of(wide, from_lower, from_upper, from_below, from_above, tables):
+        cost_estimate=cost(4e9, 5e6),
+        name="outer",
+    )(outer, from_below, from_above, corner_lower, corner_upper, tables["unfold"])
+
+
+def planes_of(far, tables):
     return pl.pallas_call(
-        unfold_kernel,
-        out_shape=(shape(36, 136, 256), shape(36, 8, 256), shape(36, 8, 256)),
-        in_specs=[VMEM] * 6,
-        out_specs=(VMEM, VMEM, VMEM),
-        scratch_shapes=[
-            pltpu.VMEM((2, 8, 400, 256), f32),
-            pltpu.VMEM((2, 8, 128, 256), f32),
-        ],
-        compiler_params=params(56),
-        cost_estimate=cost(4e9, 1.2e7),
-        name="unfold",
-    )(wide, from_lower, from_upper, from_below, from_above, tables["unfold"])
+        planes_kernel,
+        out_shape=shape(REACH, 136, 256),
+        in_specs=[VMEM] * 3,
+        out_specs=VMEM,
+        compiler_params=params(12),
+        cost_estimate=cost(3e9, 2e6),
+        name="planes",
+    )(far, *tables["far"][6:])
 
 
 def far_of(where, masses, tables):
@@ -730,56 +915,60 @@
     )(where, masses, along_y, along_x, column, back_x, back_y, even)
 
 
-def final_of(near, from_lower, from_upper, far, tables):
+def final_of(inner, outer, planes):
     depth = 4
-    strip = pl.BlockSpec((36, 8, 256), lambda i: (0, 0, 0))
+    operands = (*inner, *outer, planes)
     return pl.pallas_call(
         functools.partial(final_kernel, depth=depth),
         grid=(PATCH // depth,),
         out_shape=(shape(PATCH, 128, 128), shape(3, PATCH, 128, 128, dtype=b16)),
-        in_specs=[
-            pl.BlockSpec((36, 136, 256), lambda i: (0, 0, 0)),
-            strip,
-            strip,
-            pl.BlockSpec(far.shape, lambda i: (0, 0, 0)),
-            pl.BlockSpec((REACH * 136, LANES), lambda i: (0, 0)),
-            pl.BlockSpec((40, 256), lambda i: (0, 0)),
-        ],
+        in_specs=[pl.BlockSpec(values.shape, lambda i: (0, 0, 0)) for values in operands],
         out_specs=(
             pl.BlockSpec((depth, 128, 128), lambda i: (i, 0, 0)),
             pl.BlockSpec((3, depth, 128, 128), lambda i: (0, i, 0, 0)),
         ),
-        scratch_shapes=[pltpu.VMEM((36, 136, 256), f32), pltpu.VMEM((REACH, 136, 256), f32)],
-        compiler_params=params(48),
+        scratch_shapes=[pltpu.VMEM((36, 136, 256), f32)],
+        compiler_params=params(32),
         cost_estimate=cost(2e8, 1.2e7),
         name="final",
-    )(near, from_lower, from_upper, far, *tables["far"][6:])
-
-
-def exchange(upper, lower, axis):
-    count = lax.axis_size(axis)
-    up = [(i, (i + 1) % count) for i in range(count)]
-    down = [(target, source) for source, target in up]
-    return lax.ppermute(upper, axis, up), lax.ppermute(lower, axis, down)
+    )(*operands)
+
+
+def moved(values, **steps):
+    axes = tuple(steps)
+    sizes = [lax.axis_size(axis) for axis in axes]
+    pairs = []
+    for source in np.ndindex(*sizes):
+        target = [(i + step) % size for i, step, size in zip(source, steps.values(), sizes)]
+        pairs.append(
+            (int(np.ravel_multi_index(source, sizes)), int(np.ravel_multi_index(target, sizes)))
+        )
+    return lax.ppermute(values, axes, pairs)
 
 
 def body(tables, density):
     size_gz = lax.axis_size("gz")
     where = jnp.stack([lax.axis_index(axis) for axis in ("gx", "gy", "gz")]).astype(jnp.int32)
-    masses = masses_of(density, tables, size_gz)
+    masses = masses_of(density, size_gz)
     masses = lax.all_to_all(masses, "gz", 0, 0, tiled=True)
-    wide, upper, lower = near_of(density, tables)
-    wide = wide.reshape(2, 8, 136, 400)
-    from_lower, from_upper = exchange(upper, lower, "gy")
-    from_lower = from_lower.reshape(2, 8, 8, 400)
-    from_upper = from_upper.reshape(2, 8, 8, 400)
+    wide, upper, lower, bottom, top = near_of(density, tables)
+    from_below = moved(top, gz=1)
+    from_above = moved(bottom, gz=-1)
+    from_lower = moved(upper, gy=1).reshape(2, 8, 8, 400)
+    from_upper = moved(lower, gy=-1).reshape(2, 8, 8, 400)
     far = far_of(where, masses, tables)
     far = lax.all_to_all(far, ("gx", "gy"), 0, 0, tiled=True)
-    bottom, top = faces_of(wide, from_lower, from_upper)
-    from_below, from_above = exchange(top, bottom, "gz")
-    near, upper, lower = unfold_of(wide, from_lower, from_upper, from_below, from_above, tables)
-    from_lower, from_upper = exchange(upper, lower, "gx")
-    return final_of(near, from_lower, from_upper, far, tables)
+    faces = jnp.stack([from_below, from_above])
+    corner_lower = moved(jnp.concatenate([faces[:, :, 128:132], faces[:, :, 124:128]], axis=2), gy=1)
+    corner_upper = moved(jnp.concatenate([faces[:, :, 0:4], faces[:, :, 132:136]], axis=2), gy=-1)
+    wide = wide.reshape(2, 8, 136, 400)
+    near, upper, lower, outer = inner_of(wide, from_lower, from_upper, tables)
+    inner = (near, moved(upper, gx=1), moved(lower, gx=-1))
+    near, upper, lower = outer_of(
+        outer, from_below, from_above, corner_lower, corner_upper, tables
+    )
+    outer = (near, moved(upper, gx=1), moved(lower, gx=-1))
+    return final_of(inner, outer, planes_of(far, tables))
 
 
 def solution(mesh):

time: 149 us -> 112 us (0.75)
  the two profiles are of different devices: /device:TPU:1 before, /device:TPU:39 now
where the time goes in v2:
time: 112 us; the launch traced here: 111 us
  Pallas kernels  66.8 us (60%)
  starting transfers between devices  28.6 us (26%)
  local copies, waits for them, and re-layouts  12.8 us (11%)
  waiting for transfers between devices  1.74 us (2%)
    pallas_call x1, Pallas kernels, near_of(): pl.pallas_call(near_kernel, out_shape=(shape(4, 4, 136, 400), strip, stri...  36.8 us
    ppermute x10, starting transfers between devices, moved(): return lax.ppermute(values, axes, pairs)  15.2 us
    unnamed x42, local copies, waits for them, and re-layouts  12.8 us
    pallas_call x1, Pallas kernels, final_of(): pl.pallas_call(functools.partial(final_kernel, depth=depth), grid=(PATCH...  7.54 us
    pallas_call x1, Pallas kernels, far_of(): pl.pallas_call(far_kernel, grid_spec=pltpu.PrefetchScalarGridSpec(num_sca...  6.87 us
    all_to_all x1, starting transfers between devices, body(): far = lax.all_to_all(far, ('gx', 'gy'), 0, 0, tiled=True)  6.71 us
    all_to_all x1, starting transfers between devices, body(): masses = lax.all_to_all(masses, 'gz', 0, 0, tiled=True)  6.63 us
    pallas_call x1, Pallas kernels, inner_of(): pl.pallas_call(inner_kernel, out_shape=(shape(24, 136, 256), shape(24, 8,...  5.62 us
  transfers between devices with their start and end apart: 12, of which 2 were waited for; matrix products, arithmetic and copies ran while one was open for 0% of the time, Pallas kernels for 52%

profile of v2, /device:TPU:39, one launch (start us, length us, event | category | flops | bytes accessed | tf_op | source)
XLA Modules:
  0.0 110.8 jit_solution(1804890661601218231)
XLA Ops:
  0.6 0.0 copy-start
  0.6 1.2 %copy-done = bf16[32,128,128]{2,1,0:T(8,128)(2,1)S(1)} copy-done((bf16[32,128,128]{2,1,0:T(8,128)(2,1)S(1)}, bf16[32,128,128]{2,1,0:T(8,128)(2,1)}, u32[]{:S(2)}) %copy-start) | copy-done | bytes 1048600
  1.9 1.5 %masses.1 = f32[8,64,128]{2,1,0:T(8,128)} custom-call(bf16[32,128,128]{2,1,0:T(8,128)(2,1)S(1)} %copy-done), custom_call_target="tpu_custom_call" | custom-call | flops 20000000 | bytes 1200000 | tf_op jit(solution)/shard_map/masses/pallas_call | solution.py:795
  3.3 6.6 %all-to-all-start = ((f32[8,64,128]{2,1,0:T(8,128)}), f32[8,64,128]{2,1,0:T(8,128)S(1)}, u32[]{:S(2)}, u32[]{:S(2)}) async-start(f32[8,64,128]{2,1,0:T(8,128)} %masses.1), calls=%async_computation | async-start | bytes 524288 | tf_op jit(solution)/shard_map/all_to_all | solution.py:953
  10.0 0.0 copy-start.19
  10.0 36.8 %near.1 = (f32[4,4,136,400]{3,2,1,0:T(8,128)}, f32[4,4,8,400]{3,2,1,0:T(8,128)}, f32[4,4,8,400]{3,2,1,0:T(8,128)}, f32[8,136,128]{2,1,0:T(8,128)}, f32[8,136,128]{2,1,0:T(8,128)}) custom-call(f32[37,2]{1,0:T(8,128)} %constant.50.clone.weights_ref, bf16[32,128,128]{2,1,0:T(8,128)(2,1)} %rho_ref.3, bf16[4,192,128]{2,1,0:T(8,128)(2,1)} %constant.51.clone.forward_ref, ...), custom_call_target="tpu_custom_call" | custom-call | flops 8000000000 | bytes 50000000 | tf_op jit(solution)/shard_map/near/pallas_call | solution.py:809
  46.8 2.8 %collective-permute-start.4 = (f32[8,136,128]{2,1,0:T(8,128)}, f32[8,136,128]{2,1,0:T(8,128)S(1)}, u32[]{:S(2)}, u32[]{:S(2)}) collective-permute-start(f32[8,136,128]{2,1,0:T(8,128)} %get-tuple-element.21), channel_id=1, source_target_pairs={{0,1},{1,2},{2,3},{3,4},{4,5},{5,6},{6,7},{7,0},{8,9},{9,10},{10,1... | collective-permute-start | bytes 1671176 | tf_op jit(solution)/shard_map/ppermute | solution.py:946
  49.6 0.0 collective-permute-start.5
  49.6 2.1 %collective-permute-start = (f32[4,4,8,400]{3,2,1,0:T(8,128)}, f32[4,4,8,400]{3,2,1,0:T(8,128)S(1)}, u32[]{:S(2)}, u32[]{:S(2)}) collective-permute-start(f32[4,4,8,400]{3,2,1,0:T(8,128)} %get-tuple-element.15), channel_id=1, source_target_pairs={{0,8},{8,16},{16,24},{24,0},{1,9},{9,17},{17,25},{25,1},{2,10},{10... | collective-permute-start | bytes 614408 | tf_op jit(solution)/shard_map/ppermute | solution.py:946
  51.7 0.0 collective-permute-start.1
  51.7 0.1 pad_add_fusion.where_ref
  51.8 0.0 all-to-all-done.masses_ref
  51.8 0.0 copy-done.13
  51.8 0.0 copy-start.12
  51.8 1.6 %copy-done.12 = f32[33,128,128]{2,1,0:T(8,128)S(1)} copy-done((f32[33,128,128]{2,1,0:T(8,128)S(1)}, f32[33,128,128]{2,1,0:T(8,128)}, u32[]{:S(2)}) %copy-start.12) | copy-done | bytes 2162712
  53.4 1.2 %copy-done.15 = f32[16,40,384]{2,1,0:T(8,128)S(1)} copy-done((f32[16,40,384]{2,1,0:T(8,128)S(1)}, f32[16,40,384]{2,1,0:T(8,128)}, u32[]{:S(2)}) %copy-start.15) | copy-done | bytes 983064
  54.6 6.9 %far.1 = f32[16,40,384]{2,1,0:T(8,128)} custom-call(s32[3]{0:T(128)S(1)} %pad_add_fusion.where_ref, f32[8,64,128]{2,1,0:T(8,128)S(1)} %all-to-all-done.masses_ref, bf16[4,2,128,512]{3,2,1,0:T(8,128)(2,1)S(1)} %copy-done.13, bf16[4,128,96]{2,1,0:T(8,128)(2,1)S(1)} %copy-done.17, f32[33,128,128]{2,1,0:T(8,128)S(1)} %copy-done.12, ...), custom_call_target="tpu_custom_call" | custom-call | flops 4000000000 | bytes 9000000 | tf_op jit(solution)/shard_map/far/pallas_call | solution.py:890
  61.5 6.7 %all-to-all-start.1 = ((f32[16,40,384]{2,1,0:T(8,128)}), f32[16,40,384]{2,1,0:T(8,128)}, u32[]{:S(2)}, u32[]{:S(2)}) async-start(f32[16,40,384]{2,1,0:T(8,128)} %far.1), calls=%async_computation.1 | async-start | bytes 1966080 | tf_op jit(solution)/shard_map/all_to_all | solution.py:960
  68.2 0.0 collective-permute-done.4.from_below_ref
  68.2 0.0 collective-permute-done.5.from_above_ref
  68.3 0.0 copy-start.3
  68.3 1.0 collective-permute-start.6
  69.3 0.0 collective-permute-start.7
  69.3 0.6 collective-permute-done
  69.9 0.7 copy-done.8
  70.6 1.1 collective-permute-done.1
  71.7 0.7 copy-done.10
  72.4 2.3 %copy-done.7 = f32[4,4,136,400]{3,2,1,0:T(8,128)S(1)} copy-done((f32[4,4,136,400]{3,2,1,0:T(8,128)S(1)}, f32[4,4,136,400]{3,2,1,0:T(8,128)}, u32[]{:S(2)}) %copy-start.7) | copy-done | bytes 3481624
  74.7 0.9 copy-done.9
  75.7 0.9 copy-done.11
  76.6 5.6 %inner.1 = (f32[24,136,256]{2,1,0:T(8,128)S(1)}, f32[24,8,256]{2,1,0:T(8,128)}, f32[24,8,256]{2,1,0:T(8,128)}, f32[2,8,120,256]{3,2,1,0:T(8,128)S(1)}) custom-call(f32[2,8,136,400]{3,2,1,0:T(8,128)S(1)} %bitcast.12, f32[2,8,8,400]{3,2,1,0:T(8,128)S(1)} %bitcast.13, f32[2,8,8,400]{3,2,1,0:T(8,128)S(1)} %bitcast.14, bf16[2,320,320]{2,1,0:T(8,128)(2,1)S(1)} %copy-done.16), custom_call_target="tpu_custom_call" | custom-call | flops 5000000000 | bytes 10000000 | tf_op jit(solution)/shard_map/inner/pallas_call | solution.py:840
  82.2 3.7 %collective-permute-start.2 = (f32[24,8,256]{2,1,0:T(8,128)}, f32[24,8,256]{2,1,0:T(8,128)S(1)}, u32[]{:S(2)}, u32[]{:S(2)}) collective-permute-start(f32[24,8,256]{2,1,0:T(8,128)} %get-tuple-element.18), channel_id=1, source_target_pairs={{0,32},{32,64},{64,96},{96,0},{1,33},{33,65},{65,97},{97,1},{2,34}... | collective-permute-start | bytes 589832 | tf_op jit(solution)/shard_map/ppermute | solution.py:946
  85.9 3.0 %collective-permute-start.3 = (f32[24,8,256]{2,1,0:T(8,128)}, f32[24,8,256]{2,1,0:T(8,128)}, u32[]{:S(2)}, u32[]{:S(2)}) collective-permute-start(f32[24,8,256]{2,1,0:T(8,128)} %get-tuple-element.19), channel_id=1, source_target_pairs={{0,96},{32,0},{64,32},{96,64},{1,97},{33,1},{65,33},{97,65},{2,98}... | collective-permute-start | bytes 589832 | tf_op jit(solution)/shard_map/ppermute | solution.py:946
  88.9 0.0 collective-permute-done.6.corner_lower_ref
  88.9 0.0 collective-permute-done.7.corner_upper_ref
  88.9 4.0 %outer.1 = (f32[12,136,256]{2,1,0:T(8,128)S(1)}, f32[12,8,256]{2,1,0:T(8,128)}, f32[12,8,256]{2,1,0:T(8,128)}) custom-call(f32[2,8,120,256]{3,2,1,0:T(8,128)S(1)} %get-tuple-element.20.outer_ref, f32[8,136,128]{2,1,0:T(8,128)S(1)} %copy-done.2, f32[8,136,128]{2,1,0:T(8,128)S(1)} %copy-done.4, f32[2,8,8,128]{3,2,1,0:T(8,128)S(1)} %collective-permute-done.6.corner_lower_ref, ...), custom_call_target="tpu_custom_call" | custom-call | flops 4000000000 | bytes 5000000 | tf_op jit(solution)/shard_map/outer/pallas_call | solution.py:858
  92.9 1.2 %copy-done.5 = f32[12,136,256]{2,1,0:T(8,128)} copy-done((f32[12,136,256]{2,1,0:T(8,128)}, f32[12,136,256]{2,1,0:T(8,128)S(1)}, u32[]{:S(2)}) %copy-start.5) | copy-done | bytes 1671192
  94.1 0.0 collective-permute-start.8
  94.1 2.7 %collective-permute-start.9 = (f32[12,8,256]{2,1,0:T(8,128)}, f32[12,8,256]{2,1,0:T(8,128)}, u32[]{:S(2)}, u32[]{:S(2)}) collective-permute-start(f32[12,8,256]{2,1,0:T(8,128)} %get-tuple-element.25), channel_id=1, source_target_pairs={{0,96},{32,0},{64,32},{96,64},{1,97},{33,1},{65,33},{97,65},{2,98}... | collective-permute-start | bytes 294920 | tf_op jit(solution)/shard_map/ppermute | solution.py:946
  96.8 0.0 all-to-all-done.1.far_ref
  96.8 1.2 %copy-done.14 = bf16[1360,384]{1,0:T(8,128)(2,1)S(1)} copy-done((bf16[1360,384]{1,0:T(8,128)(2,1)S(1)}, bf16[1360,384]{1,0:T(8,128)(2,1)}, u32[]{:S(2)}) %copy-start.14) | copy-done | bytes 1044504
  98.0 0.7 copy-done.20
  98.7 4.5 %planes.1.planes_ref = f32[10,136,256]{2,1,0:T(8,128)S(1)} custom-call(f32[16,40,384]{2,1,0:T(8,128)} %all-to-all-done.1.far_ref, bf16[1360,384]{1,0:T(8,128)(2,1)S(1)} %copy-done.14, bf16[40,256]{1,0:T(8,128)(2,1)S(1)} %copy-done.20), custom_call_target="tpu_custom_call" | custom-call | flops 3000000000 | bytes 2000000 | tf_op jit(solution)/shard_map/planes/pallas_call | solution.py:871
  103.2 0.0 collective-permute-done.2.inner_lower_ref
  103.2 0.0 collective-permute-done.3.inner_upper_ref
  103.2 0.0 collective-permute-done.8.outer_lower_ref
  103.2 0.0 collective-permute-done.9.outer_upper_ref
  103.3 7.5 %final.1 = (f32[32,128,128]{2,1,0:T(8,128)}, bf16[3,32,128,128]{3,2,1,0:T(8,128)(2,1)}) custom-call(f32[24,136,256]{2,1,0:T(8,128)S(1)} %get-tuple-element.17.inner_ref, f32[24,8,256]{2,1,0:T(8,128)S(1)} %collective-permute-done.2.inner_lower_ref, f32[24,8,256]{2,1,0:T(8,128)} %collective-permute-done.3.inner_upper_ref, f32[12,136,256]{2,1,0:T(8,128)S(1)} %copy-done.6, ...), custom_call_target="tpu_custom_call" | custom-call | flops 200000000 | bytes 12000000 | tf_op jit(solution)/shard_map/final/pallas_call | solution.py:921
  (28 shorter events, 0.1 us)
Async XLA Ops:
  0.6 1.2 %copy-start = (bf16[32,128,128]{2,1,0:T(8,128)(2,1)S(1)}, bf16[32,128,128]{2,1,0:T(8,128)(2,1)}, u32[]{:S(2)}) copy-start(bf16[32,128,128]{2,1,0:T(8,128)(2,1)} %rho_ref.3) | copy-start | bytes 3145732
  3.3 48.5 %all-to-all-start = ((f32[8,64,128]{2,1,0:T(8,128)}), f32[8,64,128]{2,1,0:T(8,128)S(1)}, u32[]{:S(2)}, u32[]{:S(2)}) async-start(f32[8,64,128]{2,1,0:T(8,128)} %masses.1), calls=%async_computation | async-start | bytes 524288 | tf_op jit(solution)/shard_map/all_to_all | solution.py:953
  9.9 41.9 %copy-start.13 = (bf16[4,2,128,512]{3,2,1,0:T(8,128)(2,1)S(1)}, bf16[4,2,128,512]{3,2,1,0:T(8,128)(2,1)}, u32[]{:S(2)}) copy-start(bf16[4,2,128,512]{3,2,1,0:T(8,128)(2,1)} %constant.60.clone.along_y_ref) | copy-start | bytes 3145732
  9.9 41.9 %copy-start.17 = (bf16[4,128,96]{2,1,0:T(8,128)(2,1)S(1)}, bf16[4,128,96]{2,1,0:T(8,128)(2,1)}, u32[]{:S(2)}) copy-start(bf16[4,128,96]{2,1,0:T(8,128)(2,1)} %constant.61.clone.along_x_ref) | copy-start | bytes 294916
  9.9 41.9 %copy-start.18 = (bf16[160,256]{1,0:T(8,128)(2,1)S(1)}, bf16[160,256]{1,0:T(8,128)(2,1)}, u32[]{:S(2)}) copy-start(bf16[160,256]{1,0:T(8,128)(2,1)} %constant.63.clone.back_x_ref) | copy-start | bytes 245764
  10.0 41.9 %copy-start.19 = (bf16[2,160,128]{2,1,0:T(8,128)(2,1)S(1)}, bf16[2,160,128]{2,1,0:T(8,128)(2,1)}, u32[]{:S(2)}) copy-start(bf16[2,160,128]{2,1,0:T(8,128)(2,1)} %constant.64.clone.back_y_ref) | copy-start | bytes 245764
  46.8 21.4 %collective-permute-start.4 = (f32[8,136,128]{2,1,0:T(8,128)}, f32[8,136,128]{2,1,0:T(8,128)S(1)}, u32[]{:S(2)}, u32[]{:S(2)}) collective-permute-start(f32[8,136,128]{2,1,0:T(8,128)} %get-tuple-element.21), channel_id=1, source_target_pairs={{0,1},{1,2},{2,3},{3,4},{4,5},{5,6},{6,7},{7,0},{8,9},{9,10},{10,1... | collective-permute-start | bytes 1671176 | tf_op jit(solution)/shard_map/ppermute | solution.py:946
  49.6 18.7 %collective-permute-start.5 = (f32[8,136,128]{2,1,0:T(8,128)}, f32[8,136,128]{2,1,0:T(8,128)S(1)}, u32[]{:S(2)}, u32[]{:S(2)}) collective-permute-start(f32[8,136,128]{2,1,0:T(8,128)} %get-tuple-element.22), channel_id=1, source_target_pairs={{0,7},{1,0},{2,1},{3,2},{4,3},{5,4},{6,5},{7,6},{8,15},{9,8},{10,9... | collective-permute-start | bytes 1671176 | tf_op jit(solution)/shard_map/ppermute | solution.py:946
  49.6 20.3 %collective-permute-start = (f32[4,4,8,400]{3,2,1,0:T(8,128)}, f32[4,4,8,400]{3,2,1,0:T(8,128)S(1)}, u32[]{:S(2)}, u32[]{:S(2)}) collective-permute-start(f32[4,4,8,400]{3,2,1,0:T(8,128)} %get-tuple-element.15), channel_id=1, source_target_pairs={{0,8},{8,16},{16,24},{24,0},{1,9},{9,17},{17,25},{25,1},{2,10},{10... | collective-permute-start | bytes 614408 | tf_op jit(solution)/shard_map/ppermute | solution.py:946
  51.7 20.0 %collective-permute-start.1 = (f32[4,4,8,400]{3,2,1,0:T(8,128)}, f32[4,4,8,400]{3,2,1,0:T(8,128)S(1)}, u32[]{:S(2)}, u32[]{:S(2)}) collective-permute-start(f32[4,4,8,400]{3,2,1,0:T(8,128)} %get-tuple-element.16), channel_id=1, source_target_pairs={{0,24},{8,0},{16,8},{24,16},{1,25},{9,1},{17,9},{25,17},{2,26},{10... | collective-permute-start | bytes 614408 | tf_op jit(solution)/shard_map/ppermute | solution.py:946
  51.8 1.6 %copy-start.12 = (f32[33,128,128]{2,1,0:T(8,128)S(1)}, f32[33,128,128]{2,1,0:T(8,128)}, u32[]{:S(2)}) copy-start(f32[33,128,128]{2,1,0:T(8,128)} %constant.62.clone.column_ref) | copy-start | bytes 6488068
  53.4 1.2 %copy-start.15 = (f32[16,40,384]{2,1,0:T(8,128)S(1)}, f32[16,40,384]{2,1,0:T(8,128)}, u32[]{:S(2)}) copy-start(f32[16,40,384]{2,1,0:T(8,128)} %constant.65.clone.even_ref) | copy-start | bytes 2949124
  61.5 35.3 %all-to-all-start.1 = ((f32[16,40,384]{2,1,0:T(8,128)}), f32[16,40,384]{2,1,0:T(8,128)}, u32[]{:S(2)}, u32[]{:S(2)}) async-start(f32[16,40,384]{2,1,0:T(8,128)} %far.1), calls=%async_computation.1 | async-start | bytes 1966080 | tf_op jit(solution)/shard_map/all_to_all | solution.py:960
  68.2 4.2 %copy-start.16 = (bf16[2,320,320]{2,1,0:T(8,128)(2,1)S(1)}, bf16[2,320,320]{2,1,0:T(8,128)(2,1)}, u32[]{:S(2)}) copy-start(bf16[2,320,320]{2,1,0:T(8,128)(2,1)} %constant.66.clone.unfold_ref) | copy-start | bytes 1228804
  68.2 4.2 %copy-start.1 = (f32[8,136,128]{2,1,0:T(8,128)}, f32[8,136,128]{2,1,0:T(8,128)S(1)}, u32[]{:S(2)}) copy-start(f32[8,136,128]{2,1,0:T(8,128)S(1)} %collective-permute-done.4.from_below_ref) | copy-start | bytes 1671172
  68.3 4.2 %copy-start.3 = (f32[8,136,128]{2,1,0:T(8,128)}, f32[8,136,128]{2,1,0:T(8,128)S(1)}, u32[]{:S(2)}) copy-start(f32[8,136,128]{2,1,0:T(8,128)S(1)} %collective-permute-done.5.from_above_ref) | copy-start | bytes 1671172
  68.3 20.6 %collective-permute-start.6 = (f32[2,8,8,128]{3,2,1,0:T(8,128)S(1)}, f32[2,8,8,128]{3,2,1,0:T(8,128)S(1)}, u32[]{:S(2)}, u32[]{:S(2)}) collective-permute-start(f32[2,8,8,128]{3,2,1,0:T(8,128)S(1)} %fusion.1), channel_id=1, source_target_pairs={{0,8},{8,16},{16,24},{24,0},{1,9},{9,17},{17,25},{25,1},{2,10},{10... | collective-permute-start | bytes 196616 | tf_op jit(solution)/shard_map/ppermute | solution.py:946
  69.3 19.6 %collective-permute-start.7 = (f32[2,8,8,128]{3,2,1,0:T(8,128)S(1)}, f32[2,8,8,128]{3,2,1,0:T(8,128)S(1)}, u32[]{:S(2)}, u32[]{:S(2)}) collective-permute-start(f32[2,8,8,128]{3,2,1,0:T(8,128)S(1)} %get-tuple-element.26), channel_id=1, source_target_pairs={{0,24},{8,0},{16,8},{24,16},{1,25},{9,1},{17,9},{25,17},{2,26},{10... | collective-permute-start | bytes 196616 | tf_op jit(solution)/shard_map/ppermute | solution.py:946
  69.9 0.7 copy-start.8
  71.7 0.7 copy-start.10
  72.4 2.3 %copy-start.7 = (f32[4,4,136,400]{3,2,1,0:T(8,128)S(1)}, f32[4,4,136,400]{3,2,1,0:T(8,128)}, u32[]{:S(2)}) copy-start(f32[4,4,136,400]{3,2,1,0:T(8,128)} %get-tuple-element.14) | copy-start | bytes 10444804
  74.7 0.9 copy-start.9
  75.6 0.9 copy-start.11
  76.6 12.3 %copy-start.2 = (f32[8,136,128]{2,1,0:T(8,128)S(1)}, f32[8,136,128]{2,1,0:T(8,128)}, u32[]{:S(2)}) copy-start(f32[8,136,128]{2,1,0:T(8,128)} %copy-done.1) | copy-start | bytes 1671172
  76.6 12.3 %copy-start.4 = (f32[8,136,128]{2,1,0:T(8,128)S(1)}, f32[8,136,128]{2,1,0:T(8,128)}, u32[]{:S(2)}) copy-start(f32[8,136,128]{2,1,0:T(8,128)} %copy-done.3) | copy-start | bytes 1671172
  82.2 21.0 %collective-permute-start.2 = (f32[24,8,256]{2,1,0:T(8,128)}, f32[24,8,256]{2,1,0:T(8,128)S(1)}, u32[]{:S(2)}, u32[]{:S(2)}) collective-permute-start(f32[24,8,256]{2,1,0:T(8,128)} %get-tuple-element.18), channel_id=1, source_target_pairs={{0,32},{32,64},{64,96},{96,0},{1,33},{33,65},{65,97},{97,1},{2,34}... | collective-permute-start | bytes 589832 | tf_op jit(solution)/shard_map/ppermute | solution.py:946
  85.9 17.3 %collective-permute-start.3 = (f32[24,8,256]{2,1,0:T(8,128)}, f32[24,8,256]{2,1,0:T(8,128)}, u32[]{:S(2)}, u32[]{:S(2)}) collective-permute-start(f32[24,8,256]{2,1,0:T(8,128)} %get-tuple-element.19), channel_id=1, source_target_pairs={{0,96},{32,0},{64,32},{96,64},{1,97},{33,1},{65,33},{97,65},{2,98}... | collective-permute-start | bytes 589832 | tf_op jit(solution)/shard_map/ppermute | solution.py:946
  92.9 1.2 %copy-start.5 = (f32[12,136,256]{2,1,0:T(8,128)}, f32[12,136,256]{2,1,0:T(8,128)S(1)}, u32[]{:S(2)}) copy-start(f32[12,136,256]{2,1,0:T(8,128)S(1)} %get-tuple-element.23.outer_ref) | copy-start | bytes 5013508
  94.1 9.1 %collective-permute-start.8 = (f32[12,8,256]{2,1,0:T(8,128)}, f32[12,8,256]{2,1,0:T(8,128)}, u32[]{:S(2)}, u32[]{:S(2)}) collective-permute-start(f32[12,8,256]{2,1,0:T(8,128)} %get-tuple-element.24), channel_id=1, source_target_pairs={{0,32},{32,64},{64,96},{96,0},{1,33},{33,65},{65,97},{97,1},{2,34}... | collective-permute-start | bytes 294920 | tf_op jit(solution)/shard_map/ppermute | solution.py:946
  94.1 9.1 %collective-permute-start.9 = (f32[12,8,256]{2,1,0:T(8,128)}, f32[12,8,256]{2,1,0:T(8,128)}, u32[]{:S(2)}, u32[]{:S(2)}) collective-permute-start(f32[12,8,256]{2,1,0:T(8,128)} %get-tuple-element.25), channel_id=1, source_target_pairs={{0,96},{32,0},{64,32},{96,64},{1,97},{33,1},{65,33},{97,65},{2,98}... | collective-permute-start | bytes 294920 | tf_op jit(solution)/shard_map/ppermute | solution.py:946
  96.8 1.2 %copy-start.14 = (bf16[1360,384]{1,0:T(8,128)(2,1)S(1)}, bf16[1360,384]{1,0:T(8,128)(2,1)}, u32[]{:S(2)}) copy-start(bf16[1360,384]{1,0:T(8,128)(2,1)} %constant.67.clone.spread_x_ref) | copy-start | bytes 3133444
  98.0 0.7 copy-start.20
  98.7 4.5 %copy-start.6 = (f32[12,136,256]{2,1,0:T(8,128)S(1)}, f32[12,136,256]{2,1,0:T(8,128)}, u32[]{:S(2)}) copy-start(f32[12,136,256]{2,1,0:T(8,128)} %copy-done.5) | copy-start | bytes 5013508

commit v3 on v2

--- a/solution.py
+++ b/solution.py
@@ -225,7 +225,8 @@
         inside = (cells >= -RATIO) & (cells < PATCH + RATIO)
         values = fine_basis(cells) * inside
         table[:152, :NF, :, patch] = values.transpose(2, 0, 1)
-    return np.stack(halves(table.reshape(160, 304)))
+    high, low = halves(table.reshape(160, 304))
+    return np.concatenate([high, high, low], axis=1)
 
 
 def unfold_table():
@@ -310,15 +311,7 @@
 
     back_x = np.concatenate(halves(windows(total_x, parts_x, basis_x)), axis=1)
     back_y = np.stack(halves(windows(total_y, parts_y, basis_y)))
-    spread = refine_table(PLACES[:136], np.arange(SIDE) - 1)
-    spread_x = np.zeros((REACH, 136, LANES))
-    for layer in range(REACH):
-        spread_x[layer, :, layer * SIDE : layer * SIDE + SIDE] = spread
-    spread_y = np.zeros((40, 256))
-    spread_y[:SIDE, :136] = spread.T
-    spread_x = spread_x.reshape(REACH * 136, LANES).astype(ml_dtypes.bfloat16)
-    spread_y = spread_y.astype(ml_dtypes.bfloat16)
-    return along_y, along_x, column, back_x, back_y, even, spread_x, spread_y
+    return along_y, along_x, column, back_x, back_y, even
 
 
 def parts_of(values):
@@ -414,7 +407,7 @@
 
         right = [rows(0, 0), rows(0, 1), rows(1, 0), rows(1, 1)]
 
-        def chunk(index, carry):
+        def chunk(index):
             left = forward_ref[index]
             sums = []
             for mirror in range(4):
@@ -422,14 +415,14 @@
                 sums.append(both[:96] + both[96:])
             even, odd = sums[0] + sums[1], sums[0] - sums[1]
             even_far, odd_far = sums[2] + sums[3], sums[2] - sums[3]
-            freqs = pl.ds(index * 12, 12)
+            freqs = slice(index * 12, index * 12 + 12)
             lines[freqs, 0, patch] = (even + even_far).reshape(12, 8, 256)
             lines[freqs, 1, patch] = (odd + odd_far).reshape(12, 8, 256)
             lines[freqs, 2, patch] = (even - even_far).reshape(12, 8, 256)
             lines[freqs, 3, patch] = (odd - odd_far).reshape(12, 8, 256)
-            return carry
-
-        lax.fori_loop(0, 4, chunk, 0)
+
+        for index in range(4):
+            chunk(index)
 
     for parity in range(4):
         values = lines[NF : NF + NC, parity].reshape(NC * 32, 256)
@@ -443,20 +436,24 @@
                 value[32:] + mul(both[:32], coarse_ref[freq, parity, 1])
             )
 
-    def prepare(index, carry):
+    def prepare(index):
         freqs = pl.ds(index * 4, 4)
         for slot, parity in ((0, 0), (1, 3)):
             values = lines[freqs, parity].reshape(128, 256)
             ready[freqs, slot] = mul_exact(values, inward_ref[...]).reshape(4, 32, 384)
         values = lines[freqs, 2].reshape(128, 256)
         ready[freqs, 2, :, 0:256] = mul_exact(values, turn_ref[...]).reshape(4, 32, 256)
+
+    def prepare_two(index, carry):
+        prepare(2 * index)
+        prepare(2 * index + 1)
         return carry
 
-    lax.fori_loop(0, NR // 4, prepare, 0)
+    lax.fori_loop(0, NR // 8, prepare_two, 0)
     spectra[:, :, 8 * NF :, :] = jnp.zeros((4, 4, 8, 512), f32)
     row = lax.broadcasted_iota(jnp.int32, (32, 1), 0)
 
-    def solve(freq, carry):
+    def solve(freq):
         slot = lax.rem(freq, RING)
         fetch(freq, slot).wait()
         rest = lax.rem(freq, CH)
@@ -491,24 +488,31 @@
         def _():
             fetch(freq + RING, slot).start()
 
+    def solve_two(index, carry):
+        solve(2 * index)
+        solve(2 * index + 1)
         return carry
 
-    lax.fori_loop(0, NF, solve, 0)
+    lax.fori_loop(0, NF // 2, solve_two, 0)
+    solve(jnp.int32(NF - 1))
 
     for parity in range(4):
-        def back(patch, carry):
+        values = []
+        for patch in range(4):
             high, low = parts_of(spectra[parity, patch])
-            value = mul(backward_ref[0], high) + (
-                mul(backward_ref[1], high) + mul(backward_ref[0], low)
-            )
-            if parity != 1:
-                value = mul_exact(value, outward_ref[1 if parity == 2 else 0])
-            wide_ref[parity, patch] = value[:136, :400]
-            upper_ref[parity, patch] = value[136:144, :400]
-            lower_ref[parity, patch] = value[144:152, :400]
-            return carry
-
-        lax.fori_loop(0, 4, back, 0)
+            values.append(mul(backward_ref[...], jnp.concatenate([high, low, high], axis=0)))
+        if parity != 1:
+            pairs = [part for value in values for part in parts_of(value)]
+            table = outward_ref[1 if parity == 2 else 0]
+            both = mul(jnp.concatenate(pairs, axis=0), table)
+            values = [
+                both[320 * patch : 320 * patch + 160] + both[320 * patch + 160 : 320 * patch + 320]
+                for patch in range(4)
+            ]
+        for patch in range(4):
+            wide_ref[parity, patch] = values[patch][:136, :400]
+            upper_ref[parity, patch] = values[patch][136:144, :400]
+            lower_ref[parity, patch] = values[patch][144:152, :400]
 
     for odd_x in range(2):
         for patch in range(4):
@@ -556,17 +560,38 @@
 
 
 def inner_kernel(
+    wide_hbm,
+    from_lower_hbm,
+    from_upper_hbm,
+    unfold_ref,
+    near_hbm,
+    upper_ref,
+    lower_ref,
+    outer_hbm,
+    standing,
     wide_ref,
     from_lower_ref,
     from_upper_ref,
-    unfold_ref,
     near_ref,
-    upper_ref,
-    lower_ref,
-    outer_ref,
-    standing,
+    arrived,
+    written,
 ):
+    def fetch(index):
+        return pltpu.make_async_copy(wide_hbm.at[:, index], wide_ref.at[:, index], arrived.at[index])
+
+    strips = [
+        pltpu.make_async_copy(from_lower_hbm, from_lower_ref, arrived.at[8]),
+        pltpu.make_async_copy(from_upper_hbm, from_upper_ref, arrived.at[9]),
+    ]
+    for strip in strips:
+        strip.start()
+    for index in range(8):
+        fetch(index).start()
+    for strip in strips:
+        strip.wait()
+
     def turn(index, carry):
+        fetch(index).wait()
         even = with_neighbours(wide_ref[0, index], from_lower_ref[0, index], from_upper_ref[0, index])
         odd = with_neighbours(wide_ref[1, index], from_lower_ref[1, index], from_upper_ref[1, index])
         turned_into(standing, 0, index, even + odd)
@@ -574,7 +599,8 @@
         return carry
 
     lax.fori_loop(0, 8, turn, 0)
-    outer_ref[...] = standing[:, :, 40:160, :]
+    results = [pltpu.make_async_copy(standing.at[:, :, 40:160, :], outer_hbm, written.at[0])]
+    results[0].start()
     for pair in range(4, 10):
         for side in range(2):
             value = unfolded(unfold_ref[0], rows_of(standing, side, pair))
@@ -582,6 +608,15 @@
             if side == 1:
                 places = [23 - z for z in places]
             store_layers(value, places, near_ref, upper_ref, lower_ref)
+            pieces = pl.ds(min(places), 2)
+            results.append(
+                pltpu.make_async_copy(
+                    near_ref.at[pieces], near_hbm.at[pieces], written.at[len(results)]
+                )
+            )
+            results[-1].start()
+    for result in results:
+        result.wait()
 
 
 def outer_kernel(
@@ -620,15 +655,24 @@
     masses_ref,
     along_y_ref,
     along_x_ref,
-    column_ref,
+    column_hbm,
     back_x_ref,
     back_y_ref,
-    even_ref,
+    even_hbm,
     out_ref,
     spectra,
     lines,
     turned,
+    column_ref,
+    even_ref,
+    arrived,
 ):
+    tables = [
+        pltpu.make_async_copy(column_hbm, column_ref, arrived.at[0]),
+        pltpu.make_async_copy(even_hbm, even_ref, arrived.at[1]),
+    ]
+    for table in tables:
+        table.start()
     blocks = masses_ref.shape[0]
     total = spectra.shape[0]
     masses = masses_ref[...].reshape(blocks * 64, 128)
@@ -646,6 +690,8 @@
             spectra[half * 4 + layer] = value[:, layer * 128 : layer * 128 + 128]
 
     start = where_ref[2] * CQ
+    for table in tables:
+        table.wait()
 
     def solve(tile, carry):
         rows = pl.ds(pl.multiple_of(tile * 8, 8), 8)
@@ -679,16 +725,31 @@
             out_ref[part * 4 + other] = value[other * 40 : other * 40 + 40] + mean * even_ref[apart]
 
 
-def planes_kernel(far_ref, spread_x_ref, spread_y_ref, out_ref):
+def share(fine, coarse):
+    fine = jnp.where(fine < 132, fine, fine - 136).astype(f32)
+    return jnp.maximum(0.0, 1.0 - jnp.abs((fine + 0.5) / RATIO - 0.5 - coarse.astype(f32)))
+
+
+def planes_kernel(far_ref, out_ref):
     sums = far_ref[0]
     for source in range(1, far_ref.shape[0]):
         sums = sums + far_ref[source]
-    high, low = parts_of(sums)
+    right = jnp.concatenate(parts_of(sums), axis=0)
+    row = lax.broadcasted_iota(jnp.int32, (136, LANES), 0)
+    lane = lax.broadcasted_iota(jnp.int32, (136, LANES), 1)
+    spread_x = []
     for layer in range(REACH):
-        left = spread_x_ref[layer * 136 : layer * 136 + 136, :]
-        value = mul_nt(left, high) + mul_nt(left, low)
-        first, second = parts_of(value)
-        out_ref[layer] = mul(first, spread_y_ref[...]) + mul(second, spread_y_ref[...])
+        coarse = lane - layer * SIDE
+        inside = (coarse >= 0) & (coarse < SIDE)
+        spread_x.append(jnp.where(inside, share(row, coarse - 1), 0.0).astype(b16))
+    value = mul_nt(jnp.concatenate(spread_x, axis=0), right)
+    first, second = parts_of(value[:, :40] + value[:, 40:])
+    row = lax.broadcasted_iota(jnp.int32, (40, 256), 0)
+    lane = lax.broadcasted_iota(jnp.int32, (40, 256), 1)
+    spread_y = jnp.where(row < SIDE, share(lane, row - 1), 0.0).astype(b16)
+    value = mul(first, spread_y) + mul(second, spread_y)
+    for layer in range(REACH):
+        out_ref[layer] = value[layer * 136 : layer * 136 + 136]
 
 
 def final_kernel(
@@ -711,14 +772,14 @@
         for z in range(36):
             place = (z - 2 + 0.5) / RATIO - 0.5
             below = math.floor(place)
-            share = place - below
+            part = place - below
             if 6 <= z < 30:
                 refs, spot = (inner_ref, inner_lower_ref, inner_upper_ref), z - 6
             else:
                 refs, spot = (outer_ref, outer_lower_ref, outer_upper_ref), z % 24
             value = with_neighbours(*(ref[spot] for ref in refs))
             whole[z] = value + (
-                (1.0 - share) * planes_ref[below + 1] + share * planes_ref[below + 2]
+                (1.0 - part) * planes_ref[below + 1] + part * planes_ref[below + 2]
             )
 
     row = lax.broadcasted_iota(jnp.int32, (128, 128), 0)
@@ -761,6 +822,7 @@
 
 
 VMEM = pl.BlockSpec(memory_space=pltpu.VMEM)
+HBM = pl.BlockSpec(memory_space=pltpu.HBM)
 SMEM = pl.BlockSpec(memory_space=pltpu.SMEM)
 
 
@@ -845,10 +907,18 @@
             shape(24, 8, 256),
             shape(2, 8, 120, 256),
         ),
-        in_specs=[VMEM] * 4,
-        out_specs=(VMEM,) * 4,
-        scratch_shapes=[pltpu.VMEM((2, 8, 400, 256), f32)],
-        compiler_params=params(28),
+        in_specs=[HBM] * 3 + [VMEM],
+        out_specs=(HBM, VMEM, VMEM, HBM),
+        scratch_shapes=[
+            pltpu.VMEM((2, 8, 400, 256), f32),
+            pltpu.VMEM((2, 8, 136, 400), f32),
+            pltpu.VMEM((2, 8, 8, 400), f32),
+            pltpu.VMEM((2, 8, 8, 400), f32),
+            pltpu.VMEM((24, 136, 256), f32),
+            pltpu.SemaphoreType.DMA((10,)),
+            pltpu.SemaphoreType.DMA((13,)),
+        ],
+        compiler_params=params(60),
         cost_estimate=cost(5e9, 1e7),
         name="inner",
     )(wide, from_lower, from_upper, tables["unfold"])
@@ -867,20 +937,20 @@
     )(outer, from_below, from_above, corner_lower, corner_upper, tables["unfold"])
 
 
-def planes_of(far, tables):
+def planes_of(far):
     return pl.pallas_call(
         planes_kernel,
         out_shape=shape(REACH, 136, 256),
-        in_specs=[VMEM] * 3,
+        in_specs=[VMEM],
         out_specs=VMEM,
         compiler_params=params(12),
         cost_estimate=cost(3e9, 2e6),
         name="planes",
-    )(far, *tables["far"][6:])
+    )(far)
 
 
 def far_of(where, masses, tables):
-    along_y, along_x, column, back_x, back_y, even = tables["far"][:6]
+    along_y, along_x, column, back_x, back_y, even = tables["far"]
     parts = along_x.shape[0] * along_y.shape[0]
     total = masses.shape[0] * CQ
 
@@ -896,20 +966,23 @@
                 fixed(*masses.shape),
                 pl.BlockSpec((1, 2, 128, 512), lambda i, w: (w[1], 0, 0, 0)),
                 pl.BlockSpec((1, 128, 96), lambda i, w: (w[0], 0, 0)),
-                fixed(*column.shape),
+                HBM,
                 fixed(*back_x.shape),
                 fixed(*back_y.shape),
-                fixed(*even.shape),
+                HBM,
             ],
             out_specs=fixed(parts, 40, LANES),
             scratch_shapes=[
                 pltpu.VMEM((total, 128, 128), f32),
                 pltpu.VMEM((REACH, 128, 128), f32),
                 pltpu.VMEM((4, LANES, 128), f32),
+                pltpu.VMEM(column.shape, f32),
+                pltpu.VMEM(even.shape, f32),
+                pltpu.SemaphoreType.DMA((2,)),
             ],
         ),
         out_shape=shape(parts, 40, LANES),
-        compiler_params=params(48),
+        compiler_params=params(60),
         cost_estimate=cost(4e9, 9e6),
         name="far",
     )(where, masses, along_y, along_x, column, back_x, back_y, even)
@@ -928,7 +1001,7 @@
             pl.BlockSpec((3, depth, 128, 128), lambda i: (0, i, 0, 0)),
         ),
         scratch_shapes=[pltpu.VMEM((36, 136, 256), f32)],
-        compiler_params=params(32),
+        compiler_params=params(26),
         cost_estimate=cost(2e8, 1.2e7),
         name="final",
     )(*operands)
@@ -968,7 +1041,7 @@
         outer, from_below, from_above, corner_lower, corner_upper, tables
     )
     outer = (near, moved(upper, gx=1), moved(lower, gx=-1))
-    return final_of(inner, outer, planes_of(far, tables))
+    return final_of(inner, outer, planes_of(far))
 
 
 def solution(mesh):

time: 112 us -> 97.8 us (0.87)
  local copies, waits for them, and re-layouts: 12.8 us -> 5.22 us
  Pallas kernels: 66.8 us -> 59.6 us
    pallas_call x1, Pallas kernels: 36.8 us -> 28.1 us  [near_of(): pl.pallas_call(near_kernel, out_shape=(shape(4, 4, 136, 400), strip, stri...]
    unnamed x42 -> x14, local copies, waits for them, and re-layouts: 12.8 us -> 5.22 us
    pallas_call x1, Pallas kernels: 5.62 us -> 8.79 us  [inner_of(): pl.pallas_call(inner_kernel, out_shape=(shape(24, 136, 256), shape(24, 8,...]
    pallas_call x1, Pallas kernels: 6.87 us -> 8.7 us  [far_of(): pl.pallas_call(far_kernel, grid_spec=pltpu.PrefetchScalarGridSpec(num_sca...]
    pallas_call x1, Pallas kernels: 4.45 us -> 2.79 us  [planes_of(): pl.pallas_call(planes_kernel, out_shape=shape(REACH, 136, 256), in_specs=...]
  transfers between devices with their start and end apart: 12 -> 12, of which waited for: 2 -> 2; matrix products, arithmetic and copies ran while one was open for 0% -> 1% of each run, Pallas kernels for 52% -> 53%
where the time goes in v3:
time: 97.8 us; the launch traced here: 97.3 us
  Pallas kernels  59.6 us (61%)
  starting transfers between devices  28.5 us (29%)
  local copies, waits for them, and re-layouts  5.22 us (5%)
  waiting for transfers between devices  2.45 us (3%)
    pallas_call x1, Pallas kernels, near_of(): pl.pallas_call(near_kernel, out_shape=(shape(4, 4, 136, 400), strip, stri...  28.1 us
    ppermute x10, starting transfers between devices, moved(): return lax.ppermute(values, axes, pairs)  15.2 us
    pallas_call x1, Pallas kernels, inner_of(): pl.pallas_call(inner_kernel, out_shape=(shape(24, 136, 256), shape(24, 8,...  8.79 us
    pallas_call x1, Pallas kernels, far_of(): pl.pallas_call(far_kernel, grid_spec=pltpu.PrefetchScalarGridSpec(num_sca...  8.7 us
    all_to_all x1, starting transfers between devices, body(): far = lax.all_to_all(far, ('gx', 'gy'), 0, 0, tiled=True)  6.73 us
    all_to_all x1, starting transfers between devices, body(): masses = lax.all_to_all(masses, 'gz', 0, 0, tiled=True)  6.63 us
    pallas_call x1, Pallas kernels, final_of(): pl.pallas_call(functools.partial(final_kernel, depth=depth), grid=(PATCH...  6.49 us
    unnamed x14, local copies, waits for them, and re-layouts  5.22 us
  transfers between devices with their start and end apart: 12, of which 2 were waited for; matrix products, arithmetic and copies ran while one was open for 1% of the time, Pallas kernels for 53%

profile of v3, /device:TPU:39, one launch (start us, length us, event | category | flops | bytes accessed | tf_op | source)
XLA Modules:
  0.0 97.3 jit_solution(8677186021660426277)
XLA Ops:
  0.6 0.0 copy-start
  0.6 1.2 %copy-done = bf16[32,128,128]{2,1,0:T(8,128)(2,1)S(1)} copy-done((bf16[32,128,128]{2,1,0:T(8,128)(2,1)S(1)}, bf16[32,128,128]{2,1,0:T(8,128)(2,1)}, u32[]{:S(2)}) %copy-start) | copy-done | bytes 1048600
  1.9 1.5 %masses.1 = f32[8,64,128]{2,1,0:T(8,128)} custom-call(bf16[32,128,128]{2,1,0:T(8,128)(2,1)S(1)} %copy-done), custom_call_target="tpu_custom_call" | custom-call | flops 20000000 | bytes 1200000 | tf_op jit(solution)/shard_map/masses/pallas_call | solution.py:857
  3.3 6.6 %all-to-all-start = ((f32[8,64,128]{2,1,0:T(8,128)}), f32[8,64,128]{2,1,0:T(8,128)S(1)}, u32[]{:S(2)}, u32[]{:S(2)}) async-start(f32[8,64,128]{2,1,0:T(8,128)} %masses.1), calls=%async_computation | async-start | bytes 524288 | tf_op jit(solution)/shard_map/all_to_all | solution.py:1026
  9.9 28.1 %near.1 = (f32[4,4,136,400]{3,2,1,0:T(8,128)}, f32[4,4,8,400]{3,2,1,0:T(8,128)}, f32[4,4,8,400]{3,2,1,0:T(8,128)}, f32[8,136,128]{2,1,0:T(8,128)}, f32[8,136,128]{2,1,0:T(8,128)}) custom-call(f32[37,2]{1,0:T(8,128)} %constant.46.clone.weights_ref, bf16[32,128,128]{2,1,0:T(8,128)(2,1)} %rho_ref.3, bf16[4,192,128]{2,1,0:T(8,128)(2,1)} %constant.47.clone.forward_ref, ...), custom_call_target="tpu_custom_call" | custom-call | flops 8000000000 | bytes 50000000 | tf_op jit(solution)/shard_map/near/pallas_call | solution.py:871
  38.0 2.8 %collective-permute-start.4 = (f32[8,136,128]{2,1,0:T(8,128)}, f32[8,136,128]{2,1,0:T(8,128)S(1)}, u32[]{:S(2)}, u32[]{:S(2)}) collective-permute-start(f32[8,136,128]{2,1,0:T(8,128)} %get-tuple-element.21), channel_id=1, source_target_pairs={{0,1},{1,2},{2,3},{3,4},{4,5},{5,6},{6,7},{7,0},{8,9},{9,10},{10,1... | collective-permute-start | bytes 1671176 | tf_op jit(solution)/shard_map/ppermute | solution.py:1019
  40.8 0.0 collective-permute-start.5
  40.8 2.1 %collective-permute-start = (f32[4,4,8,400]{3,2,1,0:T(8,128)}, f32[4,4,8,400]{3,2,1,0:T(8,128)S(1)}, u32[]{:S(2)}, u32[]{:S(2)}) collective-permute-start(f32[4,4,8,400]{3,2,1,0:T(8,128)} %get-tuple-element.15), channel_id=1, source_target_pairs={{0,8},{8,16},{16,24},{24,0},{1,9},{9,17},{17,25},{25,1},{2,10},{10... | collective-permute-start | bytes 614408 | tf_op jit(solution)/shard_map/ppermute | solution.py:1019
  42.9 0.0 collective-permute-start.1
  42.9 0.7 pad_add_fusion.where_ref
  43.6 0.0 all-to-all-done.masses_ref
  43.6 0.0 copy-start.4
  43.6 0.7 copy-done.4
  44.3 8.7 %far.1 = f32[16,40,384]{2,1,0:T(8,128)} custom-call(s32[3]{0:T(128)} %pad_add_fusion.where_ref, f32[8,64,128]{2,1,0:T(8,128)} %copy-done.4, bf16[4,2,128,512]{3,2,1,0:T(8,128)(2,1)} %constant.56.clone.along_y_ref, bf16[4,128,96]{2,1,0:T(8,128)(2,1)} %constant.57.clone.along_x_ref, f32[33,128,128]{2,1,0:T(8,128)} %constant.58.clone.column_hbm, ...), custom_call_target="tpu_custom_call" | custom-call | flops 4000000000 | bytes 9000000 | tf_op jit(solution)/shard_map/far/pallas_call | solution.py:960
  53.0 6.7 %all-to-all-start.1 = ((f32[16,40,384]{2,1,0:T(8,128)}), f32[16,40,384]{2,1,0:T(8,128)}, u32[]{:S(2)}, u32[]{:S(2)}) async-start(f32[16,40,384]{2,1,0:T(8,128)} %far.1), calls=%async_computation.1 | async-start | bytes 1966080 | tf_op jit(solution)/shard_map/all_to_all | solution.py:1033
  59.7 0.0 collective-permute-done.4.from_below_ref
  59.7 0.0 collective-permute-done.5.from_above_ref
  59.8 0.7 collective-permute-start.6
  60.5 0.0 collective-permute-start.7
  60.5 0.6 collective-permute-done
  61.1 0.0 copy-start.5
  61.1 1.8 %collective-permute-done.1 = f32[4,4,8,400]{3,2,1,0:T(8,128)S(1)} collective-permute-done((f32[4,4,8,400]{3,2,1,0:T(8,128)}, f32[4,4,8,400]{3,2,1,0:T(8,128)S(1)}, u32[]{:S(2)}, u32[]{:S(2)}) %collective-permute-start.1) | collective-permute-done | bytes 204832 | tf_op jit(solution)/shard_map/ppermute | solution.py:1019
  62.9 0.0 copy-start.6
  62.9 0.0 copy-done.5
  62.9 0.7 copy-done.6
  63.6 8.8 %inner.1 = (f32[24,136,256]{2,1,0:T(8,128)}, f32[24,8,256]{2,1,0:T(8,128)}, f32[24,8,256]{2,1,0:T(8,128)}, f32[2,8,120,256]{3,2,1,0:T(8,128)}) custom-call(f32[2,8,136,400]{3,2,1,0:T(8,128)} %bitcast.12, f32[2,8,8,400]{3,2,1,0:T(8,128)} %bitcast.13, f32[2,8,8,400]{3,2,1,0:T(8,128)} %bitcast.14, bf16[2,320,320]{2,1,0:T(8,128)(2,1)} %constant.62.clone.unfold_ref), custom_call_target="tpu_custom_call" | custom-call | flops 5000000000 | bytes 10000000 | tf_op jit(solution)/shard_map/inner/pallas_call | solution.py:902
  72.4 3.0 %collective-permute-start.2 = (f32[24,8,256]{2,1,0:T(8,128)}, f32[24,8,256]{2,1,0:T(8,128)S(1)}, u32[]{:S(2)}, u32[]{:S(2)}) collective-permute-start(f32[24,8,256]{2,1,0:T(8,128)} %get-tuple-element.18), channel_id=1, source_target_pairs={{0,32},{32,64},{64,96},{96,0},{1,33},{33,65},{65,97},{97,1},{2,34}... | collective-permute-start | bytes 589832 | tf_op jit(solution)/shard_map/ppermute | solution.py:1019
  75.4 3.8 %collective-permute-start.3 = (f32[24,8,256]{2,1,0:T(8,128)}, f32[24,8,256]{2,1,0:T(8,128)S(1)}, u32[]{:S(2)}, u32[]{:S(2)}) collective-permute-start(f32[24,8,256]{2,1,0:T(8,128)} %get-tuple-element.19), channel_id=1, source_target_pairs={{0,96},{32,0},{64,32},{96,64},{1,97},{33,1},{65,33},{97,65},{2,98}... | collective-permute-start | bytes 589832 | tf_op jit(solution)/shard_map/ppermute | solution.py:1019
  79.3 0.0 collective-permute-done.6.corner_lower_ref
  79.3 0.0 collective-permute-done.7.corner_upper_ref
  79.3 0.0 copy-start.2
  79.3 1.0 %copy-done.2 = bf16[2,320,320]{2,1,0:T(8,128)(2,1)S(1)} copy-done((bf16[2,320,320]{2,1,0:T(8,128)(2,1)S(1)}, bf16[2,320,320]{2,1,0:T(8,128)(2,1)}, u32[]{:S(2)}) %copy-start.2) | copy-done | bytes 409624
  80.3 0.0 copy-start.3
  80.3 1.5 %copy-done.3 = f32[2,8,120,256]{3,2,1,0:T(8,128)S(1)} copy-done((f32[2,8,120,256]{3,2,1,0:T(8,128)S(1)}, f32[2,8,120,256]{3,2,1,0:T(8,128)}, u32[]{:S(2)}) %copy-start.3) | copy-done | bytes 1966104
  81.9 3.3 %outer.1 = (f32[12,136,256]{2,1,0:T(8,128)S(1)}, f32[12,8,256]{2,1,0:T(8,128)S(1)}, f32[12,8,256]{2,1,0:T(8,128)S(1)}) custom-call(f32[2,8,120,256]{3,2,1,0:T(8,128)S(1)} %copy-done.3, f32[8,136,128]{2,1,0:T(8,128)S(1)} %collective-permute-done.4.from_below_ref, f32[8,136,128]{2,1,0:T(8,128)S(1)} %collective-permute-done.5.from_above_ref, ...), custom_call_target="tpu_custom_call" | custom-call | flops 4000000000 | bytes 5000000 | tf_op jit(solution)/shard_map/outer/pallas_call | solution.py:928
  85.2 0.1 collective-permute-start.8
  85.3 2.7 %collective-permute-start.9 = (f32[12,8,256]{2,1,0:T(8,128)S(1)}, f32[12,8,256]{2,1,0:T(8,128)S(1)}, u32[]{:S(2)}, u32[]{:S(2)}) collective-permute-start(f32[12,8,256]{2,1,0:T(8,128)S(1)} %get-tuple-element.25), channel_id=1, source_target_pairs={{0,96},{32,0},{64,32},{96,64},{1,97},{33,1},{65,33},{97,65},{2,98}... | collective-permute-start | bytes 294920 | tf_op jit(solution)/shard_map/ppermute | solution.py:1019
  87.9 0.0 all-to-all-done.1.far_ref
  87.9 0.0 copy-start.1
  87.9 2.8 %planes.1.planes_ref = f32[10,136,256]{2,1,0:T(8,128)S(1)} custom-call(f32[16,40,384]{2,1,0:T(8,128)} %all-to-all-done.1.far_ref), custom_call_target="tpu_custom_call" | custom-call | flops 3000000000 | bytes 2000000 | tf_op jit(solution)/shard_map/planes/pallas_call | solution.py:941
  90.7 0.0 collective-permute-done.2.inner_lower_ref
  90.7 0.0 collective-permute-done.3.inner_upper_ref
  90.7 0.0 collective-permute-done.8.outer_lower_ref
  90.8 0.0 collective-permute-done.9.outer_upper_ref
  90.8 0.0 copy-done.1
  90.8 6.5 %final.1 = (f32[32,128,128]{2,1,0:T(8,128)}, bf16[3,32,128,128]{3,2,1,0:T(8,128)(2,1)}) custom-call(f32[24,136,256]{2,1,0:T(8,128)S(1)} %copy-done.1, f32[24,8,256]{2,1,0:T(8,128)S(1)} %collective-permute-done.2.inner_lower_ref, f32[24,8,256]{2,1,0:T(8,128)S(1)} %collective-permute-done.3.inner_upper_ref, f32[12,136,256]{2,1,0:T(8,128)S(1)} %get-tuple-element.23.outer_ref, ...), custom_call_target="tpu_custom_call" | custom-call | flops 200000000 | bytes 12000000 | tf_op jit(solution)/shard_map/final/pallas_call | solution.py:994
  (2 shorter events, 0.0 us)
Async XLA Ops:
  0.6 1.2 %copy-start = (bf16[32,128,128]{2,1,0:T(8,128)(2,1)S(1)}, bf16[32,128,128]{2,1,0:T(8,128)(2,1)}, u32[]{:S(2)}) copy-start(bf16[32,128,128]{2,1,0:T(8,128)(2,1)} %rho_ref.3) | copy-start | bytes 3145732
  3.3 40.3 %all-to-all-start = ((f32[8,64,128]{2,1,0:T(8,128)}), f32[8,64,128]{2,1,0:T(8,128)S(1)}, u32[]{:S(2)}, u32[]{:S(2)}) async-start(f32[8,64,128]{2,1,0:T(8,128)} %masses.1), calls=%async_computation | async-start | bytes 524288 | tf_op jit(solution)/shard_map/all_to_all | solution.py:1026
  38.0 21.7 %collective-permute-start.4 = (f32[8,136,128]{2,1,0:T(8,128)}, f32[8,136,128]{2,1,0:T(8,128)S(1)}, u32[]{:S(2)}, u32[]{:S(2)}) collective-permute-start(f32[8,136,128]{2,1,0:T(8,128)} %get-tuple-element.21), channel_id=1, source_target_pairs={{0,1},{1,2},{2,3},{3,4},{4,5},{5,6},{6,7},{7,0},{8,9},{9,10},{10,1... | collective-permute-start | bytes 1671176 | tf_op jit(solution)/shard_map/ppermute | solution.py:1019
  40.8 19.0 %collective-permute-start.5 = (f32[8,136,128]{2,1,0:T(8,128)}, f32[8,136,128]{2,1,0:T(8,128)S(1)}, u32[]{:S(2)}, u32[]{:S(2)}) collective-permute-start(f32[8,136,128]{2,1,0:T(8,128)} %get-tuple-element.22), channel_id=1, source_target_pairs={{0,7},{1,0},{2,1},{3,2},{4,3},{5,4},{6,5},{7,6},{8,15},{9,8},{10,9... | collective-permute-start | bytes 1671176 | tf_op jit(solution)/shard_map/ppermute | solution.py:1019
  40.8 20.3 %collective-permute-start = (f32[4,4,8,400]{3,2,1,0:T(8,128)}, f32[4,4,8,400]{3,2,1,0:T(8,128)S(1)}, u32[]{:S(2)}, u32[]{:S(2)}) collective-permute-start(f32[4,4,8,400]{3,2,1,0:T(8,128)} %get-tuple-element.15), channel_id=1, source_target_pairs={{0,8},{8,16},{16,24},{24,0},{1,9},{9,17},{17,25},{25,1},{2,10},{10... | collective-permute-start | bytes 614408 | tf_op jit(solution)/shard_map/ppermute | solution.py:1019
  42.9 20.0 %collective-permute-start.1 = (f32[4,4,8,400]{3,2,1,0:T(8,128)}, f32[4,4,8,400]{3,2,1,0:T(8,128)S(1)}, u32[]{:S(2)}, u32[]{:S(2)}) collective-permute-start(f32[4,4,8,400]{3,2,1,0:T(8,128)} %get-tuple-element.16), channel_id=1, source_target_pairs={{0,24},{8,0},{16,8},{24,16},{1,25},{9,1},{17,9},{25,17},{2,26},{10... | collective-permute-start | bytes 614408 | tf_op jit(solution)/shard_map/ppermute | solution.py:1019
  43.6 0.7 copy-start.4
  53.0 34.9 %all-to-all-start.1 = ((f32[16,40,384]{2,1,0:T(8,128)}), f32[16,40,384]{2,1,0:T(8,128)}, u32[]{:S(2)}, u32[]{:S(2)}) async-start(f32[16,40,384]{2,1,0:T(8,128)} %far.1), calls=%async_computation.1 | async-start | bytes 1966080 | tf_op jit(solution)/shard_map/all_to_all | solution.py:1033
  59.8 19.5 %collective-permute-start.6 = (f32[2,8,8,128]{3,2,1,0:T(8,128)S(1)}, f32[2,8,8,128]{3,2,1,0:T(8,128)S(1)}, u32[]{:S(2)}, u32[]{:S(2)}) collective-permute-start(f32[2,8,8,128]{3,2,1,0:T(8,128)S(1)} %fusion.1), channel_id=1, source_target_pairs={{0,8},{8,16},{16,24},{24,0},{1,9},{9,17},{17,25},{25,1},{2,10},{10... | collective-permute-start | bytes 196616 | tf_op jit(solution)/shard_map/ppermute | solution.py:1019
  60.5 18.8 %collective-permute-start.7 = (f32[2,8,8,128]{3,2,1,0:T(8,128)S(1)}, f32[2,8,8,128]{3,2,1,0:T(8,128)S(1)}, u32[]{:S(2)}, u32[]{:S(2)}) collective-permute-start(f32[2,8,8,128]{3,2,1,0:T(8,128)S(1)} %get-tuple-element.26), channel_id=1, source_target_pairs={{0,24},{8,0},{16,8},{24,16},{1,25},{9,1},{17,9},{25,17},{2,26},{10... | collective-permute-start | bytes 196616 | tf_op jit(solution)/shard_map/ppermute | solution.py:1019
  61.1 1.8 %copy-start.5 = (f32[4,4,8,400]{3,2,1,0:T(8,128)}, f32[4,4,8,400]{3,2,1,0:T(8,128)S(1)}, u32[]{:S(2)}) copy-start(f32[4,4,8,400]{3,2,1,0:T(8,128)S(1)} %collective-permute-done) | copy-start | bytes 614404
  62.9 0.7 copy-start.6
  72.4 18.3 %collective-permute-start.2 = (f32[24,8,256]{2,1,0:T(8,128)}, f32[24,8,256]{2,1,0:T(8,128)S(1)}, u32[]{:S(2)}, u32[]{:S(2)}) collective-permute-start(f32[24,8,256]{2,1,0:T(8,128)} %get-tuple-element.18), channel_id=1, source_target_pairs={{0,32},{32,64},{64,96},{96,0},{1,33},{33,65},{65,97},{97,1},{2,34}... | collective-permute-start | bytes 589832 | tf_op jit(solution)/shard_map/ppermute | solution.py:1019
  75.4 15.3 %collective-permute-start.3 = (f32[24,8,256]{2,1,0:T(8,128)}, f32[24,8,256]{2,1,0:T(8,128)S(1)}, u32[]{:S(2)}, u32[]{:S(2)}) collective-permute-start(f32[24,8,256]{2,1,0:T(8,128)} %get-tuple-element.19), channel_id=1, source_target_pairs={{0,96},{32,0},{64,32},{96,64},{1,97},{33,1},{65,33},{97,65},{2,98}... | collective-permute-start | bytes 589832 | tf_op jit(solution)/shard_map/ppermute | solution.py:1019
  79.3 1.0 %copy-start.2 = (bf16[2,320,320]{2,1,0:T(8,128)(2,1)S(1)}, bf16[2,320,320]{2,1,0:T(8,128)(2,1)}, u32[]{:S(2)}) copy-start(bf16[2,320,320]{2,1,0:T(8,128)(2,1)} %constant.62.clone.unfold_ref) | copy-start | bytes 1228804
  80.3 1.5 %copy-start.3 = (f32[2,8,120,256]{3,2,1,0:T(8,128)S(1)}, f32[2,8,120,256]{3,2,1,0:T(8,128)}, u32[]{:S(2)}) copy-start(f32[2,8,120,256]{3,2,1,0:T(8,128)} %get-tuple-element.20.outer_ref) | copy-start | bytes 5898244
  85.2 5.6 %collective-permute-start.8 = (f32[12,8,256]{2,1,0:T(8,128)S(1)}, f32[12,8,256]{2,1,0:T(8,128)S(1)}, u32[]{:S(2)}, u32[]{:S(2)}) collective-permute-start(f32[12,8,256]{2,1,0:T(8,128)S(1)} %get-tuple-element.24), channel_id=1, source_target_pairs={{0,32},{32,64},{64,96},{96,0},{1,33},{33,65},{65,97},{97,1},{2,34}... | collective-permute-start | bytes 294920 | tf_op jit(solution)/shard_map/ppermute | solution.py:1019
  85.3 5.5 %collective-permute-start.9 = (f32[12,8,256]{2,1,0:T(8,128)S(1)}, f32[12,8,256]{2,1,0:T(8,128)S(1)}, u32[]{:S(2)}, u32[]{:S(2)}) collective-permute-start(f32[12,8,256]{2,1,0:T(8,128)S(1)} %get-tuple-element.25), channel_id=1, source_target_pairs={{0,96},{32,0},{64,32},{96,64},{1,97},{33,1},{65,33},{97,65},{2,98}... | collective-permute-start | bytes 294920 | tf_op jit(solution)/shard_map/ppermute | solution.py:1019
  87.9 2.8 %copy-start.1 = (f32[24,136,256]{2,1,0:T(8,128)S(1)}, f32[24,136,256]{2,1,0:T(8,128)}, u32[]{:S(2)}) copy-start(f32[24,136,256]{2,1,0:T(8,128)} %get-tuple-element.17.inner_ref) | copy-start | bytes 10027012

commit v4 on v3

--- a/solution.py
+++ b/solution.py
@@ -444,12 +444,8 @@
         values = lines[freqs, 2].reshape(128, 256)
         ready[freqs, 2, :, 0:256] = mul_exact(values, turn_ref[...]).reshape(4, 32, 256)
 
-    def prepare_two(index, carry):
-        prepare(2 * index)
-        prepare(2 * index + 1)
-        return carry
-
-    lax.fori_loop(0, NR // 8, prepare_two, 0)
+    for index in range(NR // 4):
+        prepare(index)
     spectra[:, :, 8 * NF :, :] = jnp.zeros((4, 4, 8, 512), f32)
     row = lax.broadcasted_iota(jnp.int32, (32, 1), 0)
 
@@ -488,12 +484,12 @@
         def _():
             fetch(freq + RING, slot).start()
 
-    def solve_two(index, carry):
-        solve(2 * index)
-        solve(2 * index + 1)
+    def solve_some(index, carry):
+        for part in range(4):
+            solve(4 * index + part)
         return carry
 
-    lax.fori_loop(0, NF // 2, solve_two, 0)
+    lax.fori_loop(0, NF // 4, solve_some, 0)
     solve(jnp.int32(NF - 1))
 
     for parity in range(4):
@@ -590,15 +586,15 @@
     for strip in strips:
         strip.wait()
 
-    def turn(index, carry):
+    def turn(index):
         fetch(index).wait()
         even = with_neighbours(wide_ref[0, index], from_lower_ref[0, index], from_upper_ref[0, index])
         odd = with_neighbours(wide_ref[1, index], from_lower_ref[1, index], from_upper_ref[1, index])
         turned_into(standing, 0, index, even + odd)
         turned_into(standing, 1, index, even - odd)
-        return carry
-
-    lax.fori_loop(0, 8, turn, 0)
+
+    for index in range(8):
+        turn(index)
     results = [pltpu.make_async_copy(standing.at[:, :, 40:160, :], outer_hbm, written.at[0])]
     results[0].start()
     for pair in range(4, 10):

time: 97.8 us -> 96.6 us (0.988)
  Pallas kernels: 59.6 us -> 58.5 us
where the time goes in v4:
time: 96.6 us; the launch traced here: 96.1 us
  Pallas kernels  58.5 us (61%)
  starting transfers between devices  28.5 us (30%)
  local copies, waits for them, and re-layouts  5.22 us (5%)
  waiting for transfers between devices  2.45 us (3%)
    pallas_call x1, Pallas kernels, near_of(): pl.pallas_call(near_kernel, out_shape=(shape(4, 4, 136, 400), strip, stri...  27.3 us
    ppermute x10, starting transfers between devices, moved(): return lax.ppermute(values, axes, pairs)  15.2 us
    pallas_call x1, Pallas kernels, far_of(): pl.pallas_call(far_kernel, grid_spec=pltpu.PrefetchScalarGridSpec(num_sca...  8.7 us
    pallas_call x1, Pallas kernels, inner_of(): pl.pallas_call(inner_kernel, out_shape=(shape(24, 136, 256), shape(24, 8,...  8.47 us
    all_to_all x1, starting transfers between devices, body(): far = lax.all_to_all(far, ('gx', 'gy'), 0, 0, tiled=True)  6.72 us
    all_to_all x1, starting transfers between devices, body(): masses = lax.all_to_all(masses, 'gz', 0, 0, tiled=True)  6.63 us
    pallas_call x1, Pallas kernels, final_of(): pl.pallas_call(functools.partial(final_kernel, depth=depth), grid=(PATCH...  6.49 us
    unnamed x14, local copies, waits for them, and re-layouts  5.22 us
  transfers between devices with their start and end apart: 12, of which 2 were waited for; matrix products, arithmetic and copies ran while one was open for 1% of the time, Pallas kernels for 53%

profile of v4, /device:TPU:39, one launch (start us, length us, event | category | flops | bytes accessed | tf_op | source)
XLA Modules:
  0.0 96.1 jit_solution(8797230731229642739)
XLA Ops:
  0.6 0.0 copy-start
  0.6 1.2 %copy-done = bf16[32,128,128]{2,1,0:T(8,128)(2,1)S(1)} copy-done((bf16[32,128,128]{2,1,0:T(8,128)(2,1)S(1)}, bf16[32,128,128]{2,1,0:T(8,128)(2,1)}, u32[]{:S(2)}) %copy-start) | copy-done | bytes 1048600
  1.9 1.5 %masses.1 = f32[8,64,128]{2,1,0:T(8,128)} custom-call(bf16[32,128,128]{2,1,0:T(8,128)(2,1)S(1)} %copy-done), custom_call_target="tpu_custom_call" | custom-call | flops 20000000 | bytes 1200000 | tf_op jit(solution)/shard_map/masses/pallas_call | solution.py:853
  3.3 6.6 %all-to-all-start = ((f32[8,64,128]{2,1,0:T(8,128)}), f32[8,64,128]{2,1,0:T(8,128)S(1)}, u32[]{:S(2)}, u32[]{:S(2)}) async-start(f32[8,64,128]{2,1,0:T(8,128)} %masses.1), calls=%async_computation | async-start | bytes 524288 | tf_op jit(solution)/shard_map/all_to_all | solution.py:1022
  9.9 27.3 %near.1 = (f32[4,4,136,400]{3,2,1,0:T(8,128)}, f32[4,4,8,400]{3,2,1,0:T(8,128)}, f32[4,4,8,400]{3,2,1,0:T(8,128)}, f32[8,136,128]{2,1,0:T(8,128)}, f32[8,136,128]{2,1,0:T(8,128)}) custom-call(f32[37,2]{1,0:T(8,128)} %constant.46.clone.weights_ref, bf16[32,128,128]{2,1,0:T(8,128)(2,1)} %rho_ref.3, bf16[4,192,128]{2,1,0:T(8,128)(2,1)} %constant.47.clone.forward_ref, ...), custom_call_target="tpu_custom_call" | custom-call | flops 8000000000 | bytes 50000000 | tf_op jit(solution)/shard_map/near/pallas_call | solution.py:867
  37.2 2.8 %collective-permute-start.4 = (f32[8,136,128]{2,1,0:T(8,128)}, f32[8,136,128]{2,1,0:T(8,128)S(1)}, u32[]{:S(2)}, u32[]{:S(2)}) collective-permute-start(f32[8,136,128]{2,1,0:T(8,128)} %get-tuple-element.21), channel_id=1, source_target_pairs={{0,1},{1,2},{2,3},{3,4},{4,5},{5,6},{6,7},{7,0},{8,9},{9,10},{10,1... | collective-permute-start | bytes 1671176 | tf_op jit(solution)/shard_map/ppermute | solution.py:1015
  40.0 0.0 collective-permute-start.5
  40.0 2.1 %collective-permute-start = (f32[4,4,8,400]{3,2,1,0:T(8,128)}, f32[4,4,8,400]{3,2,1,0:T(8,128)S(1)}, u32[]{:S(2)}, u32[]{:S(2)}) collective-permute-start(f32[4,4,8,400]{3,2,1,0:T(8,128)} %get-tuple-element.15), channel_id=1, source_target_pairs={{0,8},{8,16},{16,24},{24,0},{1,9},{9,17},{17,25},{25,1},{2,10},{10... | collective-permute-start | bytes 614408 | tf_op jit(solution)/shard_map/ppermute | solution.py:1015
  42.1 0.0 collective-permute-start.1
  42.1 0.7 pad_add_fusion.where_ref
  42.8 0.0 all-to-all-done.masses_ref
  42.8 0.0 copy-start.4
  42.8 0.7 copy-done.4
  43.5 8.7 %far.1 = f32[16,40,384]{2,1,0:T(8,128)} custom-call(s32[3]{0:T(128)} %pad_add_fusion.where_ref, f32[8,64,128]{2,1,0:T(8,128)} %copy-done.4, bf16[4,2,128,512]{3,2,1,0:T(8,128)(2,1)} %constant.56.clone.along_y_ref, bf16[4,128,96]{2,1,0:T(8,128)(2,1)} %constant.57.clone.along_x_ref, f32[33,128,128]{2,1,0:T(8,128)} %constant.58.clone.column_hbm, ...), custom_call_target="tpu_custom_call" | custom-call | flops 4000000000 | bytes 9000000 | tf_op jit(solution)/shard_map/far/pallas_call | solution.py:956
  52.2 6.7 %all-to-all-start.1 = ((f32[16,40,384]{2,1,0:T(8,128)}), f32[16,40,384]{2,1,0:T(8,128)}, u32[]{:S(2)}, u32[]{:S(2)}) async-start(f32[16,40,384]{2,1,0:T(8,128)} %far.1), calls=%async_computation.1 | async-start | bytes 1966080 | tf_op jit(solution)/shard_map/all_to_all | solution.py:1029
  58.9 0.0 collective-permute-done.4.from_below_ref
  58.9 0.0 collective-permute-done.5.from_above_ref
  59.0 0.7 collective-permute-start.6
  59.7 0.0 collective-permute-start.7
  59.7 0.6 collective-permute-done
  60.3 0.0 copy-start.5
  60.3 1.8 %collective-permute-done.1 = f32[4,4,8,400]{3,2,1,0:T(8,128)S(1)} collective-permute-done((f32[4,4,8,400]{3,2,1,0:T(8,128)}, f32[4,4,8,400]{3,2,1,0:T(8,128)S(1)}, u32[]{:S(2)}, u32[]{:S(2)}) %collective-permute-start.1) | collective-permute-done | bytes 204832 | tf_op jit(solution)/shard_map/ppermute | solution.py:1015
  62.1 0.0 copy-start.6
  62.1 0.0 copy-done.5
  62.1 0.7 copy-done.6
  62.8 8.5 %inner.1 = (f32[24,136,256]{2,1,0:T(8,128)}, f32[24,8,256]{2,1,0:T(8,128)}, f32[24,8,256]{2,1,0:T(8,128)}, f32[2,8,120,256]{3,2,1,0:T(8,128)}) custom-call(f32[2,8,136,400]{3,2,1,0:T(8,128)} %bitcast.12, f32[2,8,8,400]{3,2,1,0:T(8,128)} %bitcast.13, f32[2,8,8,400]{3,2,1,0:T(8,128)} %bitcast.14, bf16[2,320,320]{2,1,0:T(8,128)(2,1)} %constant.62.clone.unfold_ref), custom_call_target="tpu_custom_call" | custom-call | flops 5000000000 | bytes 10000000 | tf_op jit(solution)/shard_map/inner/pallas_call | solution.py:898
  71.3 3.0 %collective-permute-start.2 = (f32[24,8,256]{2,1,0:T(8,128)}, f32[24,8,256]{2,1,0:T(8,128)S(1)}, u32[]{:S(2)}, u32[]{:S(2)}) collective-permute-start(f32[24,8,256]{2,1,0:T(8,128)} %get-tuple-element.18), channel_id=1, source_target_pairs={{0,32},{32,64},{64,96},{96,0},{1,33},{33,65},{65,97},{97,1},{2,34}... | collective-permute-start | bytes 589832 | tf_op jit(solution)/shard_map/ppermute | solution.py:1015
  74.3 3.8 %collective-permute-start.3 = (f32[24,8,256]{2,1,0:T(8,128)}, f32[24,8,256]{2,1,0:T(8,128)S(1)}, u32[]{:S(2)}, u32[]{:S(2)}) collective-permute-start(f32[24,8,256]{2,1,0:T(8,128)} %get-tuple-element.19), channel_id=1, source_target_pairs={{0,96},{32,0},{64,32},{96,64},{1,97},{33,1},{65,33},{97,65},{2,98}... | collective-permute-start | bytes 589832 | tf_op jit(solution)/shard_map/ppermute | solution.py:1015
  78.1 0.0 collective-permute-done.6.corner_lower_ref
  78.1 0.0 collective-permute-done.7.corner_upper_ref
  78.1 0.0 copy-start.2
  78.1 1.0 %copy-done.2 = bf16[2,320,320]{2,1,0:T(8,128)(2,1)S(1)} copy-done((bf16[2,320,320]{2,1,0:T(8,128)(2,1)S(1)}, bf16[2,320,320]{2,1,0:T(8,128)(2,1)}, u32[]{:S(2)}) %copy-start.2) | copy-done | bytes 409624
  79.2 0.0 copy-start.3
  79.2 1.5 %copy-done.3 = f32[2,8,120,256]{3,2,1,0:T(8,128)S(1)} copy-done((f32[2,8,120,256]{3,2,1,0:T(8,128)S(1)}, f32[2,8,120,256]{3,2,1,0:T(8,128)}, u32[]{:S(2)}) %copy-start.3) | copy-done | bytes 1966104
  80.7 3.3 %outer.1 = (f32[12,136,256]{2,1,0:T(8,128)S(1)}, f32[12,8,256]{2,1,0:T(8,128)S(1)}, f32[12,8,256]{2,1,0:T(8,128)S(1)}) custom-call(f32[2,8,120,256]{3,2,1,0:T(8,128)S(1)} %copy-done.3, f32[8,136,128]{2,1,0:T(8,128)S(1)} %collective-permute-done.4.from_below_ref, f32[8,136,128]{2,1,0:T(8,128)S(1)} %collective-permute-done.5.from_above_ref, ...), custom_call_target="tpu_custom_call" | custom-call | flops 4000000000 | bytes 5000000 | tf_op jit(solution)/shard_map/outer/pallas_call | solution.py:924
  84.0 0.1 collective-permute-start.8
  84.1 2.7 %collective-permute-start.9 = (f32[12,8,256]{2,1,0:T(8,128)S(1)}, f32[12,8,256]{2,1,0:T(8,128)S(1)}, u32[]{:S(2)}, u32[]{:S(2)}) collective-permute-start(f32[12,8,256]{2,1,0:T(8,128)S(1)} %get-tuple-element.25), channel_id=1, source_target_pairs={{0,96},{32,0},{64,32},{96,64},{1,97},{33,1},{65,33},{97,65},{2,98}... | collective-permute-start | bytes 294920 | tf_op jit(solution)/shard_map/ppermute | solution.py:1015
  86.8 0.0 all-to-all-done.1.far_ref
  86.8 0.0 copy-start.1
  86.8 2.8 %planes.1.planes_ref = f32[10,136,256]{2,1,0:T(8,128)S(1)} custom-call(f32[16,40,384]{2,1,0:T(8,128)} %all-to-all-done.1.far_ref), custom_call_target="tpu_custom_call" | custom-call | flops 3000000000 | bytes 2000000 | tf_op jit(solution)/shard_map/planes/pallas_call | solution.py:937
  89.6 0.0 collective-permute-done.2.inner_lower_ref
  89.6 0.0 collective-permute-done.3.inner_upper_ref
  89.6 0.0 collective-permute-done.8.outer_lower_ref
  89.6 0.0 collective-permute-done.9.outer_upper_ref
  89.6 0.0 copy-done.1
  89.6 6.5 %final.1 = (f32[32,128,128]{2,1,0:T(8,128)}, bf16[3,32,128,128]{3,2,1,0:T(8,128)(2,1)}) custom-call(f32[24,136,256]{2,1,0:T(8,128)S(1)} %copy-done.1, f32[24,8,256]{2,1,0:T(8,128)S(1)} %collective-permute-done.2.inner_lower_ref, f32[24,8,256]{2,1,0:T(8,128)S(1)} %collective-permute-done.3.inner_upper_ref, f32[12,136,256]{2,1,0:T(8,128)S(1)} %get-tuple-element.23.outer_ref, ...), custom_call_target="tpu_custom_call" | custom-call | flops 200000000 | bytes 12000000 | tf_op jit(solution)/shard_map/final/pallas_call | solution.py:990
  (2 shorter events, 0.0 us)
Async XLA Ops:
  0.6 1.2 %copy-start = (bf16[32,128,128]{2,1,0:T(8,128)(2,1)S(1)}, bf16[32,128,128]{2,1,0:T(8,128)(2,1)}, u32[]{:S(2)}) copy-start(bf16[32,128,128]{2,1,0:T(8,128)(2,1)} %rho_ref.3) | copy-start | bytes 3145732
  3.3 39.4 %all-to-all-start = ((f32[8,64,128]{2,1,0:T(8,128)}), f32[8,64,128]{2,1,0:T(8,128)S(1)}, u32[]{:S(2)}, u32[]{:S(2)}) async-start(f32[8,64,128]{2,1,0:T(8,128)} %masses.1), calls=%async_computation | async-start | bytes 524288 | tf_op jit(solution)/shard_map/all_to_all | solution.py:1022
  37.2 21.7 %collective-permute-start.4 = (f32[8,136,128]{2,1,0:T(8,128)}, f32[8,136,128]{2,1,0:T(8,128)S(1)}, u32[]{:S(2)}, u32[]{:S(2)}) collective-permute-start(f32[8,136,128]{2,1,0:T(8,128)} %get-tuple-element.21), channel_id=1, source_target_pairs={{0,1},{1,2},{2,3},{3,4},{4,5},{5,6},{6,7},{7,0},{8,9},{9,10},{10,1... | collective-permute-start | bytes 1671176 | tf_op jit(solution)/shard_map/ppermute | solution.py:1015
  40.0 18.9 %collective-permute-start.5 = (f32[8,136,128]{2,1,0:T(8,128)}, f32[8,136,128]{2,1,0:T(8,128)S(1)}, u32[]{:S(2)}, u32[]{:S(2)}) collective-permute-start(f32[8,136,128]{2,1,0:T(8,128)} %get-tuple-element.22), channel_id=1, source_target_pairs={{0,7},{1,0},{2,1},{3,2},{4,3},{5,4},{6,5},{7,6},{8,15},{9,8},{10,9... | collective-permute-start | bytes 1671176 | tf_op jit(solution)/shard_map/ppermute | solution.py:1015
  40.0 20.3 %collective-permute-start = (f32[4,4,8,400]{3,2,1,0:T(8,128)}, f32[4,4,8,400]{3,2,1,0:T(8,128)S(1)}, u32[]{:S(2)}, u32[]{:S(2)}) collective-permute-start(f32[4,4,8,400]{3,2,1,0:T(8,128)} %get-tuple-element.15), channel_id=1, source_target_pairs={{0,8},{8,16},{16,24},{24,0},{1,9},{9,17},{17,25},{25,1},{2,10},{10... | collective-permute-start | bytes 614408 | tf_op jit(solution)/shard_map/ppermute | solution.py:1015
  42.1 20.0 %collective-permute-start.1 = (f32[4,4,8,400]{3,2,1,0:T(8,128)}, f32[4,4,8,400]{3,2,1,0:T(8,128)S(1)}, u32[]{:S(2)}, u32[]{:S(2)}) collective-permute-start(f32[4,4,8,400]{3,2,1,0:T(8,128)} %get-tuple-element.16), channel_id=1, source_target_pairs={{0,24},{8,0},{16,8},{24,16},{1,25},{9,1},{17,9},{25,17},{2,26},{10... | collective-permute-start | bytes 614408 | tf_op jit(solution)/shard_map/ppermute | solution.py:1015
  42.8 0.7 copy-start.4
  52.2 34.6 %all-to-all-start.1 = ((f32[16,40,384]{2,1,0:T(8,128)}), f32[16,40,384]{2,1,0:T(8,128)}, u32[]{:S(2)}, u32[]{:S(2)}) async-start(f32[16,40,384]{2,1,0:T(8,128)} %far.1), calls=%async_computation.1 | async-start | bytes 1966080 | tf_op jit(solution)/shard_map/all_to_all | solution.py:1029
  59.0 19.2 %collective-permute-start.6 = (f32[2,8,8,128]{3,2,1,0:T(8,128)S(1)}, f32[2,8,8,128]{3,2,1,0:T(8,128)S(1)}, u32[]{:S(2)}, u32[]{:S(2)}) collective-permute-start(f32[2,8,8,128]{3,2,1,0:T(8,128)S(1)} %fusion.1), channel_id=1, source_target_pairs={{0,8},{8,16},{16,24},{24,0},{1,9},{9,17},{17,25},{25,1},{2,10},{10... | collective-permute-start | bytes 196616 | tf_op jit(solution)/shard_map/ppermute | solution.py:1015
  59.7 18.5 %collective-permute-start.7 = (f32[2,8,8,128]{3,2,1,0:T(8,128)S(1)}, f32[2,8,8,128]{3,2,1,0:T(8,128)S(1)}, u32[]{:S(2)}, u32[]{:S(2)}) collective-permute-start(f32[2,8,8,128]{3,2,1,0:T(8,128)S(1)} %get-tuple-element.26), channel_id=1, source_target_pairs={{0,24},{8,0},{16,8},{24,16},{1,25},{9,1},{17,9},{25,17},{2,26},{10... | collective-permute-start | bytes 196616 | tf_op jit(solution)/shard_map/ppermute | solution.py:1015
  60.3 1.8 %copy-start.5 = (f32[4,4,8,400]{3,2,1,0:T(8,128)}, f32[4,4,8,400]{3,2,1,0:T(8,128)S(1)}, u32[]{:S(2)}) copy-start(f32[4,4,8,400]{3,2,1,0:T(8,128)S(1)} %collective-permute-done) | copy-start | bytes 614404
  62.1 0.7 copy-start.6
  71.3 18.3 %collective-permute-start.2 = (f32[24,8,256]{2,1,0:T(8,128)}, f32[24,8,256]{2,1,0:T(8,128)S(1)}, u32[]{:S(2)}, u32[]{:S(2)}) collective-permute-start(f32[24,8,256]{2,1,0:T(8,128)} %get-tuple-element.18), channel_id=1, source_target_pairs={{0,32},{32,64},{64,96},{96,0},{1,33},{33,65},{65,97},{97,1},{2,34}... | collective-permute-start | bytes 589832 | tf_op jit(solution)/shard_map/ppermute | solution.py:1015
  74.3 15.3 %collective-permute-start.3 = (f32[24,8,256]{2,1,0:T(8,128)}, f32[24,8,256]{2,1,0:T(8,128)S(1)}, u32[]{:S(2)}, u32[]{:S(2)}) collective-permute-start(f32[24,8,256]{2,1,0:T(8,128)} %get-tuple-element.19), channel_id=1, source_target_pairs={{0,96},{32,0},{64,32},{96,64},{1,97},{33,1},{65,33},{97,65},{2,98}... | collective-permute-start | bytes 589832 | tf_op jit(solution)/shard_map/ppermute | solution.py:1015
  78.1 1.0 %copy-start.2 = (bf16[2,320,320]{2,1,0:T(8,128)(2,1)S(1)}, bf16[2,320,320]{2,1,0:T(8,128)(2,1)}, u32[]{:S(2)}) copy-start(bf16[2,320,320]{2,1,0:T(8,128)(2,1)} %constant.62.clone.unfold_ref) | copy-start | bytes 1228804
  79.2 1.5 %copy-start.3 = (f32[2,8,120,256]{3,2,1,0:T(8,128)S(1)}, f32[2,8,120,256]{3,2,1,0:T(8,128)}, u32[]{:S(2)}) copy-start(f32[2,8,120,256]{3,2,1,0:T(8,128)} %get-tuple-element.20.outer_ref) | copy-start | bytes 5898244
  84.0 5.6 %collective-permute-start.8 = (f32[12,8,256]{2,1,0:T(8,128)S(1)}, f32[12,8,256]{2,1,0:T(8,128)S(1)}, u32[]{:S(2)}, u32[]{:S(2)}) collective-permute-start(f32[12,8,256]{2,1,0:T(8,128)S(1)} %get-tuple-element.24), channel_id=1, source_target_pairs={{0,32},{32,64},{64,96},{96,0},{1,33},{33,65},{65,97},{97,1},{2,34}... | collective-permute-start | bytes 294920 | tf_op jit(solution)/shard_map/ppermute | solution.py:1015
  84.1 5.5 %collective-permute-start.9 = (f32[12,8,256]{2,1,0:T(8,128)S(1)}, f32[12,8,256]{2,1,0:T(8,128)S(1)}, u32[]{:S(2)}, u32[]{:S(2)}) collective-permute-start(f32[12,8,256]{2,1,0:T(8,128)S(1)} %get-tuple-element.25), channel_id=1, source_target_pairs={{0,96},{32,0},{64,32},{96,64},{1,97},{33,1},{65,33},{97,65},{2,98}... | collective-permute-start | bytes 294920 | tf_op jit(solution)/shard_map/ppermute | solution.py:1015
  86.8 2.8 %copy-start.1 = (f32[24,136,256]{2,1,0:T(8,128)S(1)}, f32[24,136,256]{2,1,0:T(8,128)}, u32[]{:S(2)}) copy-start(f32[24,136,256]{2,1,0:T(8,128)} %get-tuple-element.17.inner_ref) | copy-start | bytes 10027012
